TPU v7x, 768 devices: a whole 4x8x12 slice. The times are simulated.
768 devices in a mesh: dp: 96 (over z, y), expert: 8 (over x, core).
Axes of the slice: x: 4, y: 8, z: 12, core: 2. Of those that a mesh axis runs over, the one named last changes fastest.
Arguments:
- tokens: bfloat16 [13824, 2048], P('dp', 'expert'), may hold values from -6 to 6
- target: bfloat16 [13824, 2048], P('dp', 'expert'), may hold values from -6 to 6
- expert_ids: int32 [13824, 8], P('dp'), may hold values from 0 to 95, all different within a row; in each aligned block of 24 rows (0 to 23, 24 to 47, ...) at most 2 rows name the same one
- gate_weights: float32 [13824, 8], P('dp'), may hold values from 0.1 to 1
- w_in: bfloat16 [96, 2048, 2, 384], P('dp'), may hold values from -0.125 to 0.125
- m_in: bfloat16 [96, 2048, 2, 384], P('dp', 'expert'), may hold values from -24 to 24
- v_in: bfloat16 [96, 2048, 2, 384], P('dp', 'expert'), may hold values from 1 to 100
- w_out: bfloat16 [96, 384, 2048], P('dp'), may hold values from -0.3125 to 0.3125
- m_out: bfloat16 [96, 384, 2048], P('dp', None, 'expert'), may hold values from -24 to 24
- v_out: bfloat16 [96, 384, 2048], P('dp', None, 'expert'), may hold values from 1 to 100
Outputs:
- mixed: bfloat16 [13824, 2048], P('dp', 'expert')
- new_w_in: bfloat16 [96, 2048, 2, 384], P('dp', 'expert')
- new_m_in: bfloat16 [96, 2048, 2, 384], P('dp', 'expert')
- new_v_in: bfloat16 [96, 2048, 2, 384], P('dp', 'expert')
- new_w_out: bfloat16 [96, 384, 2048], P('dp', None, 'expert')
- new_m_out: bfloat16 [96, 384, 2048], P('dp', None, 'expert')
- new_v_out: bfloat16 [96, 384, 2048], P('dp', None, 'expert')
Inputs may be any that keep to these rules, and one draw needn't show every extreme that they name: `expert_ids`: each token names 8 different experts. In each block of 24 rows (one micro-batch of one index of dp) no expert is named more than 2 times, a bound that some block reaches.
All inputs are finite; a program needn't handle non-finite values.
Results may differ from a plain program's by a relative error of at most 0.011.
Values may be sent and summed in bfloat16 or wider, within the bound.
No kernel may reach another device: no remote copies, remote signals or barrier semaphores. Data moves between devices by JAX's collectives and lax.ppermute only.
A program may use at most 64 MiB of HBM per device.

v0:
```python
import jax
import jax.numpy as jnp
from jax import lax
from jax.sharding import PartitionSpec as P

MICRO = 6


beta_one = 0.9
beta_two = 0.95
adam_epsilon = 1e-08
learn_rate = 0.01
decay_rate = 0.1
first_fix = 0.99997343860111
second_fix = 0.994079470779666


def silu_slope(gate_pre):
    sigmoid_gate = jax.nn.sigmoid(gate_pre)
    return sigmoid_gate * (1.0 + gate_pre * (1.0 - sigmoid_gate))


def adamw(weight, moment_one, moment_two, gradient):
    first_new = beta_one * moment_one.astype(jnp.float32) + (1.0 - beta_one) * gradient
    second_new = beta_two * moment_two.astype(jnp.float32) + (1.0 - beta_two) * gradient * gradient
    master = weight.astype(jnp.float32)
    update = (
        first_new / first_fix / (jnp.sqrt(second_new / second_fix) + adam_epsilon)
        + decay_rate * master
    )
    return (
        (master - learn_rate * update).astype(jnp.bfloat16),
        first_new.astype(jnp.bfloat16),
        second_new.astype(jnp.bfloat16),
    )


def contract_last(left, right):
    return lax.dot_general(
        left, right, (((1,), (1,)), ((), ())), preferred_element_type=jnp.float32
    )


def slot_map_of(routed_ids, experts, capacity):
    flat_ids = routed_ids.reshape(-1)
    onehot = (flat_ids[:, None] == lax.iota(jnp.int32, experts)[None, :]).astype(jnp.int32)
    before = jnp.cumsum(onehot, axis=0) - onehot
    slot_rank = jnp.sum(before * onehot, axis=1)
    target_slot = flat_ids * capacity + slot_rank
    return (lax.iota(jnp.int32, experts * capacity)[:, None] == target_slot[None, :]).astype(
        jnp.float32
    )


def to_experts(rows):
    return lax.all_to_all(rows, "dp", split_axis=0, concat_axis=0, tiled=True)


def widen_rows(rows):
    return lax.all_to_all(rows, "expert", split_axis=0, concat_axis=1, tiled=True)


def to_tokens(rows):
    return lax.all_to_all(
        lax.all_to_all(rows, "expert", split_axis=1, concat_axis=0, tiled=True),
        "dp",
        split_axis=0,
        concat_axis=0,
        tiled=True,
    )


def sync_units(unit_stack, rows_stack, grads_stack, totals, hidden_width):
    portion = lax.all_gather(unit_stack, "expert", axis=1, tiled=True)
    hidden_part = portion[:, :, :hidden_width]
    pre_part = portion[:, :, hidden_width:]
    pairing = (((0, 1), (0, 1)), ((), ()))
    next_in = totals[0] + lax.dot_general(
        rows_stack, pre_part, pairing, preferred_element_type=jnp.float32
    )
    next_down = totals[1] + lax.dot_general(
        hidden_part, grads_stack, pairing, preferred_element_type=jnp.float32
    )
    return (next_in, next_down)


def shards(tokens, target, expert_ids, gate_weights, w_in, m_in, v_in, w_out, m_out, v_out):
    experts = lax.axis_size("dp")
    column = lax.axis_index("expert")
    block_rows = tokens.shape[0] // MICRO
    topk_count = expert_ids.shape[1]
    capacity = max(2, (block_rows * topk_count + experts - 1) // experts)
    width_local = tokens.shape[1]
    width_full = w_in.shape[1]
    hidden_width = w_out.shape[1]
    slot_rows = experts * capacity
    w_gate_up = w_in.reshape(width_full, 2 * hidden_width)
    w_down = w_out.reshape(hidden_width, width_full)
    totals = (
        jnp.zeros((width_local, 2 * hidden_width), jnp.float32),
        jnp.zeros((hidden_width, width_local), jnp.float32),
    )
    mixed_blocks = []
    for micro_index in range(MICRO):
        lower_row = micro_index * block_rows
        token_block = tokens[lower_row : lower_row + block_rows]
        target_block = target[lower_row : lower_row + block_rows]
        routed_ids = expert_ids[lower_row : lower_row + block_rows]
        gate_block = gate_weights[lower_row : lower_row + block_rows]
        slot_map = slot_map_of(routed_ids, experts, capacity)
        per_token = slot_map.reshape(slot_rows, block_rows, topk_count).sum(axis=2)
        send_rows = jnp.dot(
            per_token.astype(jnp.bfloat16), token_block, preferred_element_type=jnp.float32
        ).astype(jnp.bfloat16)
        arrived = to_experts(send_rows)
        full_rows = widen_rows(arrived)
        preacts = jnp.dot(full_rows, w_gate_up, preferred_element_type=jnp.float32)
        gate_pre = preacts[:, :hidden_width]
        up_pre = preacts[:, hidden_width:]
        hidden = (jax.nn.silu(gate_pre) * up_pre).astype(jnp.bfloat16)
        out_rows = jnp.dot(hidden, w_down, preferred_element_type=jnp.float32).astype(jnp.bfloat16)
        returned = to_tokens(out_rows)
        weighted = (
            (slot_map * gate_block.reshape(1, -1))
            .reshape(slot_rows, block_rows, topk_count)
            .sum(axis=2)
        )
        mixed_sum = lax.dot_general(
            weighted,
            returned.astype(jnp.float32),
            (((0,), (0,)), ((), ())),
            precision=lax.Precision.HIGHEST,
        )
        mixed_block = mixed_sum.astype(jnp.bfloat16)
        mixed_blocks.append(mixed_block)
        out_grad = mixed_block.astype(jnp.float32) - target_block.astype(jnp.float32)
        slot_grad = jnp.dot(weighted, out_grad, precision=lax.Precision.HIGHEST).astype(
            jnp.bfloat16
        )
        grad_slice = to_experts(slot_grad)
        grad_full = widen_rows(grad_slice)
        hidden_grad = contract_last(grad_full, w_down)
        gate_grad = hidden_grad * up_pre * silu_slope(gate_pre)
        up_grad = hidden_grad * jax.nn.silu(gate_pre)
        pre_grad = jnp.concatenate([gate_grad, up_grad], axis=1).astype(jnp.bfloat16)
        unit_block = jnp.concatenate([hidden, pre_grad], axis=1)
        totals = sync_units(unit_block[None], arrived[None], grad_slice[None], totals, hidden_width)
    w_in_own = lax.dynamic_slice_in_dim(w_in, column * width_local, width_local, 1)
    w_out_own = lax.dynamic_slice_in_dim(w_out, column * width_local, width_local, 2)
    new_w_in, new_m_in, new_v_in = adamw(w_in_own, m_in, v_in, totals[0].reshape(m_in.shape))
    new_w_out, new_m_out, new_v_out = adamw(w_out_own, m_out, v_out, totals[1].reshape(m_out.shape))
    mixed = jnp.concatenate(mixed_blocks, axis=0)
    return (mixed, new_w_in, new_m_in, new_v_in, new_w_out, new_m_out, new_v_out)


def solution(mesh):
    return jax.shard_map(
        shards,
        mesh=mesh,
        in_specs=(
            P("dp", "expert"),
            P("dp", "expert"),
            P("dp", None),
            P("dp", None),
            P("dp", None, None, None),
            P("dp", "expert", None, None),
            P("dp", "expert", None, None),
            P("dp", None, None),
            P("dp", None, "expert"),
            P("dp", None, "expert"),
        ),
        out_specs=(
            P("dp", "expert"),
            P("dp", "expert", None, None),
            P("dp", "expert", None, None),
            P("dp", "expert", None, None),
            P("dp", None, "expert"),
            P("dp", None, "expert"),
            P("dp", None, "expert"),
        ),
        check_vma=False,
    )
```

profile of v0, /device:TPU:1, one launch (start us, length us, event | category | flops | bytes accessed | tf_op | source)
XLA Modules:
  0.0 673.6 jit_solution(5146036741371326589)
XLA Ops:
  5.8 22.5 %all-to-all-start = ((bf16[96,2,256]{2,1,0:T(2,128)(2,1)}), bf16[96,2,256]{2,1,0:T(2,128)(2,1)S(1)}, u32[]{:S(2)}, u32[]{:S(2)}) async-start(bf16[96,2,256]{2,1,0:T(2,128)(2,1)} %all_to_all.360), calls=%async_computation | async-start | bytes 196608 | tf_op jit(solution)/shard_map/all_to_all | solution.py:56
  37.6 4.3 all-to-all-done
  41.9 10.8 %all-to-all-start.4 = ((bf16[96,2,256]{2,1,0:T(2,128)(2,1)}), bf16[96,2,256]{2,1,0:T(2,128)(2,1)S(1)}, u32[]{:S(2)}, u32[]{:S(2)}) async-start(bf16[96,2,256]{2,1,0:T(2,128)(2,1)} %all_to_all.372), calls=%async_computation.4 | async-start | bytes 196608 | tf_op jit(solution)/shard_map/all_to_all | solution.py:56
  53.1 13.1 %all-to-all-done.4 = bf16[96,2,256]{2,1,0:T(2,128)(2,1)S(1)} async-done(((bf16[96,2,256]{2,1,0:T(2,128)(2,1)}), bf16[96,2,256]{2,1,0:T(2,128)(2,1)S(1)}, u32[]{:S(2)}, u32[]{:S(2)}) %all-to-all-start.4) | async-done | bytes 98336 | tf_op jit(solution)/shard_map/all_to_all | solution.py:56
  66.2 5.9 all-to-all-start.8
  73.1 12.5 %all-to-all-done.8 = bf16[96,2,256]{2,1,0:T(2,128)(2,1)S(1)} async-done(((bf16[96,2,256]{2,1,0:T(2,128)(2,1)}), bf16[96,2,256]{2,1,0:T(2,128)(2,1)S(1)}, u32[]{:S(2)}, u32[]{:S(2)}) %all-to-all-start.8) | async-done | bytes 98336 | tf_op jit(solution)/shard_map/all_to_all | solution.py:56
  85.6 5.9 all-to-all-start.12
  92.4 12.7 %all-to-all-done.12 = bf16[96,2,256]{2,1,0:T(2,128)(2,1)S(1)} async-done(((bf16[96,2,256]{2,1,0:T(2,128)(2,1)}), bf16[96,2,256]{2,1,0:T(2,128)(2,1)S(1)}, u32[]{:S(2)}, u32[]{:S(2)}) %all-to-all-start.12) | async-done | bytes 98336 | tf_op jit(solution)/shard_map/all_to_all | solution.py:56
  105.1 6.1 all-to-all-start.20
  112.3 12.4 %all-to-all-done.20 = bf16[96,2,256]{2,1,0:T(2,128)(2,1)S(1)} async-done(((bf16[96,2,256]{2,1,0:T(2,128)(2,1)}), bf16[96,2,256]{2,1,0:T(2,128)(2,1)S(1)}, u32[]{:S(2)}, u32[]{:S(2)}) %all-to-all-start.20) | async-done | bytes 98336 | tf_op jit(solution)/shard_map/all_to_all | solution.py:56
  124.7 5.9 all-to-all-start.16
  131.4 12.8 %all-to-all-done.16 = bf16[96,2,256]{2,1,0:T(2,128)(2,1)S(1)} async-done(((bf16[96,2,256]{2,1,0:T(2,128)(2,1)}), bf16[96,2,256]{2,1,0:T(2,128)(2,1)S(1)}, u32[]{:S(2)}, u32[]{:S(2)}) %all-to-all-start.16) | async-done | bytes 98336 | tf_op jit(solution)/shard_map/all_to_all | solution.py:56
  144.2 11.4 %all-to-all-start.21 = ((bf16[8,24,256]{2,1,0:T(8,128)(2,1)}), bf16[8,24,256]{2,1,0:T(8,128)(2,1)S(1)}, u32[]{:S(2)}, u32[]{:S(2)}) async-start(bf16[8,24,256]{2,1,0:T(8,128)(2,1)} %all_to_all.422), calls=%async_computation.21 | async-start | bytes 196608 | tf_op jit(solution)/shard_map/all_to_all | solution.py:60
  156.3 4.3 all-to-all-done.21
  160.6 4.1 all-to-all-start.17
  165.3 4.3 all-to-all-done.17
  169.7 4.1 all-to-all-start.13
  174.4 4.3 all-to-all-done.13
  178.7 4.1 all-to-all-start.9
  183.5 4.3 all-to-all-done.9
  192.6 4.3 all-to-all-done.5
  201.0 4.2 copy.179
  213.3 4.1 all-to-all-start.22
  227.2 4.3 all-to-all-done.18
  245.4 4.3 all-to-all-done.10
  263.5 4.3 all-to-all-done.2
  267.9 5.9 all-to-all-start.15
  274.5 13.1 %all-to-all-done.15 = bf16[96,2,256]{2,1,0:T(2,128)(2,1)S(1)} async-done(((bf16[96,2,256]{2,1,0:T(2,128)(2,1)}), bf16[96,2,256]{2,1,0:T(2,128)(2,1)S(1)}, u32[]{:S(2)}, u32[]{:S(2)}) %all-to-all-start.15) | async-done | bytes 98336 | tf_op jit(solution)/shard_map/all_to_all | solution.py:64
  287.6 6.2 all-to-all-start.7
  294.5 12.8 %all-to-all-done.7 = bf16[96,2,256]{2,1,0:T(2,128)(2,1)S(1)} async-done(((bf16[96,2,256]{2,1,0:T(2,128)(2,1)}), bf16[96,2,256]{2,1,0:T(2,128)(2,1)S(1)}, u32[]{:S(2)}, u32[]{:S(2)}) %all-to-all-start.7) | async-done | bytes 98336 | tf_op jit(solution)/shard_map/all_to_all | solution.py:64
  307.3 5.9 all-to-all-start.3
  313.9 12.8 %all-to-all-done.3 = bf16[96,2,256]{2,1,0:T(2,128)(2,1)S(1)} async-done(((bf16[96,2,256]{2,1,0:T(2,128)(2,1)}), bf16[96,2,256]{2,1,0:T(2,128)(2,1)S(1)}, u32[]{:S(2)}, u32[]{:S(2)}) %all-to-all-start.3) | async-done | bytes 98336 | tf_op jit(solution)/shard_map/all_to_all | solution.py:64
  326.8 5.9 all-to-all-start.11
  334.9 11.3 %all-to-all-done.11 = bf16[96,2,256]{2,1,0:T(2,128)(2,1)S(1)} async-done(((bf16[96,2,256]{2,1,0:T(2,128)(2,1)}), bf16[96,2,256]{2,1,0:T(2,128)(2,1)S(1)}, u32[]{:S(2)}, u32[]{:S(2)}) %all-to-all-start.11) | async-done | bytes 98336 | tf_op jit(solution)/shard_map/all_to_all | solution.py:64
  346.2 5.9 all-to-all-start.19
  353.8 11.9 %all-to-all-done.19 = bf16[96,2,256]{2,1,0:T(2,128)(2,1)S(1)} async-done(((bf16[96,2,256]{2,1,0:T(2,128)(2,1)}), bf16[96,2,256]{2,1,0:T(2,128)(2,1)S(1)}, u32[]{:S(2)}, u32[]{:S(2)}) %all-to-all-start.19) | async-done | bytes 98336 | tf_op jit(solution)/shard_map/all_to_all | solution.py:64
  365.7 5.9 all-to-all-start.23
  373.2 11.9 %all-to-all-done.23 = bf16[96,2,256]{2,1,0:T(2,128)(2,1)S(1)} async-done(((bf16[96,2,256]{2,1,0:T(2,128)(2,1)}), bf16[96,2,256]{2,1,0:T(2,128)(2,1)S(1)}, u32[]{:S(2)}, u32[]{:S(2)}) %all-to-all-start.23) | async-done | bytes 98336 | tf_op jit(solution)/shard_map/all_to_all | solution.py:64
  387.0 5.9 all-to-all-start.34
  394.0 12.5 %all-to-all-done.34 = bf16[96,2,256]{2,1,0:T(2,128)(2,1)S(1)} async-done(((bf16[96,2,256]{2,1,0:T(2,128)(2,1)}), bf16[96,2,256]{2,1,0:T(2,128)(2,1)S(1)}, u32[]{:S(2)}, u32[]{:S(2)}) %all-to-all-start.34) | async-done | bytes 98336 | tf_op jit(solution)/shard_map/all_to_all | solution.py:56
  406.5 6.3 all-to-all-start.32
  413.9 12.5 %all-to-all-done.32 = bf16[96,2,256]{2,1,0:T(2,128)(2,1)S(1)} async-done(((bf16[96,2,256]{2,1,0:T(2,128)(2,1)}), bf16[96,2,256]{2,1,0:T(2,128)(2,1)S(1)}, u32[]{:S(2)}, u32[]{:S(2)}) %all-to-all-start.32) | async-done | bytes 98336 | tf_op jit(solution)/shard_map/all_to_all | solution.py:56
  426.4 5.9 all-to-all-start.30
  433.4 12.5 %all-to-all-done.30 = bf16[96,2,256]{2,1,0:T(2,128)(2,1)S(1)} async-done(((bf16[96,2,256]{2,1,0:T(2,128)(2,1)}), bf16[96,2,256]{2,1,0:T(2,128)(2,1)S(1)}, u32[]{:S(2)}, u32[]{:S(2)}) %all-to-all-start.30) | async-done | bytes 98336 | tf_op jit(solution)/shard_map/all_to_all | solution.py:56
  445.8 5.9 all-to-all-start.28
  452.8 12.5 %all-to-all-done.28 = bf16[96,2,256]{2,1,0:T(2,128)(2,1)S(1)} async-done(((bf16[96,2,256]{2,1,0:T(2,128)(2,1)}), bf16[96,2,256]{2,1,0:T(2,128)(2,1)S(1)}, u32[]{:S(2)}, u32[]{:S(2)}) %all-to-all-start.28) | async-done | bytes 98336 | tf_op jit(solution)/shard_map/all_to_all | solution.py:56
  465.3 5.9 all-to-all-start.24
  472.3 12.5 %all-to-all-done.24 = bf16[96,2,256]{2,1,0:T(2,128)(2,1)S(1)} async-done(((bf16[96,2,256]{2,1,0:T(2,128)(2,1)}), bf16[96,2,256]{2,1,0:T(2,128)(2,1)S(1)}, u32[]{:S(2)}, u32[]{:S(2)}) %all-to-all-start.24) | async-done | bytes 98336 | tf_op jit(solution)/shard_map/all_to_all | solution.py:56
  484.7 5.9 all-to-all-start.26
  491.4 12.8 %all-to-all-done.26 = bf16[96,2,256]{2,1,0:T(2,128)(2,1)S(1)} async-done(((bf16[96,2,256]{2,1,0:T(2,128)(2,1)}), bf16[96,2,256]{2,1,0:T(2,128)(2,1)S(1)}, u32[]{:S(2)}, u32[]{:S(2)}) %all-to-all-start.26) | async-done | bytes 98336 | tf_op jit(solution)/shard_map/all_to_all | solution.py:56
  504.2 17.9 %all-to-all-start.25 = ((bf16[8,24,256]{2,1,0:T(8,128)(2,1)}), bf16[8,24,256]{2,1,0:T(8,128)(2,1)S(1)}, u32[]{:S(2)}, u32[]{:S(2)}) async-start(bf16[8,24,256]{2,1,0:T(8,128)(2,1)} %all_to_all.434), calls=%async_computation.25 | async-start | bytes 196608 | tf_op jit(solution)/shard_map/all_to_all | solution.py:60
  531.2 4.8 all-to-all-start.27
  536.6 4.4 all-to-all-done.27
  545.6 4.5 all-to-all-done.29
  554.7 4.5 all-to-all-done.31
  563.8 4.5 all-to-all-done.33
  572.9 4.5 all-to-all-done.35
  577.9 13.9 %all-gather.5 = bf16[192,1152]{1,0:T(8,128)(2,1)S(1)} all-gather(bf16[24,1152]{1,0:T(8,128)(2,1)S(1)} %pad_maximum_fusion.5), channel_id=7, replica_groups=mesh['dp'=96,'expert'=8] {'expert'}, dimensions={0}, use_global_device_ids=true | all-gather | bytes 497664 | tf_op jit(solution)/shard_map/all_gather | solution.py:74
  591.8 13.0 %all-gather.4 = bf16[192,1152]{1,0:T(8,128)(2,1)S(1)} all-gather(bf16[24,1152]{1,0:T(8,128)(2,1)S(1)} %pad_maximum_fusion.4), channel_id=6, replica_groups=mesh['dp'=96,'expert'=8] {'expert'}, dimensions={0}, use_global_device_ids=true | all-gather | bytes 497664 | tf_op jit(solution)/shard_map/all_gather | solution.py:74
  604.8 13.0 %all-gather.3 = bf16[192,1152]{1,0:T(8,128)(2,1)S(1)} all-gather(bf16[24,1152]{1,0:T(8,128)(2,1)S(1)} %pad_maximum_fusion.3), channel_id=5, replica_groups=mesh['dp'=96,'expert'=8] {'expert'}, dimensions={0}, use_global_device_ids=true | all-gather | bytes 497664 | tf_op jit(solution)/shard_map/all_gather | solution.py:74
  617.9 13.0 %all-gather.2 = bf16[192,1152]{1,0:T(8,128)(2,1)S(1)} all-gather(bf16[24,1152]{1,0:T(8,128)(2,1)S(1)} %pad_maximum_fusion.2), channel_id=4, replica_groups=mesh['dp'=96,'expert'=8] {'expert'}, dimensions={0}, use_global_device_ids=true | all-gather | bytes 497664 | tf_op jit(solution)/shard_map/all_gather | solution.py:74
  630.9 13.2 %all-gather.1 = bf16[192,1152]{1,0:T(8,128)(2,1)S(1)} all-gather(bf16[24,1152]{1,0:T(8,128)(2,1)S(1)} %pad_maximum_fusion.1), channel_id=3, replica_groups=mesh['dp'=96,'expert'=8] {'expert'}, dimensions={0}, use_global_device_ids=true | all-gather | bytes 497664 | tf_op jit(solution)/shard_map/all_gather | solution.py:74
  644.1 13.0 %all-gather = bf16[192,1152]{1,0:T(8,128)(2,1)S(1)} all-gather(bf16[24,1152]{1,0:T(8,128)(2,1)S(1)} %pad_maximum_fusion), channel_id=2, replica_groups=mesh['dp'=96,'expert'=8] {'expert'}, dimensions={0}, use_global_device_ids=true | all-gather | bytes 497664 | tf_op jit(solution)/shard_map/all_gather | solution.py:74
  665.2 5.9 fusion.86
  (271 shorter events, 129.3 us)
Async XLA Ops:
  5.8 36.0 %all-to-all-start = ((bf16[96,2,256]{2,1,0:T(2,128)(2,1)}), bf16[96,2,256]{2,1,0:T(2,128)(2,1)S(1)}, u32[]{:S(2)}, u32[]{:S(2)}) async-start(bf16[96,2,256]{2,1,0:T(2,128)(2,1)} %all_to_all.360), calls=%async_computation | async-start | bytes 196608 | tf_op jit(solution)/shard_map/all_to_all | solution.py:56
  30.4 4.8 copy-start.16
  41.9 24.3 %all-to-all-start.4 = ((bf16[96,2,256]{2,1,0:T(2,128)(2,1)}), bf16[96,2,256]{2,1,0:T(2,128)(2,1)S(1)}, u32[]{:S(2)}, u32[]{:S(2)}) async-start(bf16[96,2,256]{2,1,0:T(2,128)(2,1)} %all_to_all.372), calls=%async_computation.4 | async-start | bytes 196608 | tf_op jit(solution)/shard_map/all_to_all | solution.py:56
  66.2 19.5 %all-to-all-start.8 = ((bf16[96,2,256]{2,1,0:T(2,128)(2,1)}), bf16[96,2,256]{2,1,0:T(2,128)(2,1)S(1)}, u32[]{:S(2)}, u32[]{:S(2)}) async-start(bf16[96,2,256]{2,1,0:T(2,128)(2,1)} %all_to_all.384), calls=%async_computation.8 | async-start | bytes 196608 | tf_op jit(solution)/shard_map/all_to_all | solution.py:56
  85.6 19.5 %all-to-all-start.12 = ((bf16[96,2,256]{2,1,0:T(2,128)(2,1)}), bf16[96,2,256]{2,1,0:T(2,128)(2,1)S(1)}, u32[]{:S(2)}, u32[]{:S(2)}) async-start(bf16[96,2,256]{2,1,0:T(2,128)(2,1)} %all_to_all.396), calls=%async_computation.12 | async-start | bytes 196608 | tf_op jit(solution)/shard_map/all_to_all | solution.py:56
  105.1 19.6 %all-to-all-start.20 = ((bf16[96,2,256]{2,1,0:T(2,128)(2,1)}), bf16[96,2,256]{2,1,0:T(2,128)(2,1)S(1)}, u32[]{:S(2)}, u32[]{:S(2)}) async-start(bf16[96,2,256]{2,1,0:T(2,128)(2,1)} %all_to_all.420), calls=%async_computation.20 | async-start | bytes 196608 | tf_op jit(solution)/shard_map/all_to_all | solution.py:56
  124.7 19.5 %all-to-all-start.16 = ((bf16[96,2,256]{2,1,0:T(2,128)(2,1)}), bf16[96,2,256]{2,1,0:T(2,128)(2,1)S(1)}, u32[]{:S(2)}, u32[]{:S(2)}) async-start(bf16[96,2,256]{2,1,0:T(2,128)(2,1)} %all_to_all.408), calls=%async_computation.16 | async-start | bytes 196608 | tf_op jit(solution)/shard_map/all_to_all | solution.py:56
  144.2 16.4 %all-to-all-start.21 = ((bf16[8,24,256]{2,1,0:T(8,128)(2,1)}), bf16[8,24,256]{2,1,0:T(8,128)(2,1)S(1)}, u32[]{:S(2)}, u32[]{:S(2)}) async-start(bf16[8,24,256]{2,1,0:T(8,128)(2,1)} %all_to_all.422), calls=%async_computation.21 | async-start | bytes 196608 | tf_op jit(solution)/shard_map/all_to_all | solution.py:60
  160.6 9.1 %all-to-all-start.17 = ((bf16[8,24,256]{2,1,0:T(8,128)(2,1)}), bf16[8,24,256]{2,1,0:T(8,128)(2,1)S(1)}, u32[]{:S(2)}, u32[]{:S(2)}) async-start(bf16[8,24,256]{2,1,0:T(8,128)(2,1)} %all_to_all.410), calls=%async_computation.17 | async-start | bytes 196608 | tf_op jit(solution)/shard_map/all_to_all | solution.py:60
  169.7 9.1 %all-to-all-start.13 = ((bf16[8,24,256]{2,1,0:T(8,128)(2,1)}), bf16[8,24,256]{2,1,0:T(8,128)(2,1)S(1)}, u32[]{:S(2)}, u32[]{:S(2)}) async-start(bf16[8,24,256]{2,1,0:T(8,128)(2,1)} %all_to_all.398), calls=%async_computation.13 | async-start | bytes 196608 | tf_op jit(solution)/shard_map/all_to_all | solution.py:60
  178.7 9.1 %all-to-all-start.9 = ((bf16[8,24,256]{2,1,0:T(8,128)(2,1)}), bf16[8,24,256]{2,1,0:T(8,128)(2,1)S(1)}, u32[]{:S(2)}, u32[]{:S(2)}) async-start(bf16[8,24,256]{2,1,0:T(8,128)(2,1)} %all_to_all.386), calls=%async_computation.9 | async-start | bytes 196608 | tf_op jit(solution)/shard_map/all_to_all | solution.py:60
  187.8 9.1 %all-to-all-start.5 = ((bf16[8,24,256]{2,1,0:T(8,128)(2,1)}), bf16[8,24,256]{2,1,0:T(8,128)(2,1)S(1)}, u32[]{:S(2)}, u32[]{:S(2)}) async-start(bf16[8,24,256]{2,1,0:T(8,128)(2,1)} %all_to_all.374), calls=%async_computation.5 | async-start | bytes 196608 | tf_op jit(solution)/shard_map/all_to_all | solution.py:60
  196.9 9.1 %all-to-all-start.1 = ((bf16[8,24,256]{2,1,0:T(8,128)(2,1)}), bf16[8,24,256]{2,1,0:T(8,128)(2,1)S(1)}, u32[]{:S(2)}, u32[]{:S(2)}) async-start(bf16[8,24,256]{2,1,0:T(8,128)(2,1)} %all_to_all.362), calls=%async_computation.1 | async-start | bytes 196608 | tf_op jit(solution)/shard_map/all_to_all | solution.py:60
  206.0 2.8 copy-start.1
  210.9 1.4 copy-start
  213.3 9.1 %all-to-all-start.22 = ((bf16[24,8,256]{2,0,1:T(8,128)(2,1)}), bf16[24,8,256]{2,0,1:T(8,128)(2,1)S(1)}, u32[]{:S(2)}, u32[]{:S(2)}) async-start(bf16[24,8,256]{2,0,1:T(8,128)(2,1)} %bitcast.290), calls=%async_computation.22 | async-start | bytes 196608 | tf_op jit(solution)/shard_map/all_to_all | solution.py:65
  222.4 9.1 %all-to-all-start.18 = ((bf16[24,8,256]{2,0,1:T(8,128)(2,1)}), bf16[24,8,256]{2,0,1:T(8,128)(2,1)S(1)}, u32[]{:S(2)}, u32[]{:S(2)}) async-start(bf16[24,8,256]{2,0,1:T(8,128)(2,1)} %bitcast.291), calls=%async_computation.18 | async-start | bytes 196608 | tf_op jit(solution)/shard_map/all_to_all | solution.py:65
  231.5 9.1 %all-to-all-start.14 = ((bf16[24,8,256]{2,0,1:T(8,128)(2,1)}), bf16[24,8,256]{2,0,1:T(8,128)(2,1)S(1)}, u32[]{:S(2)}, u32[]{:S(2)}) async-start(bf16[24,8,256]{2,0,1:T(8,128)(2,1)} %bitcast.292), calls=%async_computation.14 | async-start | bytes 196608 | tf_op jit(solution)/shard_map/all_to_all | solution.py:65
  240.6 9.1 %all-to-all-start.10 = ((bf16[24,8,256]{2,0,1:T(8,128)(2,1)}), bf16[24,8,256]{2,0,1:T(8,128)(2,1)S(1)}, u32[]{:S(2)}, u32[]{:S(2)}) async-start(bf16[24,8,256]{2,0,1:T(8,128)(2,1)} %bitcast.293), calls=%async_computation.10 | async-start | bytes 196608 | tf_op jit(solution)/shard_map/all_to_all | solution.py:65
  249.7 9.1 %all-to-all-start.6 = ((bf16[24,8,256]{2,0,1:T(8,128)(2,1)}), bf16[24,8,256]{2,0,1:T(8,128)(2,1)S(1)}, u32[]{:S(2)}, u32[]{:S(2)}) async-start(bf16[24,8,256]{2,0,1:T(8,128)(2,1)} %bitcast.294), calls=%async_computation.6 | async-start | bytes 196608 | tf_op jit(solution)/shard_map/all_to_all | solution.py:65
  258.8 9.1 %all-to-all-start.2 = ((bf16[24,8,256]{2,0,1:T(8,128)(2,1)}), bf16[24,8,256]{2,0,1:T(8,128)(2,1)S(1)}, u32[]{:S(2)}, u32[]{:S(2)}) async-start(bf16[24,8,256]{2,0,1:T(8,128)(2,1)} %bitcast.295), calls=%async_computation.2 | async-start | bytes 196608 | tf_op jit(solution)/shard_map/all_to_all | solution.py:65
  267.9 19.8 %all-to-all-start.15 = ((bf16[96,2,256]{2,1,0:T(2,128)(2,1)}), bf16[96,2,256]{2,1,0:T(2,128)(2,1)S(1)}, u32[]{:S(2)}, u32[]{:S(2)}) async-start(bf16[96,2,256]{2,1,0:T(2,128)(2,1)} %all_to_all.405), calls=%async_computation.15 | async-start | bytes 196608 | tf_op jit(solution)/shard_map/all_to_all | solution.py:64
  287.6 19.7 %all-to-all-start.7 = ((bf16[96,2,256]{2,1,0:T(2,128)(2,1)}), bf16[96,2,256]{2,1,0:T(2,128)(2,1)S(1)}, u32[]{:S(2)}, u32[]{:S(2)}) async-start(bf16[96,2,256]{2,1,0:T(2,128)(2,1)} %all_to_all.381), calls=%async_computation.7 | async-start | bytes 196608 | tf_op jit(solution)/shard_map/all_to_all | solution.py:64
  307.3 19.5 %all-to-all-start.3 = ((bf16[96,2,256]{2,1,0:T(2,128)(2,1)}), bf16[96,2,256]{2,1,0:T(2,128)(2,1)S(1)}, u32[]{:S(2)}, u32[]{:S(2)}) async-start(bf16[96,2,256]{2,1,0:T(2,128)(2,1)} %all_to_all.369), calls=%async_computation.3 | async-start | bytes 196608 | tf_op jit(solution)/shard_map/all_to_all | solution.py:64
  313.9 72.1 %copy-start.15 = (bf16[144,256]{1,0:T(8,128)(2,1)S(1)}, bf16[144,256]{1,0:T(8,128)(2,1)}, u32[]{:S(2)}) copy-start(bf16[144,256]{1,0:T(8,128)(2,1)} %param.11) | copy-start | bytes 221188
  326.8 19.5 %all-to-all-start.11 = ((bf16[96,2,256]{2,1,0:T(2,128)(2,1)}), bf16[96,2,256]{2,1,0:T(2,128)(2,1)S(1)}, u32[]{:S(2)}, u32[]{:S(2)}) async-start(bf16[96,2,256]{2,1,0:T(2,128)(2,1)} %all_to_all.393), calls=%async_computation.11 | async-start | bytes 196608 | tf_op jit(solution)/shard_map/all_to_all | solution.py:64
  346.2 19.5 %all-to-all-start.19 = ((bf16[96,2,256]{2,1,0:T(2,128)(2,1)}), bf16[96,2,256]{2,1,0:T(2,128)(2,1)S(1)}, u32[]{:S(2)}, u32[]{:S(2)}) async-start(bf16[96,2,256]{2,1,0:T(2,128)(2,1)} %all_to_all.417), calls=%async_computation.19 | async-start | bytes 196608 | tf_op jit(solution)/shard_map/all_to_all | solution.py:64
  353.8 78.5 %copy-start.18 = (bf16[24,256]{1,0:T(8,128)(2,1)S(1)}, bf16[24,256]{1,0:T(8,128)(2,1)}, u32[]{:S(2)}) copy-start(bf16[24,256]{1,0:T(8,128)(2,1)} %get-tuple-element.54) | copy-start | bytes 36868
  353.8 97.9 %copy-start.17 = (bf16[24,256]{1,0:T(8,128)(2,1)S(1)}, bf16[24,256]{1,0:T(8,128)(2,1)}, u32[]{:S(2)}) copy-start(bf16[24,256]{1,0:T(8,128)(2,1)} %get-tuple-element.50) | copy-start | bytes 36868
  365.7 19.5 %all-to-all-start.23 = ((bf16[96,2,256]{2,1,0:T(2,128)(2,1)}), bf16[96,2,256]{2,1,0:T(2,128)(2,1)S(1)}, u32[]{:S(2)}, u32[]{:S(2)}) async-start(bf16[96,2,256]{2,1,0:T(2,128)(2,1)} %all_to_all.429), calls=%async_computation.23 | async-start | bytes 196608 | tf_op jit(solution)/shard_map/all_to_all | solution.py:64
  387.0 19.5 %all-to-all-start.34 = ((bf16[96,2,256]{2,1,0:T(2,128)(2,1)}), bf16[96,2,256]{2,1,0:T(2,128)(2,1)S(1)}, u32[]{:S(2)}, u32[]{:S(2)}) async-start(bf16[96,2,256]{2,1,0:T(2,128)(2,1)} %all_to_all.462), calls=%async_computation.34 | async-start | bytes 196608 | tf_op jit(solution)/shard_map/all_to_all | solution.py:56
  406.5 19.9 %all-to-all-start.32 = ((bf16[96,2,256]{2,1,0:T(2,128)(2,1)}), bf16[96,2,256]{2,1,0:T(2,128)(2,1)S(1)}, u32[]{:S(2)}, u32[]{:S(2)}) async-start(bf16[96,2,256]{2,1,0:T(2,128)(2,1)} %all_to_all.456), calls=%async_computation.32 | async-start | bytes 196608 | tf_op jit(solution)/shard_map/all_to_all | solution.py:56
  426.4 19.5 %all-to-all-start.30 = ((bf16[96,2,256]{2,1,0:T(2,128)(2,1)}), bf16[96,2,256]{2,1,0:T(2,128)(2,1)S(1)}, u32[]{:S(2)}, u32[]{:S(2)}) async-start(bf16[96,2,256]{2,1,0:T(2,128)(2,1)} %all_to_all.450), calls=%async_computation.30 | async-start | bytes 196608 | tf_op jit(solution)/shard_map/all_to_all | solution.py:56
  445.8 19.5 %all-to-all-start.28 = ((bf16[96,2,256]{2,1,0:T(2,128)(2,1)}), bf16[96,2,256]{2,1,0:T(2,128)(2,1)S(1)}, u32[]{:S(2)}, u32[]{:S(2)}) async-start(bf16[96,2,256]{2,1,0:T(2,128)(2,1)} %all_to_all.444), calls=%async_computation.28 | async-start | bytes 196608 | tf_op jit(solution)/shard_map/all_to_all | solution.py:56
  465.3 19.5 %all-to-all-start.24 = ((bf16[96,2,256]{2,1,0:T(2,128)(2,1)}), bf16[96,2,256]{2,1,0:T(2,128)(2,1)S(1)}, u32[]{:S(2)}, u32[]{:S(2)}) async-start(bf16[96,2,256]{2,1,0:T(2,128)(2,1)} %all_to_all.432), calls=%async_computation.24 | async-start | bytes 196608 | tf_op jit(solution)/shard_map/all_to_all | solution.py:56
  484.7 19.5 %all-to-all-start.26 = ((bf16[96,2,256]{2,1,0:T(2,128)(2,1)}), bf16[96,2,256]{2,1,0:T(2,128)(2,1)S(1)}, u32[]{:S(2)}, u32[]{:S(2)}) async-start(bf16[96,2,256]{2,1,0:T(2,128)(2,1)} %all_to_all.438), calls=%async_computation.26 | async-start | bytes 196608 | tf_op jit(solution)/shard_map/all_to_all | solution.py:56
  504.2 27.0 %all-to-all-start.25 = ((bf16[8,24,256]{2,1,0:T(8,128)(2,1)}), bf16[8,24,256]{2,1,0:T(8,128)(2,1)S(1)}, u32[]{:S(2)}, u32[]{:S(2)}) async-start(bf16[8,24,256]{2,1,0:T(8,128)(2,1)} %all_to_all.434), calls=%async_computation.25 | async-start | bytes 196608 | tf_op jit(solution)/shard_map/all_to_all | solution.py:60
  531.2 9.8 %all-to-all-start.27 = ((bf16[8,24,256]{2,1,0:T(8,128)(2,1)}), bf16[8,24,256]{2,1,0:T(8,128)(2,1)S(1)}, u32[]{:S(2)}, u32[]{:S(2)}) async-start(bf16[8,24,256]{2,1,0:T(8,128)(2,1)} %all_to_all.440), calls=%async_computation.27 | async-start | bytes 196608 | tf_op jit(solution)/shard_map/all_to_all | solution.py:60
  541.0 9.1 %all-to-all-start.29 = ((bf16[8,24,256]{2,1,0:T(8,128)(2,1)}), bf16[8,24,256]{2,1,0:T(8,128)(2,1)S(1)}, u32[]{:S(2)}, u32[]{:S(2)}) async-start(bf16[8,24,256]{2,1,0:T(8,128)(2,1)} %all_to_all.446), calls=%async_computation.29 | async-start | bytes 196608 | tf_op jit(solution)/shard_map/all_to_all | solution.py:60
  550.1 9.1 %all-to-all-start.31 = ((bf16[8,24,256]{2,1,0:T(8,128)(2,1)}), bf16[8,24,256]{2,1,0:T(8,128)(2,1)S(1)}, u32[]{:S(2)}, u32[]{:S(2)}) async-start(bf16[8,24,256]{2,1,0:T(8,128)(2,1)} %all_to_all.452), calls=%async_computation.31 | async-start | bytes 196608 | tf_op jit(solution)/shard_map/all_to_all | solution.py:60
  559.2 9.1 %all-to-all-start.33 = ((bf16[8,24,256]{2,1,0:T(8,128)(2,1)}), bf16[8,24,256]{2,1,0:T(8,128)(2,1)S(1)}, u32[]{:S(2)}, u32[]{:S(2)}) async-start(bf16[8,24,256]{2,1,0:T(8,128)(2,1)} %all_to_all.458), calls=%async_computation.33 | async-start | bytes 196608 | tf_op jit(solution)/shard_map/all_to_all | solution.py:60
  568.2 9.1 %all-to-all-start.35 = ((bf16[8,24,256]{2,1,0:T(8,128)(2,1)}), bf16[8,24,256]{2,1,0:T(8,128)(2,1)S(1)}, u32[]{:S(2)}, u32[]{:S(2)}) async-start(bf16[8,24,256]{2,1,0:T(8,128)(2,1)} %all_to_all.464), calls=%async_computation.35 | async-start | bytes 196608 | tf_op jit(solution)/shard_map/all_to_all | solution.py:60
  591.8 67.5 %copy-start.6 = (bf16[192,1152]{1,0:T(8,128)(2,1)}, bf16[192,1152]{1,0:T(8,128)(2,1)S(1)}, u32[]{:S(2)}) copy-start(bf16[192,1152]{1,0:T(8,128)(2,1)S(1)} %all-gather.5) | copy-start | bytes 1327108
  604.8 54.1 %copy-start.2 = (bf16[192,1152]{1,0:T(8,128)(2,1)}, bf16[192,1152]{1,0:T(8,128)(2,1)S(1)}, u32[]{:S(2)}) copy-start(bf16[192,1152]{1,0:T(8,128)(2,1)S(1)} %all-gather.4) | copy-start | bytes 1327108
  617.8 40.7 %copy-start.3 = (bf16[192,1152]{1,0:T(8,128)(2,1)}, bf16[192,1152]{1,0:T(8,128)(2,1)S(1)}, u32[]{:S(2)}) copy-start(bf16[192,1152]{1,0:T(8,128)(2,1)S(1)} %all-gather.3) | copy-start | bytes 1327108
  630.9 27.1 %copy-start.4 = (bf16[192,1152]{1,0:T(8,128)(2,1)}, bf16[192,1152]{1,0:T(8,128)(2,1)S(1)}, u32[]{:S(2)}) copy-start(bf16[192,1152]{1,0:T(8,128)(2,1)S(1)} %all-gather.2) | copy-start | bytes 1327108
  630.9 26.8 %copy-start.13 = (bf16[192,256]{1,0:T(8,128)(2,1)S(1)}, bf16[192,256]{1,0:T(8,128)(2,1)}, u32[]{:S(2)}) copy-start(bf16[192,256]{1,0:T(8,128)(2,1)} %reshape.559) | copy-start | bytes 294916
  644.1 13.9 %copy-start.5 = (bf16[192,1152]{1,0:T(8,128)(2,1)}, bf16[192,1152]{1,0:T(8,128)(2,1)S(1)}, u32[]{:S(2)}) copy-start(bf16[192,1152]{1,0:T(8,128)(2,1)S(1)} %all-gather.1) | copy-start | bytes 1327108
  657.4 0.9 copy-start.12
  658.6 0.9 copy-start.9
  660.2 2.6 copy-start.11
  660.2 3.8 copy-start.10
  661.5 3.7 copy-start.7
  661.5 3.7 copy-start.8
  665.2 5.9 copy-start.14
  665.2 5.9 copy-start.19
  665.2 5.9 copy-start.20
where the time goes:
time: 685 us; the launch traced here: 674 us
  waiting for transfers between devices  286 us (42%)
  starting transfers between devices  225 us (33%)
  blocking collectives  79.2 us (12%)
  local copies, waits for them, and re-layouts  41.6 us (6%)
  matrix products  28.2 us (4%)
  other arithmetic  12.4 us (2%)
    all_to_all x12, waiting for transfers between devices, to_experts(): return lax.all_to_all(rows, 'dp', split_axis=0, concat_axis=0, tiled=True)  143 us
    all_to_all x12, starting transfers between devices, to_experts(): return lax.all_to_all(rows, 'dp', split_axis=0, concat_axis=0, tiled=True)  93.3 us
    all_gather x6, blocking collectives, sync_units(): portion = lax.all_gather(unit_stack, 'expert', axis=1, tiled=True)  79.2 us
    all_to_all x6, waiting for transfers between devices, to_tokens(): lax.all_to_all(lax.all_to_all(rows, 'expert', split_axis=1, concat_axis=0...  73.8 us
    all_to_all x12, starting transfers between devices, widen_rows(): lax.all_to_all(rows, 'expert', split_axis=0, concat_axis=1, tiled=True)  70.9 us
    all_to_all x12, waiting for transfers between devices, widen_rows(): lax.all_to_all(rows, 'expert', split_axis=0, concat_axis=1, tiled=True)  44.6 us
    all_to_all x6, starting transfers between devices, to_tokens(): lax.all_to_all(lax.all_to_all(rows, 'expert', split_axis=1, concat_axis=0...  35.8 us
    all_to_all x6, starting transfers between devices, to_tokens(): lax.all_to_all(rows, 'expert', split_axis=1, concat_axis=0, tiled=True)  24.5 us
  transfers between devices with their start and end apart: 36, of which 35 were waited for; matrix products, arithmetic and copies ran while one was open for 5% of the time, Pallas kernels for 0%

commit v1 on v0

v1 whole, which is shorter than its diff:
```python
import functools

import jax
import jax.numpy as jnp
from jax import lax
from jax.experimental import pallas as pl
from jax.experimental.pallas import tpu as pltpu
from jax.sharding import Mesh
from jax.sharding import PartitionSpec as P

F32 = jnp.float32
BF16 = jnp.bfloat16

NZ, NY, NE = 12, 8, 8
EXPERTS = NZ * NY
MICRO, BLOCK, TOPK, CAP = 6, 24, 8, 2
TOK = MICRO * BLOCK
SLOTS = MICRO * CAP
MSG = 2 * SLOTS
ROWS = EXPERTS * MSG
GROUP = NZ * MSG
HALF = 128
SLICE = 256
WIDTH = 2048
FF = 384
AUX = 128

beta_one = 0.9
beta_two = 0.95
adam_epsilon = 1e-08
learn_rate = 0.01
decay_rate = 0.1
first_fix = 0.99997343860111
second_fix = 0.994079470779666

NT = (((1,), (1,)), ((), ()))
NN = (((1,), (0,)), ((), ()))
TN = (((0,), (0,)), ((), ()))


def dot(left, right, dims=NN):
    return lax.dot_general(left, right, dims, preferred_element_type=F32)


def iota(shape, axis):
    return lax.broadcasted_iota(jnp.int32, shape, axis)


def params(megabytes):
    return pltpu.CompilerParams(vmem_limit_bytes=megabytes * 1024 * 1024)


def split_pair(value):
    high = value.astype(BF16)
    return high, (value - high.astype(F32)).astype(BF16)


def choices(aux):
    ids = aux[:, :TOPK].astype(jnp.int32)
    gates = aux[:, TOPK : 2 * TOPK] + aux[:, 2 * TOPK : 3 * TOPK] + aux[:, 3 * TOPK : 4 * TOPK]
    expert = iota((TOK, EXPERTS), 1)
    named = jnp.zeros((TOK, EXPERTS), F32)
    gate = jnp.zeros((TOK, EXPERTS), F32)
    for k in range(TOPK):
        hit = ids[:, k : k + 1] == expert
        named = jnp.where(hit, 1.0, named)
        gate = jnp.where(hit, gates[:, k : k + 1], gate)
    later, earlier = iota((TOK, TOK), 0), iota((TOK, TOK), 1)
    same = earlier <= later
    for edge in range(BLOCK, TOK, BLOCK):
        same = same & ((later >= edge) == (earlier >= edge))
    count = dot(same.astype(F32).astype(BF16), named.astype(BF16))
    return named * count, gate


def token_block(token):
    block = jnp.zeros(token.shape, jnp.int32)
    for edge in range(BLOCK, TOK, BLOCK):
        block = block + (token >= edge).astype(jnp.int32)
    return block


def row_expert_map():
    shape = (NY, NZ, MSG, EXPERTS)
    expert = iota(shape, 1) * NY + iota(shape, 0)
    return (expert == iota(shape, 3)).astype(F32).reshape(ROWS, EXPERTS).astype(BF16)


def row_slot(shape):
    place = iota(shape, 1)
    half = (place >= SLOTS).astype(jnp.int32)
    return half, place - SLOTS * half


def slot_hits(rank_rows):
    shape = (EXPERTS, MSG, TOK)
    _, slot = row_slot(shape)
    wanted = jnp.bitwise_and(slot, 1) + 1
    mine = jnp.right_shift(slot, 1) == token_block(iota(shape, 2))
    return mine & (rank_rows.reshape(shape).astype(jnp.int32) == wanted)


def pick_half(values):
    rows = values.shape[0]
    half, _ = row_slot((rows // MSG, MSG, HALF))
    return jnp.where(half.reshape(rows, HALF) == 0, values[:, :HALF], values[:, HALF:])


def dispatch_kernel(packed_ref, send_ref):
    packed = packed_ref[...]
    rank, _ = choices(packed[:, SLICE:].astype(F32))
    ranks = dot(row_expert_map(), rank.astype(BF16), NT)
    pick = slot_hits(ranks).astype(F32).reshape(ROWS, TOK).astype(BF16)
    send_ref[...] = pick_half(dot(pick, packed[:, :SLICE])).astype(BF16)


def weights_kernel(packed_ref, high_ref, low_ref, high_t_ref, low_t_ref):
    rank, gate = choices(packed_ref[:, SLICE:].astype(F32))
    spread = row_expert_map()
    rank = rank.astype(BF16)
    gate_high, gate_low = split_pair(gate)
    hits = slot_hits(dot(spread, rank, NT))
    weight = jnp.where(
        hits, (dot(spread, gate_high, NT) + dot(spread, gate_low, NT)).reshape(EXPERTS, MSG, TOK), 0.0
    ).reshape(ROWS, TOK)
    high, low = split_pair(weight)
    high_ref[...] = high
    low_ref[...] = low
    high_t_ref[...] = weight.T.astype(BF16)
    low_t_ref[...] = (weight - high.astype(F32)).T.astype(BF16)


def widen_rows(rows_ref, wide_ref):
    half, _ = row_slot((NZ, MSG, HALF))
    second = half.reshape(GROUP, HALF).astype(F32)
    first = (1.0 - second).astype(BF16)
    second = second.astype(BF16)
    for y in range(NY):
        part = rows_ref[pl.ds(y * GROUP, GROUP), :]
        wide_ref[:, pl.ds(y * SLICE, HALF)] = part * first
        wide_ref[:, pl.ds(y * SLICE + HALF, HALF)] = part * second


def add_halves(value):
    half, _ = row_slot((NZ, MSG, value.shape[1]))
    up = pltpu.roll(value, GROUP - SLOTS, 0)
    down = pltpu.roll(value, SLOTS, 0)
    return value + jnp.where(half.reshape(value.shape) == 0, up, down)


def compact_map(both):
    shape = (NZ * SLOTS, GROUP)
    row, column = iota(shape, 0), iota(shape, 1)
    source = row
    for edge in range(SLOTS, NZ * SLOTS, SLOTS):
        source = source + jnp.where(row >= edge, SLOTS, 0)
    hit = column == source
    if both:
        hit = hit | (column == source + SLOTS)
    return hit.astype(F32).astype(BF16)


def forward_kernel(rows_ref, w_in_ref, w_out_ref, out_ref, factors_ref, wide_ref):
    widen_rows(rows_ref, wide_ref)
    preacts = add_halves(dot(wide_ref[...], w_in_ref[...]))
    gate_pre = preacts[:, :FF]
    up_pre = preacts[:, FF:]
    sigmoid = jax.nn.sigmoid(gate_pre)
    silu = gate_pre * sigmoid
    hidden = (silu * up_pre).astype(BF16)
    slope = up_pre * sigmoid * (1.0 + gate_pre * (1.0 - sigmoid))
    compact = compact_map(False)
    factors_ref[:, :FF] = dot(compact, hidden).astype(BF16)
    factors_ref[:, FF : 2 * FF] = dot(compact, slope.astype(BF16)).astype(BF16)
    factors_ref[:, 2 * FF :] = dot(compact, silu.astype(BF16)).astype(BF16)
    for y in range(NY):
        part = dot(hidden, w_out_ref[:, pl.ds(y * SLICE, SLICE)])
        out_ref[pl.ds(y * GROUP, GROUP), :] = pick_half(part).astype(BF16)


def combine_kernel(back_ref, target_ref, high_ref, low_ref, high_t_ref, low_t_ref, mixed_ref, send_ref):
    half, _ = row_slot((EXPERTS, MSG, HALF))
    second = half.reshape(ROWS, HALF).astype(F32)
    rows = back_ref[...]
    wide = jnp.concatenate([rows * (1.0 - second).astype(BF16), rows * second.astype(BF16)], axis=1)
    mixed = (dot(high_t_ref[...], wide) + dot(low_t_ref[...], wide)).astype(BF16)
    mixed_ref[...] = mixed
    grad_high, grad_low = split_pair(mixed.astype(F32) - target_ref[...].astype(F32))
    spread = dot(high_ref[...], grad_high) + dot(high_ref[...], grad_low) + dot(low_ref[...], grad_high)
    send_ref[...] = pick_half(spread).astype(BF16)


def backward_kernel(rows_ref, w_out_ref, grad_ref, wide_ref):
    widen_rows(rows_ref, wide_ref)
    hidden_grad = add_halves(dot(wide_ref[...], w_out_ref[...], NT)).astype(BF16)
    grad_ref[...] = dot(compact_map(False), hidden_grad).astype(BF16)


def narrow_kernel(rows_ref, out_ref):
    half, _ = row_slot((NZ, MSG, HALF))
    second = half.reshape(GROUP, HALF).astype(F32)
    first = (1.0 - second).astype(BF16)
    second = second.astype(BF16)
    compact = compact_map(True)
    for y in range(NY):
        part = rows_ref[pl.ds(y * GROUP, GROUP), :]
        wide = jnp.concatenate([part * first, part * second], axis=1)
        out_ref[pl.ds(y * NZ * SLOTS, NZ * SLOTS), :] = dot(compact, wide).astype(BF16)


def shape_of(*dims, dtype=BF16):
    return jax.ShapeDtypeStruct(dims, dtype)


def call(kernel, out_shape, flops, size, scratch=()):
    return pl.pallas_call(
        kernel,
        out_shape=out_shape,
        scratch_shapes=scratch,
        compiler_params=params(48),
        cost_estimate=pl.CostEstimate(flops=flops, bytes_accessed=size, transcendentals=0),
    )


def adamw(weight, moment_one, moment_two, gradient):
    first_new = beta_one * moment_one.astype(F32) + (1.0 - beta_one) * gradient
    second_new = beta_two * moment_two.astype(F32) + (1.0 - beta_two) * gradient * gradient
    master = weight.astype(F32)
    update = (
        first_new / first_fix / (jnp.sqrt(second_new / second_fix) + adam_epsilon)
        + decay_rate * master
    )
    return (
        (master - learn_rate * update).astype(BF16),
        first_new.astype(BF16),
        second_new.astype(BF16),
    )


def change_places(value):
    pairs = [
        ((z * NY + y) * NE + e, (z * NY + e) * NE + y)
        for z in range(NZ)
        for y in range(NY)
        for e in range(NE)
    ]
    return lax.ppermute(value, ("z", "y", "x", "core"), pairs)


def over_experts(rows):
    messages = rows.reshape(EXPERTS, MSG, HALF)
    moved = lax.all_to_all(messages, ("y", "z"), split_axis=0, concat_axis=0, tiled=True)
    return moved.reshape(ROWS, HALF)


def slices_by_permutes(rows, column):
    blocks = rows.reshape(NY, GROUP, HALF)
    arrived = [lax.dynamic_index_in_dim(blocks, column, 0, keepdims=False)]
    for shift in range(1, NE):
        block = lax.dynamic_index_in_dim(blocks, lax.rem(column + shift, NE), 0, keepdims=False)
        pairs = [(e, (e + shift) % NE) for e in range(NE)]
        arrived.append(lax.ppermute(block, ("x", "core"), pairs))
    stacked = jnp.stack(arrived, axis=0)
    order = lax.rem(column - jnp.arange(NE, dtype=jnp.int32) + NE, NE)
    return jnp.take(stacked, order, axis=0).reshape(ROWS, HALF)


def shards(tokens, target, expert_ids, gate_weights, w_in, m_in, v_in, w_out, m_out, v_out):
    column = lax.axis_index(("x", "core"))
    w_gate_up = w_in.reshape(WIDTH, 2 * FF)
    w_down = w_out.reshape(FF, WIDTH)

    gate_high = lax.reduce_precision(gate_weights, 8, 7)
    gate_mid = lax.reduce_precision(gate_weights - gate_high, 8, 7)
    gate_last = gate_weights - gate_high - gate_mid
    gate_parts = jnp.concatenate([gate_high, gate_mid, gate_last], axis=1).astype(BF16)
    aux = jnp.concatenate([expert_ids.astype(BF16), gate_parts], axis=1)
    packed = jnp.concatenate([tokens, jnp.pad(aux, ((0, 0), (0, AUX - 4 * TOPK)))], axis=1)
    packed = change_places(packed)

    one_hot_flops = 2 * ROWS * TOK * SLICE
    send_rows = call(dispatch_kernel, shape_of(ROWS, HALF), 3 * one_hot_flops, 2 * ROWS * HALF)(packed)
    arrived = over_experts(send_rows)
    target_here = change_places(target)
    weights = call(
        weights_kernel,
        [shape_of(ROWS, TOK), shape_of(ROWS, TOK), shape_of(TOK, ROWS), shape_of(TOK, ROWS)],
        4 * one_hot_flops,
        8 * ROWS * TOK,
    )(packed)

    wide = [pltpu.VMEM((GROUP, WIDTH), BF16)]
    out_rows, factors = call(
        forward_kernel,
        [shape_of(ROWS, HALF), shape_of(NZ * SLOTS, 3 * FF)],
        6 * GROUP * WIDTH * FF,
        6 * WIDTH * FF,
        wide,
    )(arrived, w_gate_up, w_down)
    returned = over_experts(out_rows)
    all_factors = lax.all_gather(factors, ("x", "core"), axis=0, tiled=True)
    own_rows = slices_by_permutes(arrived, column)
    own_rows = call(narrow_kernel, shape_of(NE * NZ * SLOTS, SLICE), one_hot_flops, 4 * ROWS * HALF)(own_rows)

    mixed_here, slot_grad = call(
        combine_kernel,
        [shape_of(TOK, SLICE), shape_of(ROWS, HALF)],
        6 * one_hot_flops,
        8 * ROWS * TOK,
    )(returned, target_here, *weights)
    grads = over_experts(slot_grad)
    mixed = change_places(mixed_here)

    own_grads = lax.all_to_all(
        grads.reshape(NE, GROUP, HALF), ("x", "core"), split_axis=0, concat_axis=0, tiled=True
    ).reshape(ROWS, HALF)
    hidden_grad = call(
        backward_kernel, shape_of(NZ * SLOTS, FF), 2 * GROUP * WIDTH * FF, 2 * WIDTH * FF, wide
    )(grads, w_down)
    all_grads = lax.all_gather(hidden_grad, ("x", "core"), axis=0, tiled=True).astype(F32)
    own_grads = call(narrow_kernel, shape_of(NE * NZ * SLOTS, SLICE), one_hot_flops, 4 * ROWS * HALF)(own_grads)

    pre_grad = jnp.concatenate(
        [
            all_grads * all_factors[:, FF : 2 * FF].astype(F32),
            all_grads * all_factors[:, 2 * FF :].astype(F32),
        ],
        axis=1,
    ).astype(BF16)
    grad_up = dot(own_rows, pre_grad, TN)
    grad_down = dot(all_factors[:, :FF], own_grads, TN)

    w_in_own = lax.dynamic_slice_in_dim(w_in, column * SLICE, SLICE, 1)
    w_out_own = lax.dynamic_slice_in_dim(w_out, column * SLICE, SLICE, 2)
    new_w_in, new_m_in, new_v_in = adamw(w_in_own, m_in, v_in, grad_up.reshape(m_in.shape))
    new_w_out, new_m_out, new_v_out = adamw(w_out_own, m_out, v_out, grad_down.reshape(m_out.shape))
    return (mixed, new_w_in, new_m_in, new_v_in, new_w_out, new_m_out, new_v_out)


def solution(mesh):
    whole = Mesh(mesh.devices.reshape(NZ, NY, NE // 2, 2), ("z", "y", "x", "core"))
    dp, expert = ("z", "y"), ("x", "core")
    return jax.shard_map(
        shards,
        mesh=whole,
        in_specs=(
            P(dp, expert),
            P(dp, expert),
            P(dp, None),
            P(dp, None),
            P(dp, None, None, None),
            P(dp, expert, None, None),
            P(dp, expert, None, None),
            P(dp, None, None),
            P(dp, None, expert),
            P(dp, None, expert),
        ),
        out_specs=(
            P(dp, expert),
            P(dp, expert, None, None),
            P(dp, expert, None, None),
            P(dp, expert, None, None),
            P(dp, None, expert),
            P(dp, None, expert),
            P(dp, None, expert),
        ),
        check_vma=False,
    )
```

time: 685 us -> 209 us (0.31); the launches traced: 674 us -> 208 us
  waiting for transfers between devices: 286 us -> 36.2 us
  starting transfers between devices: 225 us -> 92.4 us
  blocking collectives: 79.2 us -> 16.8 us
  local copies, waits for them, and re-layouts: 41.6 us -> 17.6 us
  matrix products: 28.2 us -> 4.35 us
  Pallas kernels: 0 us -> 14.7 us
  between operations: 1.89 us -> 14.4 us
    all_to_all x36 -> x4, waiting for transfers between devices: 286 us -> 29.9 us  [the longest x3 29.9 us: over_experts(): lax.all_to_all(messages, ('y', 'z'), split_axis=0, concat_axis=0, tiled=T...]
    all_to_all x36 -> x4, starting transfers between devices: 225 us -> 57.8 us  [the longest x3 49 us: over_experts(): lax.all_to_all(messages, ('y', 'z'), split_axis=0, concat_axis=0, tiled=T...]
    all_gather x6 -> x1, blocking collectives: 79.2 us -> 16.8 us  [shards(): lax.all_gather(hidden_grad, ('x', 'core'), axis=0, tiled=True).astype(F32)]
    ppermute x0 -> x10, starting transfers between devices: none -> 34.6 us  [the longest x7 22.3 us: slices_by_permutes(): arrived.append(lax.ppermute(block, ('x', 'core'), pairs))]
    all_to_all x54 -> x0, local copies, waits for them, and re-layouts: 24.8 us -> none  [the longest x24 8.27 us: widen_rows(): lax.all_to_all(rows, 'expert', split_axis=0, concat_axis=1, tiled=True)]
    dot_general x48 -> x2, matrix products: 28.2 us -> 4.35 us  [dot(): return lax.dot_general(left, right, dims, preferred_element_type=F32)]
    pallas_call x0 -> x7, Pallas kernels: none -> 14.7 us  [the longest x1 5.3 us: shards(): call(forward_kernel, [shape_of(ROWS, HALF), shape_of(NZ * SLOTS, 3 * FF)]...]
    unnamed x49 -> x40, local copies, waits for them, and re-layouts: 6.23 us -> 14.1 us
  transfers between devices with their start and end apart: 36 -> 15, of which waited for: 35 -> 6; matrix products, arithmetic and copies ran while one was open for 5% -> 3% of each run, Pallas kernels for 0% -> 4%
where the time goes in v1:
time: 209 us; the launch traced here: 208 us
  starting transfers between devices  92.4 us (44%)
  waiting for transfers between devices  36.2 us (17%)
  local copies, waits for them, and re-layouts  17.6 us (8%)
  blocking collectives  16.8 us (8%)
  Pallas kernels  14.7 us (7%)
  between operations  14.4 us (7%)
  other arithmetic  11.6 us (6%)
  matrix products  4.35 us (2%)
    all_to_all x3, starting transfers between devices, over_experts(): lax.all_to_all(messages, ('y', 'z'), split_axis=0, concat_axis=0, tiled=T...  49 us
    all_to_all x3, waiting for transfers between devices, over_experts(): lax.all_to_all(messages, ('y', 'z'), split_axis=0, concat_axis=0, tiled=T...  29.9 us
    ppermute x7, starting transfers between devices, slices_by_permutes(): arrived.append(lax.ppermute(block, ('x', 'core'), pairs))  22.3 us
    all_gather x1, blocking collectives, shards(): lax.all_gather(hidden_grad, ('x', 'core'), axis=0, tiled=True).astype(F32)  16.8 us
    unnamed x40, local copies, waits for them, and re-layouts  14.1 us
    ppermute x3, starting transfers between devices, change_places(): return lax.ppermute(value, ('z', 'y', 'x', 'core'), pairs)  12.3 us
    all_to_all x1, starting transfers between devices, shards(): lax.all_to_all(grads.reshape(NE, GROUP, HALF), ('x', 'core'), split_axis=...  8.76 us
    convert_element_type x1, other arithmetic, adamw(): second_new.astype(BF16)  5.96 us
  transfers between devices with their start and end apart: 15, of which 6 were waited for; matrix products, arithmetic and copies ran while one was open for 3% of the time, Pallas kernels for 4%

profile of v1, /device:TPU:1, one launch (start us, length us, event | category | flops | bytes accessed | tf_op | source)
XLA Modules:
  0.0 208.1 jit_solution(16785862078784071040)
XLA Ops:
  7.2 0.7 reduce-precision_convert_fusion.1
  7.9 0.7 convert_element_type.52
  8.6 0.1 copy.20
  8.7 0.9 fusion.20
  9.6 4.6 %collective-permute-start = (bf16[144,384]{1,0:T(8,128)(2,1)S(1)}, bf16[144,384]{1,0:T(8,128)(2,1)S(1)}, u32[]{:S(2)}, u32[]{:S(2)}) collective-permute-start(bf16[144,384]{1,0:T(8,128)(2,1)S(1)} %fusion.20), channel_id=1, source_target_pairs={{0,0},{1,8},{2,16},{3,24},{4,32},{5,40},{6,48},{7,56},{8,1},{9,9},... | collective-permute-start | bytes 331784 | tf_op jit(solution)/shard_map/ppermute | solution.py:247
  14.2 2.4 %collective-permute-done.packed_ref = bf16[144,384]{1,0:T(8,128)(2,1)S(1)} collective-permute-done((bf16[144,384]{1,0:T(8,128)(2,1)S(1)}, bf16[144,384]{1,0:T(8,128)(2,1)S(1)}, u32[]{:S(2)}, u32[]{:S(2)}) %collective-permute-start) | collective-permute-done | bytes 110624 | tf_op jit(solution)/shard_map/ppermute | solution.py:247
  16.6 2.1 %shard_map.153 = bf16[2304,128]{1,0:T(8,128)(2,1)} custom-call(bf16[144,384]{1,0:T(8,128)(2,1)S(1)} %collective-permute-done.packed_ref), custom_call_target="tpu_custom_call" | custom-call | flops 509607936 | bytes 589824 | tf_op jit(solution)/shard_map/pallas_call | solution.py:282
  18.8 27.5 %all-to-all-start = ((bf16[96,24,128]{2,1,0:T(8,128)(2,1)}), bf16[96,24,128]{2,1,0:T(8,128)(2,1)S(1)}, u32[]{:S(2)}, u32[]{:S(2)}) async-start(bf16[96,24,128]{2,1,0:T(8,128)(2,1)} %bitcast), calls=%async_computation | async-start | bytes 1179648 | tf_op jit(solution)/shard_map/all_to_all | solution.py:252
  46.3 0.0 copy-start
  46.3 4.3 %copy.21 = bf16[256,8,2,384]{3,1,2,0:T(8,128)(2,1)} copy(bf16[256,8,2,384]{3,2,1,0:T(2,128)(2,1)} %bitcast.69) | data formatting | bytes 6291456
  50.6 18.9 %all-to-all-done = bf16[96,24,128]{2,1,0:T(8,128)(2,1)S(1)} async-done(((bf16[96,24,128]{2,1,0:T(8,128)(2,1)}), bf16[96,24,128]{2,1,0:T(8,128)(2,1)S(1)}, u32[]{:S(2)}, u32[]{:S(2)}) %all-to-all-start) | async-done | bytes 589856 | tf_op jit(solution)/shard_map/all_to_all | solution.py:252
  69.5 5.3 %shard_map.154 = (bf16[2304,128]{1,0:T(8,128)(2,1)}, bf16[144,1152]{1,0:T(8,128)(2,1)}) custom-call(bf16[2304,128]{1,0:T(8,128)(2,1)S(1)} %bitcast.63, bf16[2048,768]{1,0:T(8,128)(2,1)} %bitcast.68, bf16[384,2048]{1,0:T(8,128)(2,1)S(1)} %bitcast.61), custom_call_target="tpu_custom_call" | custom-call | flops 1358954496 | bytes 4718592 | tf_op jit(solution)/shard_map/pallas_call | solution.py:293
  74.8 10.6 %all-to-all-start.1 = ((bf16[96,24,128]{2,1,0:T(8,128)(2,1)}), bf16[96,24,128]{2,1,0:T(8,128)(2,1)S(1)}, u32[]{:S(2)}, u32[]{:S(2)}) async-start(bf16[96,24,128]{2,1,0:T(8,128)(2,1)} %bitcast.3), calls=%async_computation.1 | async-start | bytes 1179648 | tf_op jit(solution)/shard_map/all_to_all | solution.py:252
  85.3 0.0 all-gather.2.cloned.1.call-start
  85.4 0.7 all-gather.2.cloned.1.call-update
  86.1 5.4 %collective-permute-start.1 = (bf16[144,256]{1,0:T(8,128)(2,1)}, bf16[144,256]{1,0:T(8,128)(2,1)S(1)}, u32[]{:S(2)}, u32[]{:S(2)}) collective-permute-start(bf16[144,256]{1,0:T(8,128)(2,1)} %param.11), channel_id=1, source_target_pairs={{0,0},{1,8},{2,16},{3,24},{4,32},{5,40},{6,48},{7,56},{8,1},{9,9},... | collective-permute-start | bytes 221192 | tf_op jit(solution)/shard_map/ppermute | solution.py:247
  91.5 0.1 broadcast_in_dim.14
  91.6 0.1 broadcast_in_dim.15
  91.7 0.9 copy-done.9
  92.6 1.9 shard_map.155
  94.6 1.0 copy-done.1
  95.6 1.0 copy-done.3
  96.6 0.8 copy-done.5
  97.5 0.0 collective-permute-done.1.target_ref
  97.5 11.1 %all-to-all-done.1 = bf16[96,24,128]{2,1,0:T(8,128)(2,1)S(1)} async-done(((bf16[96,24,128]{2,1,0:T(8,128)(2,1)}), bf16[96,24,128]{2,1,0:T(8,128)(2,1)S(1)}, u32[]{:S(2)}, u32[]{:S(2)}) %all-to-all-start.1) | async-done | bytes 589856 | tf_op jit(solution)/shard_map/all_to_all | solution.py:252
  108.6 1.3 copy-done.2
  109.9 1.4 copy-done.4
  111.3 1.1 copy-done.6
  112.4 2.2 %shard_map.156 = (bf16[144,256]{1,0:T(8,128)(2,1)S(1)}, bf16[2304,128]{1,0:T(8,128)(2,1)S(1)}) custom-call(bf16[2304,128]{1,0:T(8,128)(2,1)S(1)} %bitcast.66, bf16[144,256]{1,0:T(8,128)(2,1)S(1)} %collective-permute-done.1.target_ref, bf16[2304,144]{1,0:T(8,128)(2,1)S(1)} %copy-done.2, bf16[2304,144]{1,0:T(8,128)(2,1)S(1)} %copy-done.4, ...), custom_call_target="tpu_custom_call" | custom-call | flops 1019215872 | bytes 2654208 | tf_op jit(solution)/shard_map/pallas_call | solution.py:305
  114.6 0.8 copy-done.7
  115.4 0.6 copy-done.10
  116.1 10.9 %all-to-all-start.2 = ((bf16[96,24,128]{2,1,0:T(8,128)(2,1)}), bf16[96,24,128]{2,1,0:T(8,128)(2,1)}, u32[]{:S(2)}, u32[]{:S(2)}) async-start(bf16[96,24,128]{2,1,0:T(8,128)(2,1)} %bitcast.67), calls=%async_computation.2 | async-start | bytes 1179648 | tf_op jit(solution)/shard_map/all_to_all | solution.py:252
  127.0 0.0 copy-start.11
  127.0 0.1 dynamic-slice_bitcast_fusion
  127.1 6.4 %collective-permute-start.3 = (bf16[288,128]{1,0:T(8,128)(2,1)S(1)}, bf16[288,128]{1,0:T(8,128)(2,1)S(1)}, u32[]{:S(2)}, u32[]{:S(2)}) collective-permute-start(bf16[288,128]{1,0:T(8,128)(2,1)S(1)} %get-tuple-element.37), channel_id=1, source_target_pairs={{0,1},{1,2},{2,3},{3,4},{4,5},{5,6},{6,7},{7,0},{8,9},{9,10},{10,1... | collective-permute-start | bytes 221192 | tf_op jit(solution)/shard_map/ppermute | solution.py:262
  133.5 1.9 collective-permute-start.4
  135.5 1.9 collective-permute-start.5
  137.4 5.2 %collective-permute-start.6 = (bf16[288,128]{1,0:T(8,128)(2,1)S(1)}, bf16[288,128]{1,0:T(8,128)(2,1)S(1)}, u32[]{:S(2)}, u32[]{:S(2)}) collective-permute-start(bf16[288,128]{1,0:T(8,128)(2,1)S(1)} %get-tuple-element.34), channel_id=1, source_target_pairs={{0,4},{1,5},{2,6},{3,7},{4,0},{5,1},{6,2},{7,3},{8,12},{9,13},{10,... | collective-permute-start | bytes 221192 | tf_op jit(solution)/shard_map/ppermute | solution.py:262
  142.6 1.9 collective-permute-start.7
  144.5 0.0 collective-permute-done.3
  144.5 3.0 %collective-permute-start.8 = (bf16[288,128]{1,0:T(8,128)(2,1)S(1)}, bf16[288,128]{1,0:T(8,128)(2,1)S(1)}, u32[]{:S(2)}, u32[]{:S(2)}) collective-permute-start(bf16[288,128]{1,0:T(8,128)(2,1)S(1)} %get-tuple-element.32), channel_id=1, source_target_pairs={{0,6},{1,7},{2,0},{3,1},{4,2},{5,3},{6,4},{7,5},{8,14},{9,15},{10,... | collective-permute-start | bytes 221192 | tf_op jit(solution)/shard_map/ppermute | solution.py:262
  147.6 0.0 collective-permute-done.4
  147.6 1.9 collective-permute-start.9
  149.5 0.0 collective-permute-done.5
  149.6 0.6 collective-permute-done.7
  150.1 1.3 collective-permute-done.8
  151.4 1.3 collective-permute-done.9
  152.7 0.7 gather_fusion
  153.4 2.3 %collective-permute-start.2 = (bf16[144,256]{1,0:T(8,128)(2,1)S(1)}, bf16[144,256]{1,0:T(8,128)(2,1)S(1)}, u32[]{:S(2)}, u32[]{:S(2)}) collective-permute-start(bf16[144,256]{1,0:T(8,128)(2,1)S(1)} %copy-done.11), channel_id=1, source_target_pairs={{0,0},{1,8},{2,16},{3,24},{4,32},{5,40},{6,48},{7,56},{8,1},{9,9},... | collective-permute-start | bytes 221192 | tf_op jit(solution)/shard_map/ppermute | solution.py:247
  155.7 0.0 all-to-all-done.2
  155.8 8.8 %all-to-all-start.3 = ((bf16[8,288,128]{2,1,0:T(8,128)(2,1)}), bf16[8,288,128]{2,1,0:T(8,128)(2,1)S(1)}, u32[]{:S(2)}, u32[]{:S(2)}) async-start(bf16[8,288,128]{2,1,0:T(8,128)(2,1)} %bitcast.24), calls=%async_computation.3 | async-start | bytes 1179648 | tf_op jit(solution)/shard_map/all_to_all | solution.py:314
  164.5 1.2 bitcast_select_fusion.rows_ref
  165.7 0.5 shard_map.157
  166.2 2.1 %shard_map.158 = bf16[144,384]{1,0:T(8,128)(2,1)S(1)} custom-call(bf16[2304,128]{1,0:T(8,128)(2,1)} %bitcast.23.rows_ref, bf16[384,2048]{1,0:T(8,128)(2,1)S(1)} %bitcast.62), custom_call_target="tpu_custom_call" | custom-call | flops 452984832 | bytes 1572864 | tf_op jit(solution)/shard_map/pallas_call | solution.py:317
  168.4 16.8 %all_gather.6 = bf16[1152,384]{1,0:T(8,128)(2,1)} all-gather(bf16[144,384]{1,0:T(8,128)(2,1)S(1)} %shard_map.158), channel_id=1, replica_groups=mesh['z'=12,'y'=8,'x'=4,'core'=2] {'x','core'}, dimensions={0}, use_global_device_ids=true | all-gather | bytes 995328 | tf_op jit(solution)/shard_map/all_gather | solution.py:320
  185.1 0.0 all-to-all-done.3
  185.1 0.5 shard_map.159
  185.6 0.0 all-gather.2.cloned.1.call-done
  185.7 2.1 %fusion = (bf16[1152,384]{1,0:T(8,128)(2,1)S(1)}, bf16[1152,384]{1,0:T(8,128)(2,1)S(1)}) fusion(bf16[1152,384]{1,0:T(8,128)(2,1)} %all_gather.6, bf16[1152,1152]{1,0:T(8,128)(2,1)} %all-gather.2.cloned.1.call-done), kind=kLoop, calls=%fused_computation.3 | loop fusion | flops 3096576 | bytes 4423680 | tf_op jit(solution)/shard_map/convert
  187.8 1.6 fusion.2
  189.4 2.5 %reshape.137 = f32[1,256,2,384]{3,2,1,0:T(2,128)} reshape(f32[256,768]{1,0:T(8,128)} %fusion.2) | data formatting | bytes 1572864 | tf_op jit(solution)/shard_map/reshape | solution.py:335
  191.9 6.0 %fusion.27 = (bf16[1,256,2,384]{3,2,1,0:T(2,128)(2,1)}, bf16[1,256,2,384]{3,2,1,0:T(2,128)(2,1)}, bf16[1,256,2,384]{3,2,1,0:T(2,128)(2,1)}) fusion(f32[1,256,2,384]{3,2,1,0:T(2,128)} %reshape.137, bf16[1,256,2,384]{3,2,1,0:T(2,128)(2,1)S(1)} %copy-done.12, bf16[1,256,2,384]{3,2,1,0:T(2,128)(2,1)S(1)} %copy-done.13, bf16[1,2048,2,384]{3,2,1,0:T(2,128)(2,1)} %param.14, ...), kind=kLoop, calls=%fused_computation.68 | loop fusion | flops 4128768 | bytes 3145732 | tf_op jit(solution)/shard_map/convert_element_type | solution.py:236
  197.9 2.7 %fusion.19 = (bf16[1,384,256]{2,1,0:T(8,128)(2,1)}, bf16[1,384,256]{2,1,0:T(8,128)(2,1)}, bf16[1,384,256]{2,1,0:T(8,128)(2,1)}) fusion(bf16[1,384,256]{2,1,0:T(8,128)(2,1)S(1)} %copy-done.14, bf16[1,384,256]{2,1,0:T(8,128)(2,1)S(1)} %copy-done.15, bf16[1,384,2048]{2,1,0:T(8,128)(2,1)S(1)} %copy-done, s32[]{:T(128)S(6)} %select_n.50, ...), kind=kOutput, calls=%fused_computation.32 | convolution fusion | flops 228556800 | bytes 2654212 | tf_op jit(solution)/shard_map/dot_general | solution.py:42
  200.6 0.6 copy.30
  (34 shorter events, 0.2 us)
Async XLA Ops:
  9.6 7.0 %collective-permute-start = (bf16[144,384]{1,0:T(8,128)(2,1)S(1)}, bf16[144,384]{1,0:T(8,128)(2,1)S(1)}, u32[]{:S(2)}, u32[]{:S(2)}) collective-permute-start(bf16[144,384]{1,0:T(8,128)(2,1)S(1)} %fusion.20), channel_id=1, source_target_pairs={{0,0},{1,8},{2,16},{3,24},{4,32},{5,40},{6,48},{7,56},{8,1},{9,9},... | collective-permute-start | bytes 331784 | tf_op jit(solution)/shard_map/ppermute | solution.py:247
  16.6 29.7 %copy-start.8 = (bf16[144,384]{1,0:T(8,128)(2,1)}, bf16[144,384]{1,0:T(8,128)(2,1)S(1)}, u32[]{:S(2)}) copy-start(bf16[144,384]{1,0:T(8,128)(2,1)S(1)} %collective-permute-done.packed_ref) | copy-start | bytes 331780
  18.8 50.7 %all-to-all-start = ((bf16[96,24,128]{2,1,0:T(8,128)(2,1)}), bf16[96,24,128]{2,1,0:T(8,128)(2,1)S(1)}, u32[]{:S(2)}, u32[]{:S(2)}) async-start(bf16[96,24,128]{2,1,0:T(8,128)(2,1)} %bitcast), calls=%async_computation | async-start | bytes 1179648 | tf_op jit(solution)/shard_map/all_to_all | solution.py:252
  46.3 23.2 %copy-start = (bf16[1,384,2048]{2,1,0:T(8,128)(2,1)S(1)}, bf16[1,384,2048]{2,1,0:T(8,128)(2,1)}, u32[]{:S(2)}) copy-start(bf16[1,384,2048]{2,1,0:T(8,128)(2,1)} %param.17) | copy-start | bytes 4718596
  74.8 33.8 %all-to-all-start.1 = ((bf16[96,24,128]{2,1,0:T(8,128)(2,1)}), bf16[96,24,128]{2,1,0:T(8,128)(2,1)S(1)}, u32[]{:S(2)}, u32[]{:S(2)}) async-start(bf16[96,24,128]{2,1,0:T(8,128)(2,1)} %bitcast.3), calls=%async_computation.1 | async-start | bytes 1179648 | tf_op jit(solution)/shard_map/all_to_all | solution.py:252
  85.3 100.3 %all-gather.2.cloned.1.call-start = ((), (), s32[]{:S(2)}) async-start(), calls=%async_computation.4 | async-start | bytes 2985984 | tf_op jit(solution)/shard_map/all_gather | solution.py:301
  86.1 11.4 %collective-permute-start.1 = (bf16[144,256]{1,0:T(8,128)(2,1)}, bf16[144,256]{1,0:T(8,128)(2,1)S(1)}, u32[]{:S(2)}, u32[]{:S(2)}) collective-permute-start(bf16[144,256]{1,0:T(8,128)(2,1)} %param.11), channel_id=1, source_target_pairs={{0,0},{1,8},{2,16},{3,24},{4,32},{5,40},{6,48},{7,56},{8,1},{9,9},... | collective-permute-start | bytes 221192 | tf_op jit(solution)/shard_map/ppermute | solution.py:247
  91.7 0.9 copy-start.9
  94.6 1.0 copy-start.1
  95.6 1.0 copy-start.3
  96.6 0.8 copy-start.5
  108.6 1.3 copy-start.2
  109.9 1.4 copy-start.4
  111.3 1.1 copy-start.6
  114.6 0.8 copy-start.7
  115.4 0.6 copy-start.10
  116.1 39.7 %all-to-all-start.2 = ((bf16[96,24,128]{2,1,0:T(8,128)(2,1)}), bf16[96,24,128]{2,1,0:T(8,128)(2,1)}, u32[]{:S(2)}, u32[]{:S(2)}) async-start(bf16[96,24,128]{2,1,0:T(8,128)(2,1)} %bitcast.67), calls=%async_computation.2 | async-start | bytes 1179648 | tf_op jit(solution)/shard_map/all_to_all | solution.py:252
  127.0 26.4 %copy-start.11 = (bf16[144,256]{1,0:T(8,128)(2,1)S(1)}, bf16[144,256]{1,0:T(8,128)(2,1)}, u32[]{:S(2)}) copy-start(bf16[144,256]{1,0:T(8,128)(2,1)} %copy-done.10) | copy-start | bytes 221188
  127.1 17.4 %collective-permute-start.3 = (bf16[288,128]{1,0:T(8,128)(2,1)S(1)}, bf16[288,128]{1,0:T(8,128)(2,1)S(1)}, u32[]{:S(2)}, u32[]{:S(2)}) collective-permute-start(bf16[288,128]{1,0:T(8,128)(2,1)S(1)} %get-tuple-element.37), channel_id=1, source_target_pairs={{0,1},{1,2},{2,3},{3,4},{4,5},{5,6},{6,7},{7,0},{8,9},{9,10},{10,1... | collective-permute-start | bytes 221192 | tf_op jit(solution)/shard_map/ppermute | solution.py:262
  133.5 14.0 %collective-permute-start.4 = (bf16[288,128]{1,0:T(8,128)(2,1)S(1)}, bf16[288,128]{1,0:T(8,128)(2,1)S(1)}, u32[]{:S(2)}, u32[]{:S(2)}) collective-permute-start(bf16[288,128]{1,0:T(8,128)(2,1)S(1)} %get-tuple-element.36), channel_id=1, source_target_pairs={{0,2},{1,3},{2,4},{3,5},{4,6},{5,7},{6,0},{7,1},{8,10},{9,11},{10,... | collective-permute-start | bytes 221192 | tf_op jit(solution)/shard_map/ppermute | solution.py:262
  135.5 14.1 %collective-permute-start.5 = (bf16[288,128]{1,0:T(8,128)(2,1)S(1)}, bf16[288,128]{1,0:T(8,128)(2,1)S(1)}, u32[]{:S(2)}, u32[]{:S(2)}) collective-permute-start(bf16[288,128]{1,0:T(8,128)(2,1)S(1)} %get-tuple-element.35), channel_id=1, source_target_pairs={{0,3},{1,4},{2,5},{3,6},{4,7},{5,0},{6,1},{7,2},{8,11},{9,12},{10,... | collective-permute-start | bytes 221192 | tf_op jit(solution)/shard_map/ppermute | solution.py:262
  137.4 12.2 %collective-permute-start.6 = (bf16[288,128]{1,0:T(8,128)(2,1)S(1)}, bf16[288,128]{1,0:T(8,128)(2,1)S(1)}, u32[]{:S(2)}, u32[]{:S(2)}) collective-permute-start(bf16[288,128]{1,0:T(8,128)(2,1)S(1)} %get-tuple-element.34), channel_id=1, source_target_pairs={{0,4},{1,5},{2,6},{3,7},{4,0},{5,1},{6,2},{7,3},{8,12},{9,13},{10,... | collective-permute-start | bytes 221192 | tf_op jit(solution)/shard_map/ppermute | solution.py:262
  142.6 7.6 %collective-permute-start.7 = (bf16[288,128]{1,0:T(8,128)(2,1)S(1)}, bf16[288,128]{1,0:T(8,128)(2,1)S(1)}, u32[]{:S(2)}, u32[]{:S(2)}) collective-permute-start(bf16[288,128]{1,0:T(8,128)(2,1)S(1)} %get-tuple-element.33), channel_id=1, source_target_pairs={{0,5},{1,6},{2,7},{3,0},{4,1},{5,2},{6,3},{7,4},{8,13},{9,14},{10,... | collective-permute-start | bytes 221192 | tf_op jit(solution)/shard_map/ppermute | solution.py:262
  144.5 6.9 %collective-permute-start.8 = (bf16[288,128]{1,0:T(8,128)(2,1)S(1)}, bf16[288,128]{1,0:T(8,128)(2,1)S(1)}, u32[]{:S(2)}, u32[]{:S(2)}) collective-permute-start(bf16[288,128]{1,0:T(8,128)(2,1)S(1)} %get-tuple-element.32), channel_id=1, source_target_pairs={{0,6},{1,7},{2,0},{3,1},{4,2},{5,3},{6,4},{7,5},{8,14},{9,15},{10,... | collective-permute-start | bytes 221192 | tf_op jit(solution)/shard_map/ppermute | solution.py:262
  147.6 5.1 %collective-permute-start.9 = (bf16[288,128]{1,0:T(8,128)(2,1)S(1)}, bf16[288,128]{1,0:T(8,128)(2,1)S(1)}, u32[]{:S(2)}, u32[]{:S(2)}) collective-permute-start(bf16[288,128]{1,0:T(8,128)(2,1)S(1)} %get-tuple-element.31), channel_id=1, source_target_pairs={{0,7},{1,0},{2,1},{3,2},{4,3},{5,4},{6,5},{7,6},{8,15},{9,8},{10,9... | collective-permute-start | bytes 221192 | tf_op jit(solution)/shard_map/ppermute | solution.py:262
  153.4 12.8 %collective-permute-start.2 = (bf16[144,256]{1,0:T(8,128)(2,1)S(1)}, bf16[144,256]{1,0:T(8,128)(2,1)S(1)}, u32[]{:S(2)}, u32[]{:S(2)}) collective-permute-start(bf16[144,256]{1,0:T(8,128)(2,1)S(1)} %copy-done.11), channel_id=1, source_target_pairs={{0,0},{1,8},{2,16},{3,24},{4,32},{5,40},{6,48},{7,56},{8,1},{9,9},... | collective-permute-start | bytes 221192 | tf_op jit(solution)/shard_map/ppermute | solution.py:247
  155.8 29.4 %all-to-all-start.3 = ((bf16[8,288,128]{2,1,0:T(8,128)(2,1)}), bf16[8,288,128]{2,1,0:T(8,128)(2,1)S(1)}, u32[]{:S(2)}, u32[]{:S(2)}) async-start(bf16[8,288,128]{2,1,0:T(8,128)(2,1)} %bitcast.24), calls=%async_computation.3 | async-start | bytes 1179648 | tf_op jit(solution)/shard_map/all_to_all | solution.py:314
  189.4 2.5 %copy-start.12 = (bf16[1,256,2,384]{3,2,1,0:T(2,128)(2,1)S(1)}, bf16[1,256,2,384]{3,2,1,0:T(2,128)(2,1)}, u32[]{:S(2)}) copy-start(bf16[1,256,2,384]{3,2,1,0:T(2,128)(2,1)} %param.16) | copy-start | bytes 1179652
  189.4 2.5 %copy-start.13 = (bf16[1,256,2,384]{3,2,1,0:T(2,128)(2,1)S(1)}, bf16[1,256,2,384]{3,2,1,0:T(2,128)(2,1)}, u32[]{:S(2)}) copy-start(bf16[1,256,2,384]{3,2,1,0:T(2,128)(2,1)} %param.15) | copy-start | bytes 1179652
  191.9 6.0 %copy-start.14 = (bf16[1,384,256]{2,1,0:T(8,128)(2,1)S(1)}, bf16[1,384,256]{2,1,0:T(8,128)(2,1)}, u32[]{:S(2)}) copy-start(bf16[1,384,256]{2,1,0:T(8,128)(2,1)} %param.19) | copy-start | bytes 589828
  191.9 6.0 %copy-start.15 = (bf16[1,384,256]{2,1,0:T(8,128)(2,1)S(1)}, bf16[1,384,256]{2,1,0:T(8,128)(2,1)}, u32[]{:S(2)}) copy-start(bf16[1,384,256]{2,1,0:T(8,128)(2,1)} %param.18) | copy-start | bytes 589828
Sparse Core Ops, SparseCore 0:
  89.2 37.1 all-gather.1

commit v2 on v1

v2 whole, which is shorter than its diff:
```python
import jax
import jax.numpy as jnp
from jax import lax
from jax.experimental import pallas as pl
from jax.experimental.pallas import tpu as pltpu
from jax.sharding import Mesh
from jax.sharding import PartitionSpec as P

F32 = jnp.float32
BF16 = jnp.bfloat16

NZ, NY, NE = 12, 8, 8
EXPERTS = NZ * NY
MICRO, BLOCK, TOPK, CAP = 6, 24, 8, 2
TOK = MICRO * BLOCK
SLOTS = MICRO * CAP
MSG = 2 * SLOTS
ROWS = EXPERTS * MSG
GROUP = NZ * MSG
HALF = 128
SLICE = 256
WIDTH = 2048
FF = 384
CHIPS = NE // 2
CHUNK = NZ * SLOTS
EXPERT_ROWS = NE * CHUNK
LANES = FF // HALF
FACTORS = 3 * LANES * CHUNK
PART = 2 * GROUP + FACTORS
FAR = GROUP + FACTORS

beta_one = 0.9
beta_two = 0.95
adam_epsilon = 1e-08
learn_rate = 0.01
decay_rate = 0.1
first_fix = 0.99997343860111
second_fix = 0.994079470779666

NT = (((1,), (1,)), ((), ()))
NN = (((1,), (0,)), ((), ()))


def dot(left, right, dims=NN):
    return lax.dot_general(left, right, dims, preferred_element_type=F32)


def iota(shape, axis):
    return lax.broadcasted_iota(jnp.int32, shape, axis)


def split_pair(value):
    high = value.astype(BF16)
    return high, (value - high.astype(F32)).astype(BF16)


def choices(aux):
    expert = iota((EXPERTS, TOK), 0)
    ids = aux[:TOPK].astype(jnp.int32)
    named = jnp.zeros((EXPERTS, TOK), F32)
    gate = jnp.zeros((EXPERTS, TOK), F32)
    for k in range(TOPK):
        hit = ids[k : k + 1] == expert
        named = jnp.where(hit, 1.0, named)
        gate = jnp.where(hit, aux[TOPK + k : TOPK + k + 1], gate)
    earlier, later = iota((TOK, TOK), 0), iota((TOK, TOK), 1)
    same = earlier <= later
    for edge in range(BLOCK, TOK, BLOCK):
        same = same & ((later >= edge) == (earlier >= edge))
    count = dot(named.astype(BF16), same.astype(F32).astype(BF16))
    return named * count, gate


def token_block(token):
    block = jnp.zeros(token.shape, jnp.int32)
    for edge in range(BLOCK, TOK, BLOCK):
        block = block + (token >= edge).astype(jnp.int32)
    return block


def row_expert_map():
    shape = (NY, NZ, MSG, EXPERTS)
    expert = iota(shape, 1) * NY + iota(shape, 0)
    return (expert == iota(shape, 3)).astype(F32).reshape(ROWS, EXPERTS).astype(BF16)


def row_slot(shape):
    place = iota(shape, 1)
    half = (place >= SLOTS).astype(jnp.int32)
    return half, place - SLOTS * half


def slot_hits(rank_rows):
    shape = (EXPERTS, MSG, TOK)
    _, slot = row_slot(shape)
    wanted = jnp.bitwise_and(slot, 1) + 1
    mine = jnp.right_shift(slot, 1) == token_block(iota(shape, 2))
    return mine & (rank_rows.reshape(shape).astype(jnp.int32) == wanted)


def pick_half(values):
    rows = values.shape[0]
    half, _ = row_slot((rows // MSG, MSG, HALF))
    return jnp.where(half.reshape(rows, HALF) == 0, values[:, :HALF], values[:, HALF:])


def dispatch_kernel(tokens_ref, aux_ref, send_ref):
    rank, _ = choices(aux_ref[...])
    ranks = dot(row_expert_map(), rank.astype(BF16))
    pick = slot_hits(ranks).astype(F32).reshape(ROWS, TOK).astype(BF16)
    send_ref[...] = pick_half(dot(pick, tokens_ref[...])).astype(BF16)


def weights_kernel(aux_ref, high_ref, low_ref, high_t_ref, low_t_ref):
    rank, gate = choices(aux_ref[...])
    spread = row_expert_map()
    gate_high, gate_low = split_pair(gate)
    hits = slot_hits(dot(spread, rank.astype(BF16)))
    gates = (dot(spread, gate_high) + dot(spread, gate_low)).reshape(EXPERTS, MSG, TOK)
    weight = jnp.where(hits, gates, 0.0).reshape(ROWS, TOK)
    high, low = split_pair(weight)
    high_ref[...] = high
    low_ref[...] = low
    high_t_ref[...] = weight.T.astype(BF16)
    low_t_ref[...] = (weight - high.astype(F32)).T.astype(BF16)


def widen_rows(rows_ref, wide_ref):
    first, second = half_masks()
    for y in range(NY):
        part = rows_ref[pl.ds(y * GROUP, GROUP), :]
        wide_ref[:, pl.ds(y * SLICE, HALF)] = part * first
        wide_ref[:, pl.ds(y * SLICE + HALF, HALF)] = part * second


def add_halves(value):
    half, _ = row_slot((NZ, MSG, value.shape[1]))
    up = pltpu.roll(value, GROUP - SLOTS, 0)
    down = pltpu.roll(value, SLOTS, 0)
    return value + jnp.where(half.reshape(value.shape) == 0, up, down)


def compact_map(both):
    shape = (NZ * SLOTS, GROUP)
    row, column = iota(shape, 0), iota(shape, 1)
    source = row
    for edge in range(SLOTS, NZ * SLOTS, SLOTS):
        source = source + jnp.where(row >= edge, SLOTS, 0)
    hit = column == source
    if both:
        hit = hit | (column == source + SLOTS)
    return hit.astype(F32).astype(BF16)


def forward_kernel(rows_ref, w_in_ref, w_out_ref, out_ref, factors_ref, wide_ref):
    widen_rows(rows_ref, wide_ref)
    preacts = add_halves(dot(wide_ref[...], w_in_ref[...]))
    gate_pre = preacts[:, :FF]
    up_pre = preacts[:, FF:]
    sigmoid = jax.nn.sigmoid(gate_pre)
    silu = gate_pre * sigmoid
    hidden = (silu * up_pre).astype(BF16)
    slope = up_pre * sigmoid * (1.0 + gate_pre * (1.0 - sigmoid))
    compact = compact_map(False)
    for i, factor in enumerate((hidden, slope.astype(BF16), silu.astype(BF16))):
        values = dot(compact, factor).astype(BF16)
        for j in range(FF // HALF):
            place = (i * (FF // HALF) + j) * CHUNK
            factors_ref[pl.ds(place, CHUNK), :] = values[:, j * HALF : (j + 1) * HALF]
    for y in range(NY):
        part = dot(hidden, w_out_ref[:, pl.ds(y * SLICE, SLICE)])
        out_ref[pl.ds(y * GROUP, GROUP), :] = pick_half(part).astype(BF16)


def combine_kernel(back_ref, target_ref, high_ref, low_ref, high_t_ref, low_t_ref, mixed_ref, send_ref):
    half, _ = row_slot((EXPERTS, MSG, HALF))
    second = half.reshape(ROWS, HALF).astype(F32)
    rows = back_ref[...]
    wide = jnp.concatenate([rows * (1.0 - second).astype(BF16), rows * second.astype(BF16)], axis=1)
    mixed = (dot(high_t_ref[...], wide) + dot(low_t_ref[...], wide)).astype(BF16)
    mixed_ref[...] = mixed
    grad_high, grad_low = split_pair(mixed.astype(F32) - target_ref[...].astype(F32))
    spread = dot(high_ref[...], grad_high) + dot(high_ref[...], grad_low) + dot(low_ref[...], grad_high)
    send_ref[...] = pick_half(spread).astype(BF16)


def backward_kernel(rows_ref, w_out_ref, grad_ref, wide_ref):
    widen_rows(rows_ref, wide_ref)
    hidden_grad = add_halves(dot(wide_ref[...], w_out_ref[...], NT)).astype(BF16)
    grad_ref[...] = dot(compact_map(False), hidden_grad).astype(BF16)


def narrow(part, compact, first, second):
    return dot(compact, jnp.concatenate([part * first, part * second], axis=1))


def half_masks():
    half, _ = row_slot((NZ, MSG, HALF))
    second = half.reshape(GROUP, HALF).astype(F32)
    return (1.0 - second).astype(BF16), second.astype(BF16)


def rows_for(x, shift):
    return pl.multiple_of(2 * GROUP * lax.rem(x + shift, CHIPS), 2 * GROUP)


def parts_kernel(place_ref, rows_ref, factors_ref, *part_refs):
    for shift, part_ref in enumerate(part_refs, 1):
        part_ref[: 2 * GROUP, :] = rows_ref[pl.ds(rows_for(place_ref[0], shift), 2 * GROUP), :]
        part_ref[2 * GROUP :, :] = factors_ref[...]


def far_kernel(place_ref, rows_ref, factors_ref, part1, part2, part3, far_ref):
    x, core = place_ref[0], place_ref[1]
    across = pl.multiple_of((1 - core) * GROUP, GROUP)
    for shift, part_ref in enumerate((None, part1, part2, part3)):
        if shift:
            rows, factors = part_ref[pl.ds(across, GROUP), :], part_ref[2 * GROUP :, :]
        else:
            rows = rows_ref[pl.ds(pl.multiple_of(rows_for(x, 0) + across, GROUP), GROUP), :]
            factors = factors_ref[...]
        far_ref[pl.ds(shift * FAR, GROUP), :] = rows
        far_ref[pl.ds(shift * FAR + GROUP, FACTORS), :] = factors


def prepare_kernel(
    place_ref,
    near_rows_ref,
    near_factors_ref,
    part1,
    part2,
    part3,
    far_ref,
    rows_t_ref,
    hidden_t_ref,
    slopes_ref,
    rows_ref,
    hidden_ref,
):
    x, core = place_ref[0], place_ref[1]
    masks = (compact_map(True), *half_masks())
    same = pl.multiple_of(core * GROUP, GROUP)
    for other in range(2):
        for shift, part_ref in enumerate((None, part1, part2, part3)):
            source = 2 * lax.rem(x + (CHIPS - shift), CHIPS) + (1 - core if other else core)
            own = pl.ds(pl.multiple_of(source * CHUNK, CHUNK), CHUNK)
            if other:
                rows_of, first_row, factors_of, offset = far_ref, shift * FAR, far_ref, shift * FAR + GROUP
            elif shift:
                rows_of, first_row, factors_of, offset = part_ref, same, part_ref, 2 * GROUP
            else:
                first_row = pl.multiple_of(rows_for(x, 0) + same, GROUP)
                rows_of, factors_of, offset = near_rows_ref, near_factors_ref, 0
            rows_ref[own, :] = narrow(rows_of[pl.ds(first_row, GROUP), :], *masks)
            for j in range(LANES):
                value = factors_of[pl.ds(offset + j * CHUNK, CHUNK), :]
                hidden_ref[own, pl.ds(j * HALF, HALF)] = value.astype(F32)
            for j in range(2 * LANES):
                value = factors_of[pl.ds(offset + (LANES + j) * CHUNK, CHUNK), :]
                slopes_ref[own, pl.ds(j * HALF, HALF)] = value
    rows_t_ref[...] = rows_ref[...].T.astype(BF16)
    hidden_t_ref[...] = hidden_ref[...].T.astype(BF16)


def adamw(weight, moment_one, moment_two, gradient):
    first_new = beta_one * moment_one.astype(F32) + (1.0 - beta_one) * gradient
    second_new = beta_two * moment_two.astype(F32) + (1.0 - beta_two) * gradient * gradient
    master = weight.astype(F32)
    update = (
        first_new / first_fix / (jnp.sqrt(second_new / second_fix) + adam_epsilon)
        + decay_rate * master
    )
    return (
        (master - learn_rate * update).astype(BF16),
        first_new.astype(BF16),
        second_new.astype(BF16),
    )


def update_kernel(
    grads_ref,
    hidden_grad_ref,
    slopes_ref,
    rows_t_ref,
    hidden_t_ref,
    w_in_ref,
    m_in_ref,
    v_in_ref,
    w_out_ref,
    m_out_ref,
    v_out_ref,
    new_w_in_ref,
    new_m_in_ref,
    new_v_in_ref,
    new_w_out_ref,
    new_m_out_ref,
    new_v_out_ref,
    own_ref,
):
    masks = (compact_map(True), *half_masks())
    for source in range(NE):
        part = grads_ref[pl.ds(source * GROUP, GROUP), :]
        own_ref[pl.ds(source * CHUNK, CHUNK), :] = narrow(part, *masks).astype(BF16)
    grad_down = dot(hidden_t_ref[...], own_ref[...])
    new_w_out_ref[...], new_m_out_ref[...], new_v_out_ref[...] = adamw(
        w_out_ref[...], m_out_ref[...], v_out_ref[...], grad_down
    )
    hidden_grad = hidden_grad_ref[...].astype(F32)
    for i in range(2):
        columns = pl.ds(i * FF, FF)
        pre_grad = (hidden_grad * slopes_ref[:, columns].astype(F32)).astype(BF16)
        grad_up = dot(rows_t_ref[...], pre_grad)
        new_w_in_ref[:, columns], new_m_in_ref[:, columns], new_v_in_ref[:, columns] = adamw(
            w_in_ref[:, columns], m_in_ref[:, columns], v_in_ref[:, columns], grad_up
        )


def shape_of(*dims, dtype=BF16):
    return jax.ShapeDtypeStruct(dims, dtype)


def call(kernel, out_shape, flops, size, megabytes, scratch=(), in_specs=None):
    specs = {} if in_specs is None else {"in_specs": in_specs}
    return pl.pallas_call(
        kernel,
        out_shape=out_shape,
        scratch_shapes=scratch,
        compiler_params=pltpu.CompilerParams(vmem_limit_bytes=megabytes * 1024 * 1024),
        cost_estimate=pl.CostEstimate(flops=flops, bytes_accessed=size, transcendentals=0),
        **specs,
    )


def change_places(value):
    pairs = [
        ((z * NY + y) * NE + e, (z * NY + e) * NE + y)
        for z in range(NZ)
        for y in range(NY)
        for e in range(NE)
    ]
    return lax.ppermute(value, ("z", "y", "x", "core"), pairs)


def over_experts(rows):
    messages = rows.reshape(EXPERTS, MSG, HALF)
    moved = lax.all_to_all(messages, ("y", "z"), split_axis=0, concat_axis=0, tiled=True)
    return moved.reshape(ROWS, HALF)


def shards(tokens, target, expert_ids, gate_weights, w_in, m_in, v_in, w_out, m_out, v_out):
    x, core = lax.axis_index("x"), lax.axis_index("core")
    column = 2 * x + core
    w_gate_up = w_in.reshape(WIDTH, 2 * FF)
    w_down = w_out.reshape(FF, WIDTH)

    tokens_here = change_places(tokens)
    aux = change_places(jnp.concatenate([expert_ids.T.astype(F32), gate_weights.T], axis=0))
    one_hot_flops = 2 * ROWS * TOK * SLICE
    send_rows = call(dispatch_kernel, shape_of(ROWS, HALF), 3 * one_hot_flops, 2 * ROWS * HALF, 16)(
        tokens_here, aux
    )
    arrived = over_experts(send_rows)
    target_here = change_places(target)
    weights = call(
        weights_kernel,
        [shape_of(ROWS, TOK), shape_of(ROWS, TOK), shape_of(TOK, ROWS), shape_of(TOK, ROWS)],
        4 * one_hot_flops,
        8 * ROWS * TOK,
        16,
    )(aux)
    arrived, target_here, *weights = lax.optimization_barrier((arrived, target_here, *weights))

    wide = [pltpu.VMEM((GROUP, WIDTH), BF16)]
    out_rows, factors = call(
        forward_kernel,
        [shape_of(ROWS, HALF), shape_of(FACTORS, HALF)],
        6 * GROUP * WIDTH * FF,
        6 * WIDTH * FF,
        61,
        wide,
    )(arrived, w_gate_up, w_down)
    returned = over_experts(out_rows)
    vmem = pl.BlockSpec(memory_space=pltpu.VMEM)
    placed = [pl.BlockSpec(memory_space=pltpu.SMEM)]
    place = jnp.stack([x, core]).astype(jnp.int32)
    parts = call(
        parts_kernel, [shape_of(PART, HALF)] * 3, 0, 4 * PART * HALF, 8, (), placed + [vmem] * 2
    )(place, arrived, factors)
    parts = [
        lax.ppermute(part, "x", [(i, (i + shift) % CHIPS) for i in range(CHIPS)])
        for shift, part in enumerate(parts, 1)
    ]

    mixed_here, slot_grad = call(
        combine_kernel,
        [shape_of(TOK, SLICE), shape_of(ROWS, HALF)],
        6 * one_hot_flops,
        8 * ROWS * TOK,
        61,
    )(returned, target_here, *weights)
    grads = over_experts(slot_grad)
    mixed = change_places(mixed_here)
    slot_grad, *parts = lax.optimization_barrier((slot_grad, *parts))
    far = call(
        far_kernel, shape_of(CHIPS * FAR, HALF), 0, 4 * CHIPS * FAR * HALF, 16, (), placed + [vmem] * 5
    )(place, arrived, factors, *parts)
    far = lax.ppermute(far, "core", [(0, 1), (1, 0)])
    rows_t, hidden_t, slopes = call(
        prepare_kernel,
        [shape_of(SLICE, EXPERT_ROWS), shape_of(FF, EXPERT_ROWS), shape_of(EXPERT_ROWS, 2 * FF)],
        2 * one_hot_flops,
        8 * EXPERT_ROWS * FF,
        20,
        [pltpu.VMEM((EXPERT_ROWS, SLICE), F32), pltpu.VMEM((EXPERT_ROWS, FF), F32)],
        placed + [vmem] * 6,
    )(place, arrived, factors, *parts, far)
    grads, mixed, rows_t, hidden_t, slopes = lax.optimization_barrier(
        (grads, mixed, rows_t, hidden_t, slopes)
    )

    own_grads = lax.all_to_all(
        grads.reshape(NE, GROUP, HALF), ("x", "core"), split_axis=0, concat_axis=0, tiled=True
    ).reshape(ROWS, HALF)
    hidden_grad = call(
        backward_kernel, shape_of(CHUNK, FF), 2 * GROUP * WIDTH * FF, 2 * WIDTH * FF, 62, wide
    )(grads, w_down)
    all_grads = lax.all_gather(hidden_grad, ("x", "core"), axis=0, tiled=True)

    flat_in, flat_out = (SLICE, 2 * FF), (FF, SLICE)
    new_in = [shape_of(*flat_in)] * 3
    new_out = [shape_of(*flat_out)] * 3
    w_in_own = lax.dynamic_slice_in_dim(w_gate_up, column * SLICE, SLICE, 0)
    w_out_own = lax.dynamic_slice_in_dim(w_down, column * SLICE, SLICE, 1)
    updated = call(
        update_kernel,
        new_in + new_out,
        6 * EXPERT_ROWS * SLICE * FF,
        16 * SLICE * FF,
        61,
        [pltpu.VMEM((EXPERT_ROWS, SLICE), BF16)],
    )(
        own_grads,
        all_grads,
        slopes,
        rows_t,
        hidden_t,
        w_in_own,
        m_in.reshape(flat_in),
        v_in.reshape(flat_in),
        w_out_own,
        m_out.reshape(flat_out),
        v_out.reshape(flat_out),
    )
    new_w_in, new_m_in, new_v_in = (value.reshape(m_in.shape) for value in updated[:3])
    new_w_out, new_m_out, new_v_out = (value.reshape(m_out.shape) for value in updated[3:])
    return (mixed, new_w_in, new_m_in, new_v_in, new_w_out, new_m_out, new_v_out)


def solution(mesh):
    whole = Mesh(mesh.devices.reshape(NZ, NY, NE // 2, 2), ("z", "y", "x", "core"))
    dp, expert = ("z", "y"), ("x", "core")
    return jax.shard_map(
        shards,
        mesh=whole,
        in_specs=(
            P(dp, expert),
            P(dp, expert),
            P(dp, None),
            P(dp, None),
            P(dp, None, None, None),
            P(dp, expert, None, None),
            P(dp, expert, None, None),
            P(dp, None, None),
            P(dp, None, expert),
            P(dp, None, expert),
        ),
        out_specs=(
            P(dp, expert),
            P(dp, expert, None, None),
            P(dp, expert, None, None),
            P(dp, expert, None, None),
            P(dp, None, expert),
            P(dp, None, expert),
            P(dp, None, expert),
        ),
        check_vma=False,
    )
```

time: 209 us -> 189 us (0.904)
  Pallas kernels: 14.7 us -> 30.3 us
  between operations: 14.4 us -> 0.87 us
  other arithmetic: 11.6 us -> 1.48 us
  starting transfers between devices: 92.4 us -> 83.8 us
  local copies, waits for them, and re-layouts: 17.6 us -> 24.8 us
  waiting for transfers between devices: 36.2 us -> 31.2 us
  matrix products: 4.35 us -> 0 us
    pallas_call x4 -> x6, Pallas kernels: 8.39 us -> 21.5 us  [the longest x1 6.28 us: shards(): call(update_kernel, new_in + new_out, 6 * EXPERT_ROWS * SLICE * FF, 16 *...]
    ppermute x7 -> x4, starting transfers between devices: 22.3 us -> 12.8 us  [the longest x3 8.66 us: shards(): lax.ppermute(part, 'x', [(i, (i + shift) % CHIPS) for i in range(CHIPS)])]
    convert_element_type x2 -> x1, other arithmetic: 6.66 us -> 0.7 us  [shards(): expert_ids.T.astype(F32)]
    dot_general x2 -> x0, matrix products: 4.35 us -> none  [dot(): return lax.dot_general(left, right, dims, preferred_element_type=F32)]
    dynamic_slice x0 -> x2, local copies, waits for them, and re-layouts: none -> 3.39 us  [the longest x1 1.77 us: shards(): w_in_own = lax.dynamic_slice_in_dim(w_gate_up, column * SLICE, SLICE, 0)]
    pallas_call x1, Pallas kernels: 2.25 us -> 5.37 us  [shards(): call(combine_kernel, [shape_of(TOK, SLICE), shape_of(ROWS, HALF)], 6 * on...]
    ppermute x7 -> x4, waiting for transfers between devices: 3.12 us -> 0.01 us  [the longest x3 0.01 us: shards(): lax.ppermute(part, 'x', [(i, (i + shift) % CHIPS) for i in range(CHIPS)])]
    unnamed x40 -> x42, local copies, waits for them, and re-layouts: 14.1 us -> 16.9 us
  transfers between devices with their start and end apart: 15 -> 12, of which waited for: 6 -> 4; matrix products, arithmetic and copies ran while one was open for 3% -> 6% of each run, Pallas kernels for 4% -> 9%
where the time goes in v2:
time: 189 us; the launch traced here: 188 us
  starting transfers between devices  83.8 us (44%)
  waiting for transfers between devices  31.2 us (17%)
  Pallas kernels  30.3 us (16%)
  local copies, waits for them, and re-layouts  24.8 us (13%)
  blocking collectives  15.7 us (8%)
    all_to_all x3, starting transfers between devices, over_experts(): lax.all_to_all(messages, ('y', 'z'), split_axis=0, concat_axis=0, tiled=T...  48.5 us
    all_to_all x3, waiting for transfers between devices, over_experts(): lax.all_to_all(messages, ('y', 'z'), split_axis=0, concat_axis=0, tiled=T...  27.9 us
    unnamed x42, local copies, waits for them, and re-layouts  16.9 us
    all_gather x1, blocking collectives, shards(): all_grads = lax.all_gather(hidden_grad, ('x', 'core'), axis=0, tiled=True)  15.7 us
    ppermute x4, starting transfers between devices, change_places(): return lax.ppermute(value, ('z', 'y', 'x', 'core'), pairs)  14.4 us
    ppermute x3, starting transfers between devices, shards(): lax.ppermute(part, 'x', [(i, (i + shift) % CHIPS) for i in range(CHIPS)])  8.66 us
    all_to_all x1, starting transfers between devices, shards(): lax.all_to_all(grads.reshape(NE, GROUP, HALF), ('x', 'core'), split_axis=...  8.16 us
    pallas_call x1, Pallas kernels, shards(): call(update_kernel, new_in + new_out, 6 * EXPERT_ROWS * SLICE * FF, 16 *...  6.28 us
  transfers between devices with their start and end apart: 12, of which 4 were waited for; matrix products, arithmetic and copies ran while one was open for 6% of the time, Pallas kernels for 9%

profile of v2, /device:TPU:1, one launch (start us, length us, event | category | flops | bytes accessed | tf_op | source)
XLA Modules:
  0.0 188.2 jit_solution(1046673025023870159)
XLA Ops:
  0.6 0.0 copy-start.17
  0.6 4.7 %collective-permute-start = (bf16[144,256]{1,0:T(8,128)(2,1)}, bf16[144,256]{1,0:T(8,128)(2,1)S(1)}, u32[]{:S(2)}, u32[]{:S(2)}) collective-permute-start(bf16[144,256]{1,0:T(8,128)(2,1)} %param.10), channel_id=1, source_target_pairs={{0,0},{1,8},{2,16},{3,24},{4,32},{5,40},{6,48},{7,56},{8,1},{9,9},... | collective-permute-start | bytes 221192 | tf_op jit(solution)/shard_map/ppermute | solution.py:341
  5.4 0.7 convert_bitcast_fusion
  6.1 0.7 pad_maximum_fusion
  6.8 1.9 %collective-permute-start.1 = (f32[16,144]{1,0:T(8,128)S(1)}, f32[16,144]{1,0:T(8,128)S(1)}, u32[]{:S(2)}, u32[]{:S(2)}) collective-permute-start(f32[16,144]{1,0:T(8,128)S(1)} %pad_maximum_fusion), channel_id=1, source_target_pairs={{0,0},{1,8},{2,16},{3,24},{4,32},{5,40},{6,48},{7,56},{8,1},{9,9},... | collective-permute-start | bytes 27656 | tf_op jit(solution)/shard_map/ppermute | solution.py:341
  8.7 3.3 %collective-permute-done.1.aux_ref = f32[16,144]{1,0:T(8,128)S(1)} collective-permute-done((f32[16,144]{1,0:T(8,128)S(1)}, f32[16,144]{1,0:T(8,128)S(1)}, u32[]{:S(2)}, u32[]{:S(2)}) %collective-permute-start.1) | collective-permute-done | bytes 9248 | tf_op jit(solution)/shard_map/ppermute | solution.py:341
  12.0 0.0 collective-permute-done.tokens_ref
  12.0 1.9 shard_map.153
  13.8 28.1 %all-to-all-start = ((bf16[96,24,128]{2,1,0:T(8,128)(2,1)}), bf16[96,24,128]{2,1,0:T(8,128)(2,1)S(1)}, u32[]{:S(2)}, u32[]{:S(2)}) async-start(bf16[96,24,128]{2,1,0:T(8,128)(2,1)} %bitcast.2), calls=%async_computation | async-start | bytes 1179648 | tf_op jit(solution)/shard_map/all_to_all | solution.py:346
  41.9 0.0 copy-done.17
  41.9 4.9 %collective-permute-start.2 = (bf16[144,256]{1,0:T(8,128)(2,1)S(1)}, bf16[144,256]{1,0:T(8,128)(2,1)S(1)}, u32[]{:S(2)}, u32[]{:S(2)}) collective-permute-start(bf16[144,256]{1,0:T(8,128)(2,1)S(1)} %copy-done.17), channel_id=1, source_target_pairs={{0,0},{1,8},{2,16},{3,24},{4,32},{5,40},{6,48},{7,56},{8,1},{9,9},... | collective-permute-start | bytes 221192 | tf_op jit(solution)/shard_map/ppermute | solution.py:341
  46.9 4.2 %copy.17 = bf16[256,8,2,384]{3,1,2,0:T(8,128)(2,1)} copy(bf16[256,8,2,384]{3,2,1,0:T(2,128)(2,1)} %bitcast.38) | data formatting | bytes 6291456
  51.0 1.6 shard_map.154
  52.6 0.0 copy-start.6
  52.6 1.0 copy-done.6
  53.6 1.0 copy-done.7
  54.7 0.9 copy-done.9
  55.5 0.8 copy-done.10
  56.4 0.0 collective-permute-done.2.target_ref
  56.4 9.9 %all-to-all-done = bf16[96,24,128]{2,1,0:T(8,128)(2,1)S(1)} async-done(((bf16[96,24,128]{2,1,0:T(8,128)(2,1)}), bf16[96,24,128]{2,1,0:T(8,128)(2,1)S(1)}, u32[]{:S(2)}, u32[]{:S(2)}) %all-to-all-start) | async-done | bytes 589856 | tf_op jit(solution)/shard_map/all_to_all | solution.py:346
  66.3 0.9 copy-done
  67.2 5.9 %shard_map.155 = (bf16[2304,128]{1,0:T(8,128)(2,1)}, bf16[1296,128]{1,0:T(8,128)(2,1)}) custom-call(bf16[2304,128]{1,0:T(8,128)(2,1)} %bitcast.30, bf16[2048,768]{1,0:T(8,128)(2,1)} %bitcast.34, bf16[384,2048]{1,0:T(8,128)(2,1)} %bitcast.36), custom_call_target="tpu_custom_call" | custom-call | flops 1358954496 | bytes 4718592 | tf_op jit(solution)/shard_map/pallas_call | solution.py:374
  73.1 10.2 %all-to-all-start.1 = ((bf16[96,24,128]{2,1,0:T(8,128)(2,1)}), bf16[96,24,128]{2,1,0:T(8,128)(2,1)}, u32[]{:S(2)}, u32[]{:S(2)}) async-start(bf16[96,24,128]{2,1,0:T(8,128)(2,1)} %bitcast.43), calls=%async_computation.1 | async-start | bytes 1179648 | tf_op jit(solution)/shard_map/all_to_all | solution.py:346
  83.3 0.1 pad_add_fusion.place_ref
  83.4 1.1 copy-done.1
  84.5 1.0 copy-done.3
  85.5 1.6 shard_map.157
  87.1 2.4 %collective-permute-start.4 = (bf16[1872,128]{1,0:T(8,128)(2,1)}, bf16[1872,128]{1,0:T(8,128)(2,1)S(1)}, u32[]{:S(2)}, u32[]{:S(2)}) collective-permute-start(bf16[1872,128]{1,0:T(8,128)(2,1)} %get-tuple-element.55), channel_id=1, source_target_pairs={{0,2},{2,4},{4,6},{6,0},{1,3},{3,5},{5,7},{7,1},{8,10},{10,12},{12... | collective-permute-start | bytes 1437704 | tf_op jit(solution)/shard_map/ppermute | solution.py:390
  89.5 3.8 %collective-permute-start.5 = (bf16[1872,128]{1,0:T(8,128)(2,1)}, bf16[1872,128]{1,0:T(8,128)(2,1)S(1)}, u32[]{:S(2)}, u32[]{:S(2)}) collective-permute-start(bf16[1872,128]{1,0:T(8,128)(2,1)} %get-tuple-element.56), channel_id=1, source_target_pairs={{0,4},{2,6},{4,0},{6,2},{1,5},{3,7},{5,1},{7,3},{8,12},{10,14},{12... | collective-permute-start | bytes 1437704 | tf_op jit(solution)/shard_map/ppermute | solution.py:390
  93.4 2.4 %collective-permute-start.6 = (bf16[1872,128]{1,0:T(8,128)(2,1)S(1)}, bf16[1872,128]{1,0:T(8,128)(2,1)S(1)}, u32[]{:S(2)}, u32[]{:S(2)}) collective-permute-start(bf16[1872,128]{1,0:T(8,128)(2,1)S(1)} %get-tuple-element.57), channel_id=1, source_target_pairs={{0,6},{2,0},{4,2},{6,4},{1,7},{3,1},{5,3},{7,5},{8,14},{10,8},{12,... | collective-permute-start | bytes 1437704 | tf_op jit(solution)/shard_map/ppermute | solution.py:390
  95.8 11.7 %all-to-all-done.1 = bf16[96,24,128]{2,1,0:T(8,128)(2,1)} async-done(((bf16[96,24,128]{2,1,0:T(8,128)(2,1)}), bf16[96,24,128]{2,1,0:T(8,128)(2,1)}, u32[]{:S(2)}, u32[]{:S(2)}) %all-to-all-start.1) | async-done | bytes 589856 | tf_op jit(solution)/shard_map/all_to_all | solution.py:346
  107.5 5.4 %shard_map.156 = (bf16[144,256]{1,0:T(8,128)(2,1)}, bf16[2304,128]{1,0:T(8,128)(2,1)}) custom-call(bf16[2304,128]{1,0:T(8,128)(2,1)} %bitcast.6.back_ref, bf16[144,256]{1,0:T(8,128)(2,1)} %copy-done.16, bf16[2304,144]{1,0:T(8,128)(2,1)} %copy-done.6, bf16[2304,144]{1,0:T(8,128)(2,1)} %copy-done.7, bf16[144,2304]{1,0:T(8,128)(2,1)} %copy-done.9, ...), custom_call_target="tpu_custom_call" | custom-call | flops 1019215872 | bytes 2654208 | tf_op jit(solution)/shard_map/pallas_call | solution.py:394
  112.8 10.2 %all-to-all-start.2 = ((bf16[96,24,128]{2,1,0:T(8,128)(2,1)}), bf16[96,24,128]{2,1,0:T(8,128)(2,1)}, u32[]{:S(2)}, u32[]{:S(2)}) async-start(bf16[96,24,128]{2,1,0:T(8,128)(2,1)} %bitcast.42), calls=%async_computation.2 | async-start | bytes 1179648 | tf_op jit(solution)/shard_map/all_to_all | solution.py:346
  123.0 0.0 copy-start.18
  123.0 0.0 copy-start.13
  123.1 0.0 collective-permute-done.4.part1
  123.1 0.0 collective-permute-done.5.part2
  123.1 0.0 collective-permute-done.6.part3
  123.1 1.8 shard_map.158
  124.9 4.1 %collective-permute-start.7 = (bf16[6336,128]{1,0:T(8,128)(2,1)}, bf16[6336,128]{1,0:T(8,128)(2,1)}, u32[]{:S(2)}, u32[]{:S(2)}) collective-permute-start(bf16[6336,128]{1,0:T(8,128)(2,1)} %shard_map.158), channel_id=1, source_target_pairs={{0,1},{1,0},{2,3},{3,2},{4,5},{5,4},{6,7},{7,6},{8,9},{9,8},{10,11... | collective-permute-start | bytes 4866056 | tf_op jit(solution)/shard_map/ppermute | solution.py:407
  129.1 0.0 copy-done.18
  129.1 2.8 %collective-permute-start.3 = (bf16[144,256]{1,0:T(8,128)(2,1)S(1)}, bf16[144,256]{1,0:T(8,128)(2,1)S(1)}, u32[]{:S(2)}, u32[]{:S(2)}) collective-permute-start(bf16[144,256]{1,0:T(8,128)(2,1)S(1)} %copy-done.18), channel_id=1, source_target_pairs={{0,0},{1,8},{2,16},{3,24},{4,32},{5,40},{6,48},{7,56},{8,1},{9,9},... | collective-permute-start | bytes 221192 | tf_op jit(solution)/shard_map/ppermute | solution.py:341
  131.9 1.8 constant_dynamic-slice_fusion.w_in_ref
  133.7 0.0 copy-done.13
  133.7 0.8 copy.18
  134.5 0.8 copy.19
  135.3 0.0 collective-permute-done.7.far_ref
  135.3 2.6 %shard_map.159 = (bf16[256,1152]{1,0:T(8,128)(2,1)S(1)}, bf16[384,1152]{1,0:T(8,128)(2,1)S(1)}, bf16[1152,768]{1,0:T(8,128)(2,1)S(1)}) custom-call(s32[2]{0:T(128)S(1)} %pad_add_fusion.place_ref, bf16[2304,128]{1,0:T(8,128)(2,1)S(1)} %bitcast.33, bf16[1296,128]{1,0:T(8,128)(2,1)S(1)} %copy-done.4, bf16[1872,128]{1,0:T(8,128)(2,1)S(1)} %collective-permute-done.4.part1, ...), custom_call_target="tpu_custom_call" | custom-call | flops 339738624 | bytes 3538944 | tf_op jit(solution)/shard_map/pallas_call | solution.py:408
  137.9 1.2 copy-done.5
  139.1 0.9 copy-done.8
  140.0 0.8 copy-done.11
  140.8 0.0 collective-permute-done.3
  140.8 6.3 %all-to-all-done.2 = bf16[96,24,128]{2,1,0:T(8,128)(2,1)} async-done(((bf16[96,24,128]{2,1,0:T(8,128)(2,1)}), bf16[96,24,128]{2,1,0:T(8,128)(2,1)}, u32[]{:S(2)}, u32[]{:S(2)}) %all-to-all-start.2) | async-done | bytes 589856 | tf_op jit(solution)/shard_map/all_to_all | solution.py:346
  147.1 8.2 %all-to-all-start.3 = ((bf16[8,288,128]{2,1,0:T(8,128)(2,1)}), bf16[8,288,128]{2,1,0:T(8,128)(2,1)S(1)}, u32[]{:S(2)}, u32[]{:S(2)}) async-start(bf16[8,288,128]{2,1,0:T(8,128)(2,1)} %bitcast.11), calls=%async_computation.3 | async-start | bytes 1179648 | tf_op jit(solution)/shard_map/all_to_all | solution.py:421
  155.3 1.6 dynamic-slice_bitcast_fusion.w_out_ref
  156.9 3.3 %shard_map.160 = bf16[144,384]{1,0:T(8,128)(2,1)} custom-call(bf16[2304,128]{1,0:T(8,128)(2,1)} %bitcast.8.rows_ref, bf16[384,2048]{1,0:T(8,128)(2,1)} %bitcast.37), custom_call_target="tpu_custom_call" | custom-call | flops 452984832 | bytes 1572864 | tf_op jit(solution)/shard_map/pallas_call | solution.py:424
  160.2 15.7 %all_gather.3.hidden_grad_ref = bf16[1152,384]{1,0:T(8,128)(2,1)} all-gather(bf16[144,384]{1,0:T(8,128)(2,1)} %shard_map.160), channel_id=1, replica_groups=mesh['z'=12,'y'=8,'x'=4,'core'=2] {'x','core'}, dimensions={0}, use_global_device_ids=true | all-gather | bytes 995328 | tf_op jit(solution)/shard_map/all_gather | solution.py:427
  176.0 0.0 all-to-all-done.3
  176.0 0.8 copy-done.12
  176.8 6.3 %shard_map.161 = (bf16[256,768]{1,0:T(8,128)(2,1)}, bf16[256,768]{1,0:T(8,128)(2,1)}, bf16[256,768]{1,0:T(8,128)(2,1)}, bf16[384,256]{1,0:T(8,128)(2,1)}, bf16[3...) custom-call(bf16[2304,128]{1,0:T(8,128)(2,1)} %bitcast.39, bf16[1152,384]{1,0:T(8,128)(2,1)} %all_gather.3.hidden_grad_ref, ...), custom_call_target="tpu_custom_call" | custom-call | flops 679477248 | bytes 1572864 | tf_op jit(solution)/shard_map/pallas_call | solution.py:434
  183.1 1.9 %reshape.89 = bf16[1,256,2,384]{3,2,1,0:T(2,128)(2,1)} reshape(bf16[256,768]{1,0:T(8,128)(2,1)} %get-tuple-element.69) | data formatting | bytes 786432 | tf_op jit(solution)/shard_map/reshape | solution.py:454
  184.9 1.8 reshape.90
  186.8 0.8 reshape.91
  187.6 0.6 copy.21
  (20 shorter events, 0.0 us)
Async XLA Ops:
  0.6 41.3 %copy-start.17 = (bf16[144,256]{1,0:T(8,128)(2,1)S(1)}, bf16[144,256]{1,0:T(8,128)(2,1)}, u32[]{:S(2)}) copy-start(bf16[144,256]{1,0:T(8,128)(2,1)} %param.11) | copy-start | bytes 221188
  0.6 11.3 %collective-permute-start = (bf16[144,256]{1,0:T(8,128)(2,1)}, bf16[144,256]{1,0:T(8,128)(2,1)S(1)}, u32[]{:S(2)}, u32[]{:S(2)}) collective-permute-start(bf16[144,256]{1,0:T(8,128)(2,1)} %param.10), channel_id=1, source_target_pairs={{0,0},{1,8},{2,16},{3,24},{4,32},{5,40},{6,48},{7,56},{8,1},{9,9},... | collective-permute-start | bytes 221192 | tf_op jit(solution)/shard_map/ppermute | solution.py:341
  6.8 5.2 %collective-permute-start.1 = (f32[16,144]{1,0:T(8,128)S(1)}, f32[16,144]{1,0:T(8,128)S(1)}, u32[]{:S(2)}, u32[]{:S(2)}) collective-permute-start(f32[16,144]{1,0:T(8,128)S(1)} %pad_maximum_fusion), channel_id=1, source_target_pairs={{0,0},{1,8},{2,16},{3,24},{4,32},{5,40},{6,48},{7,56},{8,1},{9,9},... | collective-permute-start | bytes 27656 | tf_op jit(solution)/shard_map/ppermute | solution.py:341
  13.8 52.5 %all-to-all-start = ((bf16[96,24,128]{2,1,0:T(8,128)(2,1)}), bf16[96,24,128]{2,1,0:T(8,128)(2,1)S(1)}, u32[]{:S(2)}, u32[]{:S(2)}) async-start(bf16[96,24,128]{2,1,0:T(8,128)(2,1)} %bitcast.2), calls=%async_computation | async-start | bytes 1179648 | tf_op jit(solution)/shard_map/all_to_all | solution.py:346
  41.9 14.4 %collective-permute-start.2 = (bf16[144,256]{1,0:T(8,128)(2,1)S(1)}, bf16[144,256]{1,0:T(8,128)(2,1)S(1)}, u32[]{:S(2)}, u32[]{:S(2)}) collective-permute-start(bf16[144,256]{1,0:T(8,128)(2,1)S(1)} %copy-done.17), channel_id=1, source_target_pairs={{0,0},{1,8},{2,16},{3,24},{4,32},{5,40},{6,48},{7,56},{8,1},{9,9},... | collective-permute-start | bytes 221192 | tf_op jit(solution)/shard_map/ppermute | solution.py:341
  52.6 1.0 copy-start.6
  53.6 1.0 copy-start.7
  54.7 0.9 copy-start.9
  55.5 0.8 copy-start.10
  56.4 51.1 %copy-start.16 = (bf16[144,256]{1,0:T(8,128)(2,1)}, bf16[144,256]{1,0:T(8,128)(2,1)S(1)}, u32[]{:S(2)}) copy-start(bf16[144,256]{1,0:T(8,128)(2,1)S(1)} %collective-permute-done.2.target_ref) | copy-start | bytes 221188
  66.3 0.9 copy-start
  73.1 34.3 %all-to-all-start.1 = ((bf16[96,24,128]{2,1,0:T(8,128)(2,1)}), bf16[96,24,128]{2,1,0:T(8,128)(2,1)}, u32[]{:S(2)}, u32[]{:S(2)}) async-start(bf16[96,24,128]{2,1,0:T(8,128)(2,1)} %bitcast.43), calls=%async_computation.1 | async-start | bytes 1179648 | tf_op jit(solution)/shard_map/all_to_all | solution.py:346
  83.4 1.1 copy-start.1
  84.5 1.0 copy-start.3
  87.1 36.0 %collective-permute-start.4 = (bf16[1872,128]{1,0:T(8,128)(2,1)}, bf16[1872,128]{1,0:T(8,128)(2,1)S(1)}, u32[]{:S(2)}, u32[]{:S(2)}) collective-permute-start(bf16[1872,128]{1,0:T(8,128)(2,1)} %get-tuple-element.55), channel_id=1, source_target_pairs={{0,2},{2,4},{4,6},{6,0},{1,3},{3,5},{5,7},{7,1},{8,10},{10,12},{12... | collective-permute-start | bytes 1437704 | tf_op jit(solution)/shard_map/ppermute | solution.py:390
  89.5 33.5 %collective-permute-start.5 = (bf16[1872,128]{1,0:T(8,128)(2,1)}, bf16[1872,128]{1,0:T(8,128)(2,1)S(1)}, u32[]{:S(2)}, u32[]{:S(2)}) collective-permute-start(bf16[1872,128]{1,0:T(8,128)(2,1)} %get-tuple-element.56), channel_id=1, source_target_pairs={{0,4},{2,6},{4,0},{6,2},{1,5},{3,7},{5,1},{7,3},{8,12},{10,14},{12... | collective-permute-start | bytes 1437704 | tf_op jit(solution)/shard_map/ppermute | solution.py:390
  93.4 29.7 %collective-permute-start.6 = (bf16[1872,128]{1,0:T(8,128)(2,1)S(1)}, bf16[1872,128]{1,0:T(8,128)(2,1)S(1)}, u32[]{:S(2)}, u32[]{:S(2)}) collective-permute-start(bf16[1872,128]{1,0:T(8,128)(2,1)S(1)} %get-tuple-element.57), channel_id=1, source_target_pairs={{0,6},{2,0},{4,2},{6,4},{1,7},{3,1},{5,3},{7,5},{8,14},{10,8},{12,... | collective-permute-start | bytes 1437704 | tf_op jit(solution)/shard_map/ppermute | solution.py:390
  107.5 15.6 %copy-start.2 = (bf16[96,24,128]{2,1,0:T(8,128)(2,1)S(1)}, bf16[96,24,128]{2,1,0:T(8,128)(2,1)}, u32[]{:S(2)}) copy-start(bf16[96,24,128]{2,1,0:T(8,128)(2,1)} %copy-done) | copy-start | bytes 1769476
  107.5 15.6 %copy-start.4 = (bf16[1296,128]{1,0:T(8,128)(2,1)S(1)}, bf16[1296,128]{1,0:T(8,128)(2,1)}, u32[]{:S(2)}) copy-start(bf16[1296,128]{1,0:T(8,128)(2,1)} %get-tuple-element.54.factors_ref.near_factors_ref) | copy-start | bytes 995332
  112.8 34.3 %all-to-all-start.2 = ((bf16[96,24,128]{2,1,0:T(8,128)(2,1)}), bf16[96,24,128]{2,1,0:T(8,128)(2,1)}, u32[]{:S(2)}, u32[]{:S(2)}) async-start(bf16[96,24,128]{2,1,0:T(8,128)(2,1)} %bitcast.42), calls=%async_computation.2 | async-start | bytes 1179648 | tf_op jit(solution)/shard_map/all_to_all | solution.py:346
  123.0 6.0 %copy-start.18 = (bf16[144,256]{1,0:T(8,128)(2,1)S(1)}, bf16[144,256]{1,0:T(8,128)(2,1)}, u32[]{:S(2)}) copy-start(bf16[144,256]{1,0:T(8,128)(2,1)} %get-tuple-element.53) | copy-start | bytes 221188
  123.0 10.6 %copy-start.13 = (bf16[1,256,2,384]{3,2,1,0:T(2,128)(2,1)S(1)}, bf16[1,256,2,384]{3,2,1,0:T(2,128)(2,1)}, u32[]{:S(2)}) copy-start(bf16[1,256,2,384]{3,2,1,0:T(2,128)(2,1)} %param.15) | copy-start | bytes 1179652
  124.9 9.5 %copy-start.14 = (bf16[1,256,2,384]{3,2,1,0:T(2,128)(2,1)S(1)}, bf16[1,256,2,384]{3,2,1,0:T(2,128)(2,1)}, u32[]{:S(2)}) copy-start(bf16[1,256,2,384]{3,2,1,0:T(2,128)(2,1)} %param.16) | copy-start | bytes 1179652
  124.9 10.3 %collective-permute-start.7 = (bf16[6336,128]{1,0:T(8,128)(2,1)}, bf16[6336,128]{1,0:T(8,128)(2,1)}, u32[]{:S(2)}, u32[]{:S(2)}) collective-permute-start(bf16[6336,128]{1,0:T(8,128)(2,1)} %shard_map.158), channel_id=1, source_target_pairs={{0,1},{1,0},{2,3},{3,2},{4,5},{5,4},{6,7},{7,6},{8,9},{9,8},{10,11... | collective-permute-start | bytes 4866056 | tf_op jit(solution)/shard_map/ppermute | solution.py:407
  129.1 11.8 %collective-permute-start.3 = (bf16[144,256]{1,0:T(8,128)(2,1)S(1)}, bf16[144,256]{1,0:T(8,128)(2,1)S(1)}, u32[]{:S(2)}, u32[]{:S(2)}) collective-permute-start(bf16[144,256]{1,0:T(8,128)(2,1)S(1)} %copy-done.18), channel_id=1, source_target_pairs={{0,0},{1,8},{2,16},{3,24},{4,32},{5,40},{6,48},{7,56},{8,1},{9,9},... | collective-permute-start | bytes 221192 | tf_op jit(solution)/shard_map/ppermute | solution.py:341
  137.9 1.2 copy-start.5
  139.1 0.9 copy-start.8
  140.0 0.8 copy-start.11
  147.1 28.8 %all-to-all-start.3 = ((bf16[8,288,128]{2,1,0:T(8,128)(2,1)}), bf16[8,288,128]{2,1,0:T(8,128)(2,1)S(1)}, u32[]{:S(2)}, u32[]{:S(2)}) async-start(bf16[8,288,128]{2,1,0:T(8,128)(2,1)} %bitcast.11), calls=%async_computation.3 | async-start | bytes 1179648 | tf_op jit(solution)/shard_map/all_to_all | solution.py:421
  176.0 0.8 copy-start.12
  183.1 3.7 %copy-start.15 = (bf16[256,768]{1,0:T(8,128)(2,1)S(1)}, bf16[256,768]{1,0:T(8,128)(2,1)}, u32[]{:S(2)}) copy-start(bf16[256,768]{1,0:T(8,128)(2,1)} %get-tuple-element.71) | copy-start | bytes 1179652

commit v3 on v2

--- a/solution.py
+++ b/solution.py
@@ -28,6 +28,7 @@
 FACTORS = 3 * LANES * CHUNK
 PART = 2 * GROUP + FACTORS
 FAR = GROUP + FACTORS
+LOADS = 4
 
 beta_one = 0.9
 beta_two = 0.95
@@ -54,15 +55,15 @@
     return high, (value - high.astype(F32)).astype(BF16)
 
 
-def choices(aux):
+def choices(ids, gates):
     expert = iota((EXPERTS, TOK), 0)
-    ids = aux[:TOPK].astype(jnp.int32)
+    ids = ids.astype(jnp.int32)
     named = jnp.zeros((EXPERTS, TOK), F32)
     gate = jnp.zeros((EXPERTS, TOK), F32)
     for k in range(TOPK):
         hit = ids[k : k + 1] == expert
         named = jnp.where(hit, 1.0, named)
-        gate = jnp.where(hit, aux[TOPK + k : TOPK + k + 1], gate)
+        gate = jnp.where(hit, gates[k : k + 1], gate)
     earlier, later = iota((TOK, TOK), 0), iota((TOK, TOK), 1)
     same = earlier <= later
     for edge in range(BLOCK, TOK, BLOCK):
@@ -104,15 +105,31 @@
     return jnp.where(half.reshape(rows, HALF) == 0, values[:, :HALF], values[:, HALF:])
 
 
-def dispatch_kernel(tokens_ref, aux_ref, send_ref):
-    rank, _ = choices(aux_ref[...])
+def pack_kernel(tokens_ref, ids_ref, gates_ref, packed_ref):
+    packed_ref[:TOK, :] = tokens_ref[...]
+    gate = gates_ref[...]
+    high = gate.astype(BF16).astype(F32)
+    mid = (gate - high).astype(BF16).astype(F32)
+    aux = jnp.concatenate([ids_ref[...].astype(F32), high, mid, gate - high - mid], axis=0)
+    packed_ref[TOK:, :] = jnp.zeros((4 * TOPK, SLICE), BF16)
+    packed_ref[TOK:, :TOK] = aux.astype(BF16)
+
+
+def aux_of(packed_ref):
+    aux = packed_ref[TOK:, :TOK].astype(F32)
+    gates = aux[TOPK : 2 * TOPK] + aux[2 * TOPK : 3 * TOPK] + aux[3 * TOPK :]
+    return aux[:TOPK], gates
+
+
+def dispatch_kernel(packed_ref, send_ref):
+    rank, _ = choices(*aux_of(packed_ref))
     ranks = dot(row_expert_map(), rank.astype(BF16))
     pick = slot_hits(ranks).astype(F32).reshape(ROWS, TOK).astype(BF16)
-    send_ref[...] = pick_half(dot(pick, tokens_ref[...])).astype(BF16)
-
-
-def weights_kernel(aux_ref, high_ref, low_ref, high_t_ref, low_t_ref):
-    rank, gate = choices(aux_ref[...])
+    send_ref[...] = pick_half(dot(pick, packed_ref[:TOK, :])).astype(BF16)
+
+
+def weights_kernel(packed_ref, high_t_ref, low_t_ref, high_ref, low_ref):
+    rank, gate = choices(*aux_of(packed_ref))
     spread = row_expert_map()
     gate_high, gate_low = split_pair(gate)
     hits = slot_hits(dot(spread, rank.astype(BF16)))
@@ -152,34 +169,79 @@
     return hit.astype(F32).astype(BF16)
 
 
-def forward_kernel(rows_ref, w_in_ref, w_out_ref, out_ref, factors_ref, wide_ref):
-    widen_rows(rows_ref, wide_ref)
-    preacts = add_halves(dot(wide_ref[...], w_in_ref[...]))
+def fetch(pairs, sems):
+    copies = [pltpu.make_async_copy(source, target, sems.at[i]) for i, (source, target) in enumerate(pairs)]
+    for copy in copies:
+        copy.start()
+    return copies
+
+
+def fetch(pairs, sems):
+    copies = [pltpu.make_async_copy(source, target, sems.at[i]) for i, (source, target) in enumerate(pairs)]
+    for copy in copies:
+        copy.start()
+    return copies
+
+
+def forward_kernel(
+    rows_ref, w_in_hbm, w_out_hbm, out_hbm, factors_ref, w_in_ref, w_out_ref, out_ref, sems
+):
+    deep = WIDTH // LOADS
+    copies = fetch(
+        [(w_in_hbm.at[pl.ds(i * deep, deep), :], w_in_ref.at[pl.ds(i * deep, deep), :]) for i in range(LOADS)]
+        + [(w_out_hbm, w_out_ref)],
+        sems,
+    )
+    first, second = half_masks()
+    compact = compact_map(False)
+    total = jnp.zeros((GROUP, 2 * FF), F32)
+    for i in range(LOADS):
+        parts = []
+        for y in range(i * NY // LOADS, (i + 1) * NY // LOADS):
+            part = rows_ref[pl.ds(y * GROUP, GROUP), :]
+            parts += [part * first, part * second]
+        copies[i].wait()
+        total = total + dot(jnp.concatenate(parts, axis=1), w_in_ref[pl.ds(i * deep, deep), :])
+    preacts = add_halves(total)
     gate_pre = preacts[:, :FF]
     up_pre = preacts[:, FF:]
     sigmoid = jax.nn.sigmoid(gate_pre)
     silu = gate_pre * sigmoid
     hidden = (silu * up_pre).astype(BF16)
+    copies[LOADS].wait()
+    sends = []
+    for y in range(NY):
+        rows = pl.ds(y * GROUP, GROUP)
+        part = dot(hidden, w_out_ref[:, pl.ds(y * SLICE, SLICE)])
+        out_ref[rows, :] = pick_half(part).astype(BF16)
+        send = pltpu.make_async_copy(out_ref.at[rows, :], out_hbm.at[rows, :], sems.at[LOADS + 1 + y])
+        send.start()
+        sends.append(send)
     slope = up_pre * sigmoid * (1.0 + gate_pre * (1.0 - sigmoid))
-    compact = compact_map(False)
     for i, factor in enumerate((hidden, slope.astype(BF16), silu.astype(BF16))):
         values = dot(compact, factor).astype(BF16)
-        for j in range(FF // HALF):
-            place = (i * (FF // HALF) + j) * CHUNK
+        for j in range(LANES):
+            place = (i * LANES + j) * CHUNK
             factors_ref[pl.ds(place, CHUNK), :] = values[:, j * HALF : (j + 1) * HALF]
-    for y in range(NY):
-        part = dot(hidden, w_out_ref[:, pl.ds(y * SLICE, SLICE)])
-        out_ref[pl.ds(y * GROUP, GROUP), :] = pick_half(part).astype(BF16)
-
-
-def combine_kernel(back_ref, target_ref, high_ref, low_ref, high_t_ref, low_t_ref, mixed_ref, send_ref):
+    for send in sends:
+        send.wait()
+
+
+def combine_kernel(back_ref, target_ref, *refs):
+    sources, (mixed_ref, send_ref), held, sems = refs[:4], refs[4:6], refs[6:10], refs[10]
+    copies = fetch(zip(sources, held), sems)
+    high_t_ref, low_t_ref, high_ref, low_ref = held
     half, _ = row_slot((EXPERTS, MSG, HALF))
     second = half.reshape(ROWS, HALF).astype(F32)
     rows = back_ref[...]
     wide = jnp.concatenate([rows * (1.0 - second).astype(BF16), rows * second.astype(BF16)], axis=1)
+    for copy in copies[:2]:
+        copy.wait()
     mixed = (dot(high_t_ref[...], wide) + dot(low_t_ref[...], wide)).astype(BF16)
     mixed_ref[...] = mixed
     grad_high, grad_low = split_pair(mixed.astype(F32) - target_ref[...].astype(F32))
+    for copy in copies[2:]:
+        copy.wait()
     spread = dot(high_ref[...], grad_high) + dot(high_ref[...], grad_low) + dot(low_ref[...], grad_high)
     send_ref[...] = pick_half(spread).astype(BF16)
 
@@ -277,34 +339,23 @@
     )
 
 
-def update_kernel(
-    grads_ref,
-    hidden_grad_ref,
-    slopes_ref,
-    rows_t_ref,
-    hidden_t_ref,
-    w_in_ref,
-    m_in_ref,
-    v_in_ref,
-    w_out_ref,
-    m_out_ref,
-    v_out_ref,
-    new_w_in_ref,
-    new_m_in_ref,
-    new_v_in_ref,
-    new_w_out_ref,
-    new_m_out_ref,
-    new_v_out_ref,
-    own_ref,
-):
+def update_kernel(grads_ref, hidden_grad_ref, *refs):
+    sources, new_refs, held, own_ref, sems = refs[:9], refs[9:15], refs[15:24], refs[24], refs[25]
+    copies = fetch(zip(sources, held), sems)
+    hidden_t_ref, w_out_ref, m_out_ref, v_out_ref, slopes_ref, rows_t_ref, w_in_ref, m_in_ref, v_in_ref = held
+    new_w_in_ref, new_m_in_ref, new_v_in_ref, new_w_out_ref, new_m_out_ref, new_v_out_ref = new_refs
     masks = (compact_map(True), *half_masks())
     for source in range(NE):
         part = grads_ref[pl.ds(source * GROUP, GROUP), :]
         own_ref[pl.ds(source * CHUNK, CHUNK), :] = narrow(part, *masks).astype(BF16)
+    for copy in copies[:4]:
+        copy.wait()
     grad_down = dot(hidden_t_ref[...], own_ref[...])
     new_w_out_ref[...], new_m_out_ref[...], new_v_out_ref[...] = adamw(
         w_out_ref[...], m_out_ref[...], v_out_ref[...], grad_down
     )
+    for copy in copies[4:]:
+        copy.wait()
     hidden_grad = hidden_grad_ref[...].astype(F32)
     for i in range(2):
         columns = pl.ds(i * FF, FF)
@@ -319,8 +370,21 @@
     return jax.ShapeDtypeStruct(dims, dtype)
 
 
-def call(kernel, out_shape, flops, size, megabytes, scratch=(), in_specs=None):
+def in_hbm(*dims):
+    return pltpu.HBM(dims, BF16)
+
+
+def pin(value):
+    return pltpu.with_memory_space_constraint(value, pltpu.HBM)
+
+
+def call(kernel, out_shape, flops, size, megabytes, scratch=(), in_specs=None, out_specs=None):
     specs = {} if in_specs is None else {"in_specs": in_specs}
+    if out_specs is not None:
+        specs["out_specs"] = out_specs
+    else:
+        whole = pl.BlockSpec(memory_space=pltpu.VMEM)
+        specs["out_specs"] = [whole] * len(out_shape) if isinstance(out_shape, list) else whole
     return pl.pallas_call(
         kernel,
         out_shape=out_shape,
@@ -353,34 +417,41 @@
     w_gate_up = w_in.reshape(WIDTH, 2 * FF)
     w_down = w_out.reshape(FF, WIDTH)
 
-    tokens_here = change_places(tokens)
-    aux = change_places(jnp.concatenate([expert_ids.T.astype(F32), gate_weights.T], axis=0))
+    packed = call(pack_kernel, shape_of(TOK + 4 * TOPK, SLICE), 0, 4 * TOK * SLICE, 4)(
+        pin(tokens), pin(expert_ids.T), pin(gate_weights.T)
+    )
+    packed = change_places(packed)
     one_hot_flops = 2 * ROWS * TOK * SLICE
-    send_rows = call(dispatch_kernel, shape_of(ROWS, HALF), 3 * one_hot_flops, 2 * ROWS * HALF, 16)(
-        tokens_here, aux
-    )
+    send_rows = call(dispatch_kernel, shape_of(ROWS, HALF), 3 * one_hot_flops, 2 * ROWS * HALF, 16)(packed)
     arrived = over_experts(send_rows)
     target_here = change_places(target)
+    wide = [pltpu.VMEM((GROUP, WIDTH), BF16)]
+    vmem, hbm = pl.BlockSpec(memory_space=pltpu.VMEM), pl.BlockSpec(memory_space=pltpu.HBM)
+    arrived, target_here = lax.optimization_barrier((arrived, target_here))
+    out_rows, factors = call(
+        forward_kernel,
+        [in_hbm(ROWS, HALF), in_hbm(FACTORS, HALF)],
+        6 * GROUP * WIDTH * FF,
+        6 * WIDTH * FF,
+        24,
+        [
+            pltpu.VMEM((WIDTH, 2 * FF), BF16),
+            pltpu.VMEM((FF, WIDTH), BF16),
+            pltpu.VMEM((ROWS, HALF), BF16),
+            pltpu.SemaphoreType.DMA((LOADS + 1 + NY,)),
+        ],
+        [vmem, hbm, hbm],
+        [hbm, vmem],
+    )(arrived, pin(w_gate_up), pin(w_down))
+    out_rows, packed = lax.optimization_barrier((out_rows, packed))
     weights = call(
         weights_kernel,
-        [shape_of(ROWS, TOK), shape_of(ROWS, TOK), shape_of(TOK, ROWS), shape_of(TOK, ROWS)],
+        [in_hbm(TOK, ROWS)] * 2 + [in_hbm(ROWS, TOK)] * 2,
         4 * one_hot_flops,
         8 * ROWS * TOK,
         16,
-    )(aux)
-    arrived, target_here, *weights = lax.optimization_barrier((arrived, target_here, *weights))
-
-    wide = [pltpu.VMEM((GROUP, WIDTH), BF16)]
-    out_rows, factors = call(
-        forward_kernel,
-        [shape_of(ROWS, HALF), shape_of(FACTORS, HALF)],
-        6 * GROUP * WIDTH * FF,
-        6 * WIDTH * FF,
-        61,
-        wide,
-    )(arrived, w_gate_up, w_down)
+    )(packed)
     returned = over_experts(out_rows)
-    vmem = pl.BlockSpec(memory_space=pltpu.VMEM)
     placed = [pl.BlockSpec(memory_space=pltpu.SMEM)]
     place = jnp.stack([x, core]).astype(jnp.int32)
     parts = call(
@@ -393,11 +464,13 @@
 
     mixed_here, slot_grad = call(
         combine_kernel,
-        [shape_of(TOK, SLICE), shape_of(ROWS, HALF)],
+        [shape_of(TOK, SLICE), in_hbm(ROWS, HALF)],
         6 * one_hot_flops,
         8 * ROWS * TOK,
-        61,
-    )(returned, target_here, *weights)
+        24,
+        [pltpu.VMEM(value.shape, BF16) for value in weights] + [pltpu.SemaphoreType.DMA((4,))],
+        [vmem] * 2 + [hbm] * 4,
+    )(returned, target_here, *map(pin, weights))
     grads = over_experts(slot_grad)
     mixed = change_places(mixed_here)
     slot_grad, *parts = lax.optimization_barrier((slot_grad, *parts))
@@ -407,50 +480,45 @@
     far = lax.ppermute(far, "core", [(0, 1), (1, 0)])
     rows_t, hidden_t, slopes = call(
         prepare_kernel,
-        [shape_of(SLICE, EXPERT_ROWS), shape_of(FF, EXPERT_ROWS), shape_of(EXPERT_ROWS, 2 * FF)],
+        [in_hbm(SLICE, EXPERT_ROWS), in_hbm(FF, EXPERT_ROWS), in_hbm(EXPERT_ROWS, 2 * FF)],
         2 * one_hot_flops,
         8 * EXPERT_ROWS * FF,
         20,
         [pltpu.VMEM((EXPERT_ROWS, SLICE), F32), pltpu.VMEM((EXPERT_ROWS, FF), F32)],
         placed + [vmem] * 6,
     )(place, arrived, factors, *parts, far)
-    grads, mixed, rows_t, hidden_t, slopes = lax.optimization_barrier(
-        (grads, mixed, rows_t, hidden_t, slopes)
+    flat_in, flat_out = (SLICE, 2 * FF), (FF, SLICE)
+    states = [
+        lax.dynamic_slice_in_dim(w_gate_up, column * SLICE, SLICE, 0),
+        m_in.reshape(flat_in),
+        v_in.reshape(flat_in),
+        lax.dynamic_slice_in_dim(w_down, column * SLICE, SLICE, 1),
+        m_out.reshape(flat_out),
+        v_out.reshape(flat_out),
+    ]
+    grads, _, rows_t, hidden_t, slopes, *states = lax.optimization_barrier(
+        (grads, mixed[:8, :HALF], rows_t, hidden_t, slopes, *states)
     )
 
     own_grads = lax.all_to_all(
         grads.reshape(NE, GROUP, HALF), ("x", "core"), split_axis=0, concat_axis=0, tiled=True
     ).reshape(ROWS, HALF)
     hidden_grad = call(
-        backward_kernel, shape_of(CHUNK, FF), 2 * GROUP * WIDTH * FF, 2 * WIDTH * FF, 62, wide
+        backward_kernel, shape_of(CHUNK, FF), 2 * GROUP * WIDTH * FF, 2 * WIDTH * FF, 24, wide
     )(grads, w_down)
     all_grads = lax.all_gather(hidden_grad, ("x", "core"), axis=0, tiled=True)
 
-    flat_in, flat_out = (SLICE, 2 * FF), (FF, SLICE)
-    new_in = [shape_of(*flat_in)] * 3
-    new_out = [shape_of(*flat_out)] * 3
-    w_in_own = lax.dynamic_slice_in_dim(w_gate_up, column * SLICE, SLICE, 0)
-    w_out_own = lax.dynamic_slice_in_dim(w_down, column * SLICE, SLICE, 1)
+    operands = [hidden_t, *states[3:], slopes, rows_t, *states[:3]]
     updated = call(
         update_kernel,
-        new_in + new_out,
+        [pltpu.VMEM(flat_in, BF16)] * 3 + [in_hbm(*flat_out)] * 3,
         6 * EXPERT_ROWS * SLICE * FF,
         16 * SLICE * FF,
-        61,
-        [pltpu.VMEM((EXPERT_ROWS, SLICE), BF16)],
-    )(
-        own_grads,
-        all_grads,
-        slopes,
-        rows_t,
-        hidden_t,
-        w_in_own,
-        m_in.reshape(flat_in),
-        v_in.reshape(flat_in),
-        w_out_own,
-        m_out.reshape(flat_out),
-        v_out.reshape(flat_out),
-    )
+        24,
+        [pltpu.VMEM(value.shape, BF16) for value in operands]
+        + [pltpu.VMEM((EXPERT_ROWS, SLICE), BF16), pltpu.SemaphoreType.DMA((len(operands),))],
+        [vmem] * 2 + [hbm] * len(operands),
+    )(own_grads, all_grads, *map(pin, operands))
     new_w_in, new_m_in, new_v_in = (value.reshape(m_in.shape) for value in updated[:3])
     new_w_out, new_m_out, new_v_out = (value.reshape(m_out.shape) for value in updated[3:])
     return (mixed, new_w_in, new_m_in, new_v_in, new_w_out, new_m_out, new_v_out)

time: 189 us -> 187 us (0.989)
  local copies, waits for them, and re-layouts: 24.8 us -> 16.2 us
  starting transfers between devices: 83.8 us -> 89.1 us
  blocking collectives: 15.7 us -> 20.7 us
  waiting for transfers between devices: 31.2 us -> 28.4 us
    unnamed x42 -> x16, local copies, waits for them, and re-layouts: 16.9 us -> 11.2 us
    all_gather x1, blocking collectives: 15.7 us -> 20.7 us  [shards(): all_grads = lax.all_gather(hidden_grad, ('x', 'core'), axis=0, tiled=True)]
    all_to_all x3, waiting for transfers between devices: 27.9 us -> 23.2 us  [over_experts(): lax.all_to_all(messages, ('y', 'z'), split_axis=0, concat_axis=0, tiled=T...]
    all_to_all x1, starting transfers between devices: 8.16 us -> 11 us  [shards(): lax.all_to_all(grads.reshape(NE, GROUP, HALF), ('x', 'core'), split_axis=...]
    ppermute x3, starting transfers between devices: 8.66 us -> 11.2 us  [shards(): lax.ppermute(part, 'x', [(i, (i + shift) % CHIPS) for i in range(CHIPS)])]
    reshape x3, local copies, waits for them, and re-layouts: 4.55 us -> 2.51 us  [shards(): value.reshape(m_in.shape)]
    ppermute x4 -> x3, waiting for transfers between devices: 3.27 us -> 5.16 us  [change_places(): return lax.ppermute(value, ('z', 'y', 'x', 'core'), pairs)]
    pallas_call x5 -> x6, Pallas kernels: 21.7 us -> 22.7 us  [the longest x1 5.43 us: shards(): call(forward_kernel, [in_hbm(ROWS, HALF), in_hbm(FACTORS, HALF)], 6 * GRO...]
  transfers between devices with their start and end apart: 12 -> 11, of which waited for: 4 -> 6; matrix products, arithmetic and copies ran while one was open for 6% -> 6% of each run, Pallas kernels for 9% -> 10%
where the time goes in v3:
time: 187 us; the launch traced here: 186 us
  starting transfers between devices  89.1 us (48%)
  Pallas kernels  30.4 us (16%)
  waiting for transfers between devices  28.4 us (15%)
  blocking collectives  20.7 us (11%)
  local copies, waits for them, and re-layouts  16.2 us (9%)
    all_to_all x3, starting transfers between devices, over_experts(): lax.all_to_all(messages, ('y', 'z'), split_axis=0, concat_axis=0, tiled=T...  48.5 us
    all_to_all x3, waiting for transfers between devices, over_experts(): lax.all_to_all(messages, ('y', 'z'), split_axis=0, concat_axis=0, tiled=T...  23.2 us
    all_gather x1, blocking collectives, shards(): all_grads = lax.all_gather(hidden_grad, ('x', 'core'), axis=0, tiled=True)  20.7 us
    ppermute x3, starting transfers between devices, change_places(): return lax.ppermute(value, ('z', 'y', 'x', 'core'), pairs)  13.8 us
    unnamed x16, local copies, waits for them, and re-layouts  11.2 us
    ppermute x3, starting transfers between devices, shards(): lax.ppermute(part, 'x', [(i, (i + shift) % CHIPS) for i in range(CHIPS)])  11.2 us
    all_to_all x1, starting transfers between devices, shards(): lax.all_to_all(grads.reshape(NE, GROUP, HALF), ('x', 'core'), split_axis=...  11 us
    pallas_call x1, Pallas kernels, shards(): call(forward_kernel, [in_hbm(ROWS, HALF), in_hbm(FACTORS, HALF)], 6 * GRO...  5.43 us
  transfers between devices with their start and end apart: 11, of which 6 were waited for; matrix products, arithmetic and copies ran while one was open for 6% of the time, Pallas kernels for 10%

profile of v3, /device:TPU:1, one launch (start us, length us, event | category | flops | bytes accessed | tf_op | source)
XLA Modules:
  0.0 185.7 jit_solution(8673741281439568136)
XLA Ops:
  0.6 0.0 copy-start.5
  0.6 0.9 shard_map.153
  1.6 4.6 %collective-permute-start = (bf16[176,256]{1,0:T(8,128)(2,1)S(1)}, bf16[176,256]{1,0:T(8,128)(2,1)S(1)}, u32[]{:S(2)}, u32[]{:S(2)}) collective-permute-start(bf16[176,256]{1,0:T(8,128)(2,1)S(1)} %shard_map.153), channel_id=1, source_target_pairs={{0,0},{1,8},{2,16},{3,24},{4,32},{5,40},{6,48},{7,56},{8,1},{9,9},... | collective-permute-start | bytes 270344 | tf_op jit(solution)/shard_map/ppermute | solution.py:405
  6.2 2.2 %collective-permute-done.packed_ref = bf16[176,256]{1,0:T(8,128)(2,1)S(1)} collective-permute-done((bf16[176,256]{1,0:T(8,128)(2,1)S(1)}, bf16[176,256]{1,0:T(8,128)(2,1)S(1)}, u32[]{:S(2)}, u32[]{:S(2)}) %collective-permute-start) | collective-permute-done | bytes 90144 | tf_op jit(solution)/shard_map/ppermute | solution.py:405
  8.4 1.9 %shard_map.154 = bf16[2304,128]{1,0:T(8,128)(2,1)} custom-call(bf16[176,256]{1,0:T(8,128)(2,1)S(1)} %collective-permute-done.packed_ref), custom_call_target="tpu_custom_call" | custom-call | flops 509607936 | bytes 589824 | tf_op jit(solution)/shard_map/pallas_call | solution.py:425
  10.3 27.2 %all-to-all-start = ((bf16[96,24,128]{2,1,0:T(8,128)(2,1)}), bf16[96,24,128]{2,1,0:T(8,128)(2,1)S(1)}, u32[]{:S(2)}, u32[]{:S(2)}) async-start(bf16[96,24,128]{2,1,0:T(8,128)(2,1)} %bitcast.2), calls=%async_computation | async-start | bytes 1179648 | tf_op jit(solution)/shard_map/all_to_all | solution.py:410
  37.5 0.0 copy-done.5
  37.5 5.4 %collective-permute-start.1 = (bf16[144,256]{1,0:T(8,128)(2,1)S(1)}, bf16[144,256]{1,0:T(8,128)(2,1)S(1)}, u32[]{:S(2)}, u32[]{:S(2)}) collective-permute-start(bf16[144,256]{1,0:T(8,128)(2,1)S(1)} %copy-done.5), channel_id=1, source_target_pairs={{0,0},{1,8},{2,16},{3,24},{4,32},{5,40},{6,48},{7,56},{8,1},{9,9},... | collective-permute-start | bytes 221192 | tf_op jit(solution)/shard_map/ppermute | solution.py:405
  42.9 4.2 %copy.17 = bf16[256,8,2,384]{3,1,2,0:T(8,128)(2,1)} copy(bf16[256,8,2,384]{3,2,1,0:T(2,128)(2,1)} %bitcast.39) | data formatting | bytes 6291456
  47.1 0.6 collective-permute-done.1.target_ref
  47.7 13.0 %all-to-all-done = bf16[96,24,128]{2,1,0:T(8,128)(2,1)S(1)} async-done(((bf16[96,24,128]{2,1,0:T(8,128)(2,1)}), bf16[96,24,128]{2,1,0:T(8,128)(2,1)S(1)}, u32[]{:S(2)}, u32[]{:S(2)}) %all-to-all-start) | async-done | bytes 589856 | tf_op jit(solution)/shard_map/all_to_all | solution.py:410
  60.7 5.4 %shard_map.155 = (bf16[2304,128]{1,0:T(8,128)(2,1)}, bf16[1296,128]{1,0:T(8,128)(2,1)}) custom-call(bf16[2304,128]{1,0:T(8,128)(2,1)S(1)} %bitcast.29, bf16[2048,768]{1,0:T(8,128)(2,1)} %bitcast.37, bf16[384,2048]{1,0:T(8,128)(2,1)} %bitcast.33), custom_call_target="tpu_custom_call" | custom-call | flops 1358954496 | bytes 4718592 | tf_op jit(solution)/shard_map/pallas_call | solution.py:431
  66.2 10.5 %all-to-all-start.1 = ((bf16[96,24,128]{2,1,0:T(8,128)(2,1)}), bf16[96,24,128]{2,1,0:T(8,128)(2,1)S(1)}, u32[]{:S(2)}, u32[]{:S(2)}) async-start(bf16[96,24,128]{2,1,0:T(8,128)(2,1)} %bitcast.43), calls=%async_computation.1 | async-start | bytes 1179648 | tf_op jit(solution)/shard_map/all_to_all | solution.py:410
  76.7 0.1 pad_add_fusion.place_ref
  76.7 0.0 copy-start.1
  76.7 1.0 copy-done.1
  77.7 1.8 shard_map.158
  79.6 5.0 %collective-permute-start.3 = (bf16[1872,128]{1,0:T(8,128)(2,1)}, bf16[1872,128]{1,0:T(8,128)(2,1)S(1)}, u32[]{:S(2)}, u32[]{:S(2)}) collective-permute-start(bf16[1872,128]{1,0:T(8,128)(2,1)} %get-tuple-element.56), channel_id=1, source_target_pairs={{0,2},{2,4},{4,6},{6,0},{1,3},{3,5},{5,7},{7,1},{8,10},{10,12},{12... | collective-permute-start | bytes 1437704 | tf_op jit(solution)/shard_map/ppermute | solution.py:461
  84.5 2.3 %collective-permute-start.4 = (bf16[1872,128]{1,0:T(8,128)(2,1)}, bf16[1872,128]{1,0:T(8,128)(2,1)S(1)}, u32[]{:S(2)}, u32[]{:S(2)}) collective-permute-start(bf16[1872,128]{1,0:T(8,128)(2,1)} %get-tuple-element.57), channel_id=1, source_target_pairs={{0,4},{2,6},{4,0},{6,2},{1,5},{3,7},{5,1},{7,3},{8,12},{10,14},{12... | collective-permute-start | bytes 1437704 | tf_op jit(solution)/shard_map/ppermute | solution.py:461
  86.9 3.9 %collective-permute-start.5 = (bf16[1872,128]{1,0:T(8,128)(2,1)}, bf16[1872,128]{1,0:T(8,128)(2,1)S(1)}, u32[]{:S(2)}, u32[]{:S(2)}) collective-permute-start(bf16[1872,128]{1,0:T(8,128)(2,1)} %get-tuple-element.58), channel_id=1, source_target_pairs={{0,6},{2,0},{4,2},{6,4},{1,7},{3,1},{5,3},{7,5},{8,14},{10,8},{12,... | collective-permute-start | bytes 1437704 | tf_op jit(solution)/shard_map/ppermute | solution.py:461
  90.8 3.4 %shard_map.156 = (bf16[144,2304]{1,0:T(8,128)(2,1)}, bf16[144,2304]{1,0:T(8,128)(2,1)}, bf16[2304,144]{1,0:T(8,128)(2,1)}, bf16[2304,144]{1,0:T(8,128)(2,1)}) custom-call(bf16[176,256]{1,0:T(8,128)(2,1)S(1)} %collective-permute-done.packed_ref), custom_call_target="tpu_custom_call" | custom-call | flops 679477248 | bytes 2654208 | tf_op jit(solution)/shard_map/pallas_call | solution.py:447
  94.2 5.7 %all-to-all-done.1 = bf16[96,24,128]{2,1,0:T(8,128)(2,1)S(1)} async-done(((bf16[96,24,128]{2,1,0:T(8,128)(2,1)}), bf16[96,24,128]{2,1,0:T(8,128)(2,1)S(1)}, u32[]{:S(2)}, u32[]{:S(2)}) %all-to-all-start.1) | async-done | bytes 589856 | tf_op jit(solution)/shard_map/all_to_all | solution.py:410
  99.9 0.0 copy-start.2
  99.9 4.5 %shard_map.157 = (bf16[144,256]{1,0:T(8,128)(2,1)S(1)}, bf16[2304,128]{1,0:T(8,128)(2,1)}) custom-call(bf16[2304,128]{1,0:T(8,128)(2,1)S(1)} %bitcast.36, bf16[144,256]{1,0:T(8,128)(2,1)S(1)} %collective-permute-done.1.target_ref, bf16[144,2304]{1,0:T(8,128)(2,1)} %get-tuple-element.49.refs_0_, bf16[144,2304]{1,0:T(8,128)(2,1)} %get-tuple-element.50.refs_1_, ...), custom_call_target="tpu_custom_call" | custom-call | flops 1019215872 | bytes 2654208 | tf_op jit(solution)/shard_map/pallas_call | solution.py:465
  104.3 10.9 %all-to-all-start.2 = ((bf16[96,24,128]{2,1,0:T(8,128)(2,1)}), bf16[96,24,128]{2,1,0:T(8,128)(2,1)}, u32[]{:S(2)}, u32[]{:S(2)}) async-start(bf16[96,24,128]{2,1,0:T(8,128)(2,1)} %bitcast.42), calls=%async_computation.2 | async-start | bytes 1179648 | tf_op jit(solution)/shard_map/all_to_all | solution.py:410
  115.2 0.0 collective-permute-done.3.part1
  115.2 0.0 collective-permute-done.4.part2
  115.2 0.0 collective-permute-done.5.part3
  115.2 0.0 copy-done.2
  115.2 1.9 %shard_map.159 = bf16[6336,128]{1,0:T(8,128)(2,1)} custom-call(s32[2]{0:T(128)S(1)} %pad_add_fusion.place_ref, bf16[2304,128]{1,0:T(8,128)(2,1)S(1)} %bitcast.31, bf16[1296,128]{1,0:T(8,128)(2,1)S(1)} %copy-done.2, bf16[1872,128]{1,0:T(8,128)(2,1)S(1)} %collective-permute-done.3.part1, bf16[1872,128]{1,0:T(8,128)(2,1)S(1)} %collective-permute-done.4.part2, ...), custom_call_target="tpu_custom_call" | custom-call | bytes 3244032 | tf_op jit(solution)/shard_map/pallas_call | solution.py:477
  117.1 0.0 copy-start.3
  117.1 0.8 copy-done.3
  117.9 0.0 copy-start
  117.9 4.6 %collective-permute-start.6 = (bf16[6336,128]{1,0:T(8,128)(2,1)}, bf16[6336,128]{1,0:T(8,128)(2,1)}, u32[]{:S(2)}, u32[]{:S(2)}) collective-permute-start(bf16[6336,128]{1,0:T(8,128)(2,1)} %shard_map.159), channel_id=1, source_target_pairs={{0,1},{1,0},{2,3},{3,2},{4,5},{5,4},{6,7},{7,6},{8,9},{9,8},{10,11... | collective-permute-start | bytes 4866056 | tf_op jit(solution)/shard_map/ppermute | solution.py:480
  122.5 1.8 copy.18
  124.3 1.8 copy.19
  126.1 0.0 copy-done
  126.1 0.7 dynamic-slice_bitcast_fusion.refs_1_
  126.8 1.8 constant_dynamic-slice_fusion.refs_6_
  128.6 0.0 collective-permute-done.6.far_ref
  128.6 0.0 copy-start.4
  128.6 1.0 copy-done.4
  129.6 4.0 %shard_map.160 = (bf16[256,1152]{1,0:T(8,128)(2,1)}, bf16[384,1152]{1,0:T(8,128)(2,1)}, bf16[1152,768]{1,0:T(8,128)(2,1)}) custom-call(s32[2]{0:T(128)S(1)} %pad_add_fusion.place_ref, bf16[2304,128]{1,0:T(8,128)(2,1)S(1)} %bitcast.32, bf16[1296,128]{1,0:T(8,128)(2,1)S(1)} %copy-done.2, bf16[1872,128]{1,0:T(8,128)(2,1)S(1)} %collective-permute-done.3.part1, ...), custom_call_target="tpu_custom_call" | custom-call | flops 339738624 | bytes 3538944 | tf_op jit(solution)/shard_map/pallas_call | solution.py:481
  133.6 4.5 %all-to-all-done.2 = bf16[96,24,128]{2,1,0:T(8,128)(2,1)} async-done(((bf16[96,24,128]{2,1,0:T(8,128)(2,1)}), bf16[96,24,128]{2,1,0:T(8,128)(2,1)}, u32[]{:S(2)}, u32[]{:S(2)}) %all-to-all-start.2) | async-done | bytes 589856 | tf_op jit(solution)/shard_map/all_to_all | solution.py:410
  138.2 11.0 %all-to-all-start.3 = ((bf16[8,288,128]{2,1,0:T(8,128)(2,1)}), bf16[8,288,128]{2,1,0:T(8,128)(2,1)S(1)}, u32[]{:S(2)}, u32[]{:S(2)}) async-start(bf16[8,288,128]{2,1,0:T(8,128)(2,1)} %bitcast.14), calls=%async_computation.3 | async-start | bytes 1179648 | tf_op jit(solution)/shard_map/all_to_all | solution.py:503
  149.2 3.8 %collective-permute-start.2 = (bf16[144,256]{1,0:T(8,128)(2,1)S(1)}, bf16[144,256]{1,0:T(8,128)(2,1)S(1)}, u32[]{:S(2)}, u32[]{:S(2)}) collective-permute-start(bf16[144,256]{1,0:T(8,128)(2,1)S(1)} %get-tuple-element.53), channel_id=1, source_target_pairs={{0,0},{1,8},{2,16},{3,24},{4,32},{5,40},{6,48},{7,56},{8,1},{9,9},... | collective-permute-start | bytes 221192 | tf_op jit(solution)/shard_map/ppermute | solution.py:405
  153.0 2.3 %collective-permute-done.2 = bf16[144,256]{1,0:T(8,128)(2,1)S(1)} collective-permute-done((bf16[144,256]{1,0:T(8,128)(2,1)S(1)}, bf16[144,256]{1,0:T(8,128)(2,1)S(1)}, u32[]{:S(2)}, u32[]{:S(2)}) %collective-permute-start.2) | collective-permute-done | bytes 73760 | tf_op jit(solution)/shard_map/ppermute | solution.py:405
  155.3 2.1 %shard_map.161 = bf16[144,384]{1,0:T(8,128)(2,1)S(1)} custom-call(bf16[2304,128]{1,0:T(8,128)(2,1)} %bitcast.8.rows_ref, bf16[384,2048]{1,0:T(8,128)(2,1)S(1)} %bitcast.34), custom_call_target="tpu_custom_call" | custom-call | flops 452984832 | bytes 1572864 | tf_op jit(solution)/shard_map/pallas_call | solution.py:506
  157.4 20.7 %all_gather.3.hidden_grad_ref = bf16[1152,384]{1,0:T(8,128)(2,1)S(1)} all-gather(bf16[144,384]{1,0:T(8,128)(2,1)S(1)} %shard_map.161), channel_id=1, replica_groups=mesh['z'=12,'y'=8,'x'=4,'core'=2] {'x','core'}, dimensions={0}, use_global_device_ids=true | all-gather | bytes 995328 | tf_op jit(solution)/shard_map/all_gather | solution.py:509
  178.1 0.0 all-to-all-done.3
  178.1 4.4 %shard_map.162 = (bf16[256,768]{1,0:T(8,128)(2,1)S(1)}, bf16[256,768]{1,0:T(8,128)(2,1)S(1)}, bf16[256,768]{1,0:T(8,128)(2,1)S(1)}, bf16[384,256]{1,0:T(8,128)(2...) custom-call(bf16[2304,128]{1,0:T(8,128)(2,1)S(1)} %bitcast.35, bf16[1152,384]{1,0:T(8,128)(2,1)S(1)} %all_gather.3.hidden_grad_ref, ...), custom_call_target="tpu_custom_call" | custom-call | flops 679477248 | bytes 1572864 | tf_op jit(solution)/shard_map/pallas_call | solution.py:512
  182.6 0.8 reshape.89
  183.4 0.8 reshape.90
  184.2 0.8 reshape.91
  185.1 0.6 copy.21
Async XLA Ops:
  0.6 36.9 %copy-start.5 = (bf16[144,256]{1,0:T(8,128)(2,1)S(1)}, bf16[144,256]{1,0:T(8,128)(2,1)}, u32[]{:S(2)}) copy-start(bf16[144,256]{1,0:T(8,128)(2,1)} %param.11) | copy-start | bytes 221188
  1.6 6.8 %collective-permute-start = (bf16[176,256]{1,0:T(8,128)(2,1)S(1)}, bf16[176,256]{1,0:T(8,128)(2,1)S(1)}, u32[]{:S(2)}, u32[]{:S(2)}) collective-permute-start(bf16[176,256]{1,0:T(8,128)(2,1)S(1)} %shard_map.153), channel_id=1, source_target_pairs={{0,0},{1,8},{2,16},{3,24},{4,32},{5,40},{6,48},{7,56},{8,1},{9,9},... | collective-permute-start | bytes 270344 | tf_op jit(solution)/shard_map/ppermute | solution.py:405
  10.3 50.4 %all-to-all-start = ((bf16[96,24,128]{2,1,0:T(8,128)(2,1)}), bf16[96,24,128]{2,1,0:T(8,128)(2,1)S(1)}, u32[]{:S(2)}, u32[]{:S(2)}) async-start(bf16[96,24,128]{2,1,0:T(8,128)(2,1)} %bitcast.2), calls=%async_computation | async-start | bytes 1179648 | tf_op jit(solution)/shard_map/all_to_all | solution.py:410
  37.5 10.2 %collective-permute-start.1 = (bf16[144,256]{1,0:T(8,128)(2,1)S(1)}, bf16[144,256]{1,0:T(8,128)(2,1)S(1)}, u32[]{:S(2)}, u32[]{:S(2)}) collective-permute-start(bf16[144,256]{1,0:T(8,128)(2,1)S(1)} %copy-done.5), channel_id=1, source_target_pairs={{0,0},{1,8},{2,16},{3,24},{4,32},{5,40},{6,48},{7,56},{8,1},{9,9},... | collective-permute-start | bytes 221192 | tf_op jit(solution)/shard_map/ppermute | solution.py:405
  66.2 33.7 %all-to-all-start.1 = ((bf16[96,24,128]{2,1,0:T(8,128)(2,1)}), bf16[96,24,128]{2,1,0:T(8,128)(2,1)S(1)}, u32[]{:S(2)}, u32[]{:S(2)}) async-start(bf16[96,24,128]{2,1,0:T(8,128)(2,1)} %bitcast.43), calls=%async_computation.1 | async-start | bytes 1179648 | tf_op jit(solution)/shard_map/all_to_all | solution.py:410
  76.7 1.0 copy-start.1
  79.6 35.6 %collective-permute-start.3 = (bf16[1872,128]{1,0:T(8,128)(2,1)}, bf16[1872,128]{1,0:T(8,128)(2,1)S(1)}, u32[]{:S(2)}, u32[]{:S(2)}) collective-permute-start(bf16[1872,128]{1,0:T(8,128)(2,1)} %get-tuple-element.56), channel_id=1, source_target_pairs={{0,2},{2,4},{4,6},{6,0},{1,3},{3,5},{5,7},{7,1},{8,10},{10,12},{12... | collective-permute-start | bytes 1437704 | tf_op jit(solution)/shard_map/ppermute | solution.py:461
  84.5 30.7 %collective-permute-start.4 = (bf16[1872,128]{1,0:T(8,128)(2,1)}, bf16[1872,128]{1,0:T(8,128)(2,1)S(1)}, u32[]{:S(2)}, u32[]{:S(2)}) collective-permute-start(bf16[1872,128]{1,0:T(8,128)(2,1)} %get-tuple-element.57), channel_id=1, source_target_pairs={{0,4},{2,6},{4,0},{6,2},{1,5},{3,7},{5,1},{7,3},{8,12},{10,14},{12... | collective-permute-start | bytes 1437704 | tf_op jit(solution)/shard_map/ppermute | solution.py:461
  86.9 28.3 %collective-permute-start.5 = (bf16[1872,128]{1,0:T(8,128)(2,1)}, bf16[1872,128]{1,0:T(8,128)(2,1)S(1)}, u32[]{:S(2)}, u32[]{:S(2)}) collective-permute-start(bf16[1872,128]{1,0:T(8,128)(2,1)} %get-tuple-element.58), channel_id=1, source_target_pairs={{0,6},{2,0},{4,2},{6,4},{1,7},{3,1},{5,3},{7,5},{8,14},{10,8},{12,... | collective-permute-start | bytes 1437704 | tf_op jit(solution)/shard_map/ppermute | solution.py:461
  99.9 15.4 %copy-start.2 = (bf16[1296,128]{1,0:T(8,128)(2,1)S(1)}, bf16[1296,128]{1,0:T(8,128)(2,1)}, u32[]{:S(2)}) copy-start(bf16[1296,128]{1,0:T(8,128)(2,1)} %get-tuple-element.55.factors_ref.near_factors_ref) | copy-start | bytes 995332
  104.3 33.8 %all-to-all-start.2 = ((bf16[96,24,128]{2,1,0:T(8,128)(2,1)}), bf16[96,24,128]{2,1,0:T(8,128)(2,1)}, u32[]{:S(2)}, u32[]{:S(2)}) async-start(bf16[96,24,128]{2,1,0:T(8,128)(2,1)} %bitcast.42), calls=%async_computation.2 | async-start | bytes 1179648 | tf_op jit(solution)/shard_map/all_to_all | solution.py:410
  117.1 0.8 copy-start.3
  117.9 8.2 %copy-start = (bf16[1,384,2048]{2,1,0:T(8,128)(2,1)S(1)}, bf16[1,384,2048]{2,1,0:T(8,128)(2,1)}, u32[]{:S(2)}) copy-start(bf16[1,384,2048]{2,1,0:T(8,128)(2,1)} %param.17) | copy-start | bytes 4718596
  117.9 10.7 %collective-permute-start.6 = (bf16[6336,128]{1,0:T(8,128)(2,1)}, bf16[6336,128]{1,0:T(8,128)(2,1)}, u32[]{:S(2)}, u32[]{:S(2)}) collective-permute-start(bf16[6336,128]{1,0:T(8,128)(2,1)} %shard_map.159), channel_id=1, source_target_pairs={{0,1},{1,0},{2,3},{3,2},{4,5},{5,4},{6,7},{7,6},{8,9},{9,8},{10,11... | collective-permute-start | bytes 4866056 | tf_op jit(solution)/shard_map/ppermute | solution.py:480
  128.6 1.0 copy-start.4
  138.2 40.0 %all-to-all-start.3 = ((bf16[8,288,128]{2,1,0:T(8,128)(2,1)}), bf16[8,288,128]{2,1,0:T(8,128)(2,1)S(1)}, u32[]{:S(2)}, u32[]{:S(2)}) async-start(bf16[8,288,128]{2,1,0:T(8,128)(2,1)} %bitcast.14), calls=%async_computation.3 | async-start | bytes 1179648 | tf_op jit(solution)/shard_map/all_to_all | solution.py:503
  149.2 6.1 %collective-permute-start.2 = (bf16[144,256]{1,0:T(8,128)(2,1)S(1)}, bf16[144,256]{1,0:T(8,128)(2,1)S(1)}, u32[]{:S(2)}, u32[]{:S(2)}) collective-permute-start(bf16[144,256]{1,0:T(8,128)(2,1)S(1)} %get-tuple-element.53), channel_id=1, source_target_pairs={{0,0},{1,8},{2,16},{3,24},{4,32},{5,40},{6,48},{7,56},{8,1},{9,9},... | collective-permute-start | bytes 221192 | tf_op jit(solution)/shard_map/ppermute | solution.py:405

commit v4 on v3

--- a/solution.py
+++ b/solution.py
@@ -184,7 +184,7 @@
 
 
 def forward_kernel(
-    rows_ref, w_in_hbm, w_out_hbm, out_hbm, factors_ref, w_in_ref, w_out_ref, out_ref, sems
+    rows_ref, w_in_hbm, w_out_hbm, out_hbm, preacts_hbm, w_in_ref, w_out_ref, out_ref, preacts_ref, sems
 ):
     deep = WIDTH // LOADS
     copies = fetch(
@@ -193,7 +193,6 @@
         sems,
     )
     first, second = half_masks()
-    compact = compact_map(False)
     total = jnp.zeros((GROUP, 2 * FF), F32)
     for i in range(LOADS):
         parts = []
@@ -203,13 +202,12 @@
         copies[i].wait()
         total = total + dot(jnp.concatenate(parts, axis=1), w_in_ref[pl.ds(i * deep, deep), :])
     preacts = add_halves(total)
+    preacts_ref[...] = preacts
     gate_pre = preacts[:, :FF]
-    up_pre = preacts[:, FF:]
-    sigmoid = jax.nn.sigmoid(gate_pre)
-    silu = gate_pre * sigmoid
-    hidden = (silu * up_pre).astype(BF16)
+    hidden = (gate_pre * jax.nn.sigmoid(gate_pre) * preacts[:, FF:]).astype(BF16)
     copies[LOADS].wait()
-    sends = []
+    sends = [pltpu.make_async_copy(preacts_ref, preacts_hbm, sems.at[LOADS + 1 + NY])]
+    sends[0].start()
     for y in range(NY):
         rows = pl.ds(y * GROUP, GROUP)
         part = dot(hidden, w_out_ref[:, pl.ds(y * SLICE, SLICE)])
@@ -217,14 +215,20 @@
         send = pltpu.make_async_copy(out_ref.at[rows, :], out_hbm.at[rows, :], sems.at[LOADS + 1 + y])
         send.start()
         sends.append(send)
-    slope = up_pre * sigmoid * (1.0 + gate_pre * (1.0 - sigmoid))
-    for i, factor in enumerate((hidden, slope.astype(BF16), silu.astype(BF16))):
-        values = dot(compact, factor).astype(BF16)
-        for j in range(LANES):
-            place = (i * LANES + j) * CHUNK
-            factors_ref[pl.ds(place, CHUNK), :] = values[:, j * HALF : (j + 1) * HALF]
     for send in sends:
         send.wait()
+
+
+def factors_of(preacts):
+    gate_pre = preacts[:, :FF]
+    up_pre = preacts[:, FF:]
+    sigmoid = jax.nn.sigmoid(gate_pre)
+    silu = gate_pre * sigmoid
+    slope = up_pre * sigmoid * (1.0 + gate_pre * (1.0 - sigmoid))
+    compact = compact_map(False)
+    for factor in (silu * up_pre, slope, silu):
+        values = dot(compact, factor.astype(BF16)).astype(BF16)
+        yield from (values[:, j * HALF : (j + 1) * HALF] for j in range(LANES))
 
 
 def combine_kernel(back_ref, target_ref, *refs):
@@ -266,7 +270,9 @@
     return pl.multiple_of(2 * GROUP * lax.rem(x + shift, CHIPS), 2 * GROUP)
 
 
-def parts_kernel(place_ref, rows_ref, factors_ref, *part_refs):
+def parts_kernel(place_ref, rows_ref, preacts_ref, factors_ref, *part_refs):
+    for i, values in enumerate(factors_of(preacts_ref[...])):
+        factors_ref[pl.ds(i * CHUNK, CHUNK), :] = values
     for shift, part_ref in enumerate(part_refs, 1):
         part_ref[: 2 * GROUP, :] = rows_ref[pl.ds(rows_for(place_ref[0], shift), 2 * GROUP), :]
         part_ref[2 * GROUP :, :] = factors_ref[...]
@@ -366,6 +372,10 @@
         )
 
 
+def copy_kernel(value_ref, out_ref):
+    out_ref[...] = value_ref[...]
+
+
 def shape_of(*dims, dtype=BF16):
     return jax.ShapeDtypeStruct(dims, dtype)
 
@@ -428,9 +438,9 @@
     wide = [pltpu.VMEM((GROUP, WIDTH), BF16)]
     vmem, hbm = pl.BlockSpec(memory_space=pltpu.VMEM), pl.BlockSpec(memory_space=pltpu.HBM)
     arrived, target_here = lax.optimization_barrier((arrived, target_here))
-    out_rows, factors = call(
+    out_rows, preacts = call(
         forward_kernel,
-        [in_hbm(ROWS, HALF), in_hbm(FACTORS, HALF)],
+        [in_hbm(ROWS, HALF), pltpu.HBM((GROUP, 2 * FF), F32)],
         6 * GROUP * WIDTH * FF,
         6 * WIDTH * FF,
         24,
@@ -438,10 +448,11 @@
             pltpu.VMEM((WIDTH, 2 * FF), BF16),
             pltpu.VMEM((FF, WIDTH), BF16),
             pltpu.VMEM((ROWS, HALF), BF16),
-            pltpu.SemaphoreType.DMA((LOADS + 1 + NY,)),
+            pltpu.VMEM((GROUP, 2 * FF), F32),
+            pltpu.SemaphoreType.DMA((LOADS + 2 + NY,)),
         ],
         [vmem, hbm, hbm],
-        [hbm, vmem],
+        [hbm, hbm],
     )(arrived, pin(w_gate_up), pin(w_down))
     out_rows, packed = lax.optimization_barrier((out_rows, packed))
     weights = call(
@@ -454,9 +465,15 @@
     returned = over_experts(out_rows)
     placed = [pl.BlockSpec(memory_space=pltpu.SMEM)]
     place = jnp.stack([x, core]).astype(jnp.int32)
-    parts = call(
-        parts_kernel, [shape_of(PART, HALF)] * 3, 0, 4 * PART * HALF, 8, (), placed + [vmem] * 2
-    )(place, arrived, factors)
+    factors, *parts = call(
+        parts_kernel,
+        [in_hbm(FACTORS, HALF)] + [shape_of(PART, HALF)] * 3,
+        0,
+        4 * PART * HALF,
+        12,
+        (),
+        placed + [vmem] * 2,
+    )(place, arrived, preacts)
     parts = [
         lax.ppermute(part, "x", [(i, (i + shift) % CHIPS) for i in range(CHIPS)])
         for shift, part in enumerate(parts, 1)
@@ -472,7 +489,7 @@
         [vmem] * 2 + [hbm] * 4,
     )(returned, target_here, *map(pin, weights))
     grads = over_experts(slot_grad)
-    mixed = change_places(mixed_here)
+    mixed = call(copy_kernel, in_hbm(TOK, SLICE), 0, 4 * TOK * SLICE, 4)(change_places(mixed_here))
     slot_grad, *parts = lax.optimization_barrier((slot_grad, *parts))
     far = call(
         far_kernel, shape_of(CHIPS * FAR, HALF), 0, 4 * CHIPS * FAR * HALF, 16, (), placed + [vmem] * 5
@@ -496,8 +513,8 @@
         m_out.reshape(flat_out),
         v_out.reshape(flat_out),
     ]
-    grads, _, rows_t, hidden_t, slopes, *states = lax.optimization_barrier(
-        (grads, mixed[:8, :HALF], rows_t, hidden_t, slopes, *states)
+    grads, mixed, rows_t, hidden_t, slopes, *states = lax.optimization_barrier(
+        (grads, mixed, rows_t, hidden_t, slopes, *states)
     )
 
     own_grads = lax.all_to_all(

time: 187 us -> 180 us (0.963)
  blocking collectives: 20.7 us -> 17.3 us
  local copies, waits for them, and re-layouts: 16.2 us -> 13.6 us
  waiting for transfers between devices: 28.4 us -> 26.1 us
    all_to_all x3, waiting for transfers between devices: 23.2 us -> 19.2 us  [over_experts(): lax.all_to_all(messages, ('y', 'z'), split_axis=0, concat_axis=0, tiled=T...]
    all_gather x1, blocking collectives: 20.7 us -> 17.3 us  [shards(): all_grads = lax.all_gather(hidden_grad, ('x', 'core'), axis=0, tiled=True)]
    unnamed x16 -> x15, local copies, waits for them, and re-layouts: 11.2 us -> 8.59 us
    pallas_call x2 -> x3, Pallas kernels: 7.28 us -> 7.62 us  [the longest x1 4.68 us: shards(): call(forward_kernel, [in_hbm(ROWS, HALF), pltpu.HBM((GROUP, 2 * FF), F32)...]
  transfers between devices with their start and end apart: 11 -> 11, of which waited for: 6 -> 5; matrix products, arithmetic and copies ran while one was open for 6% -> 6% of each run, Pallas kernels for 10% -> 11%
where the time goes in v4:
time: 180 us; the launch traced here: 178 us
  starting transfers between devices  89.1 us (50%)
  Pallas kernels  30.8 us (17%)
  waiting for transfers between devices  26.1 us (14%)
  blocking collectives  17.3 us (10%)
  local copies, waits for them, and re-layouts  13.6 us (8%)
    all_to_all x3, starting transfers between devices, over_experts(): lax.all_to_all(messages, ('y', 'z'), split_axis=0, concat_axis=0, tiled=T...  48.9 us
    all_to_all x3, waiting for transfers between devices, over_experts(): lax.all_to_all(messages, ('y', 'z'), split_axis=0, concat_axis=0, tiled=T...  19.2 us
    all_gather x1, blocking collectives, shards(): all_grads = lax.all_gather(hidden_grad, ('x', 'core'), axis=0, tiled=True)  17.3 us
    ppermute x3, starting transfers between devices, change_places(): return lax.ppermute(value, ('z', 'y', 'x', 'core'), pairs)  12.8 us
    all_to_all x1, starting transfers between devices, shards(): lax.all_to_all(grads.reshape(NE, GROUP, HALF), ('x', 'core'), split_axis=...  11.6 us
    ppermute x3, starting transfers between devices, shards(): lax.ppermute(part, 'x', [(i, (i + shift) % CHIPS) for i in range(CHIPS)])  11.2 us
    unnamed x15, local copies, waits for them, and re-layouts  8.59 us
    ppermute x3, waiting for transfers between devices, change_places(): return lax.ppermute(value, ('z', 'y', 'x', 'core'), pairs)  6.89 us
  transfers between devices with their start and end apart: 11, of which 5 were waited for; matrix products, arithmetic and copies ran while one was open for 6% of the time, Pallas kernels for 11%

profile of v4, /device:TPU:1, one launch (start us, length us, event | category | flops | bytes accessed | tf_op | source)
XLA Modules:
  0.0 177.7 jit_solution(7526864258921798021)
XLA Ops:
  0.6 0.0 copy-start.5
  0.6 0.9 shard_map.153
  1.6 4.6 %collective-permute-start = (bf16[176,256]{1,0:T(8,128)(2,1)S(1)}, bf16[176,256]{1,0:T(8,128)(2,1)S(1)}, u32[]{:S(2)}, u32[]{:S(2)}) collective-permute-start(bf16[176,256]{1,0:T(8,128)(2,1)S(1)} %shard_map.153), channel_id=1, source_target_pairs={{0,0},{1,8},{2,16},{3,24},{4,32},{5,40},{6,48},{7,56},{8,1},{9,9},... | collective-permute-start | bytes 270344 | tf_op jit(solution)/shard_map/ppermute | solution.py:415
  6.2 2.2 %collective-permute-done.packed_ref = bf16[176,256]{1,0:T(8,128)(2,1)S(1)} collective-permute-done((bf16[176,256]{1,0:T(8,128)(2,1)S(1)}, bf16[176,256]{1,0:T(8,128)(2,1)S(1)}, u32[]{:S(2)}, u32[]{:S(2)}) %collective-permute-start) | collective-permute-done | bytes 90144 | tf_op jit(solution)/shard_map/ppermute | solution.py:415
  8.4 1.9 %shard_map.154 = bf16[2304,128]{1,0:T(8,128)(2,1)} custom-call(bf16[176,256]{1,0:T(8,128)(2,1)S(1)} %collective-permute-done.packed_ref), custom_call_target="tpu_custom_call" | custom-call | flops 509607936 | bytes 589824 | tf_op jit(solution)/shard_map/pallas_call | solution.py:435
  10.3 27.2 %all-to-all-start = ((bf16[96,24,128]{2,1,0:T(8,128)(2,1)}), bf16[96,24,128]{2,1,0:T(8,128)(2,1)S(1)}, u32[]{:S(2)}, u32[]{:S(2)}) async-start(bf16[96,24,128]{2,1,0:T(8,128)(2,1)} %bitcast.2), calls=%async_computation | async-start | bytes 1179648 | tf_op jit(solution)/shard_map/all_to_all | solution.py:420
  37.5 0.0 copy-done.5
  37.5 5.4 %collective-permute-start.1 = (bf16[144,256]{1,0:T(8,128)(2,1)S(1)}, bf16[144,256]{1,0:T(8,128)(2,1)S(1)}, u32[]{:S(2)}, u32[]{:S(2)}) collective-permute-start(bf16[144,256]{1,0:T(8,128)(2,1)S(1)} %copy-done.5), channel_id=1, source_target_pairs={{0,0},{1,8},{2,16},{3,24},{4,32},{5,40},{6,48},{7,56},{8,1},{9,9},... | collective-permute-start | bytes 221192 | tf_op jit(solution)/shard_map/ppermute | solution.py:415
  42.9 4.2 %copy.17 = bf16[256,8,2,384]{3,1,2,0:T(8,128)(2,1)} copy(bf16[256,8,2,384]{3,2,1,0:T(2,128)(2,1)} %bitcast.39) | data formatting | bytes 6291456
  47.1 0.6 collective-permute-done.1.target_ref
  47.7 13.0 %all-to-all-done = bf16[96,24,128]{2,1,0:T(8,128)(2,1)S(1)} async-done(((bf16[96,24,128]{2,1,0:T(8,128)(2,1)}), bf16[96,24,128]{2,1,0:T(8,128)(2,1)S(1)}, u32[]{:S(2)}, u32[]{:S(2)}) %all-to-all-start) | async-done | bytes 589856 | tf_op jit(solution)/shard_map/all_to_all | solution.py:420
  60.7 4.7 %shard_map.155 = (bf16[2304,128]{1,0:T(8,128)(2,1)}, f32[288,768]{1,0:T(8,128)}) custom-call(bf16[2304,128]{1,0:T(8,128)(2,1)S(1)} %bitcast.29, bf16[2048,768]{1,0:T(8,128)(2,1)} %bitcast.37, bf16[384,2048]{1,0:T(8,128)(2,1)} %bitcast.33), custom_call_target="tpu_custom_call" | custom-call | flops 1358954496 | bytes 4718592 | tf_op jit(solution)/shard_map/pallas_call | solution.py:441
  65.4 0.0 copy-start.4
  65.4 10.6 %all-to-all-start.1 = ((bf16[96,24,128]{2,1,0:T(8,128)(2,1)}), bf16[96,24,128]{2,1,0:T(8,128)(2,1)S(1)}, u32[]{:S(2)}, u32[]{:S(2)}) async-start(bf16[96,24,128]{2,1,0:T(8,128)(2,1)} %bitcast.43), calls=%async_computation.1 | async-start | bytes 1179648 | tf_op jit(solution)/shard_map/all_to_all | solution.py:420
  76.0 0.1 pad_add_fusion.place_ref
  76.1 0.0 copy-done.4
  76.1 2.3 %shard_map.159 = (bf16[1296,128]{1,0:T(8,128)(2,1)}, bf16[1872,128]{1,0:T(8,128)(2,1)}, bf16[1872,128]{1,0:T(8,128)(2,1)}, bf16[1872,128]{1,0:T(8,128)(2,1)}) custom-call(s32[2]{0:T(128)S(1)} %pad_add_fusion.place_ref, bf16[2304,128]{1,0:T(8,128)(2,1)S(1)} %bitcast.30, f32[288,768]{1,0:T(8,128)S(1)} %copy-done.4), custom_call_target="tpu_custom_call" | custom-call | bytes 958464 | tf_op jit(solution)/shard_map/pallas_call | solution.py:468
  78.4 5.0 %collective-permute-start.3 = (bf16[1872,128]{1,0:T(8,128)(2,1)}, bf16[1872,128]{1,0:T(8,128)(2,1)S(1)}, u32[]{:S(2)}, u32[]{:S(2)}) collective-permute-start(bf16[1872,128]{1,0:T(8,128)(2,1)} %get-tuple-element.59), channel_id=1, source_target_pairs={{0,2},{2,4},{4,6},{6,0},{1,3},{3,5},{5,7},{7,1},{8,10},{10,12},{12... | collective-permute-start | bytes 1437704 | tf_op jit(solution)/shard_map/ppermute | solution.py:478
  83.4 2.3 %collective-permute-start.4 = (bf16[1872,128]{1,0:T(8,128)(2,1)}, bf16[1872,128]{1,0:T(8,128)(2,1)S(1)}, u32[]{:S(2)}, u32[]{:S(2)}) collective-permute-start(bf16[1872,128]{1,0:T(8,128)(2,1)} %get-tuple-element.60), channel_id=1, source_target_pairs={{0,4},{2,6},{4,0},{6,2},{1,5},{3,7},{5,1},{7,3},{8,12},{10,14},{12... | collective-permute-start | bytes 1437704 | tf_op jit(solution)/shard_map/ppermute | solution.py:478
  85.8 3.9 %collective-permute-start.5 = (bf16[1872,128]{1,0:T(8,128)(2,1)}, bf16[1872,128]{1,0:T(8,128)(2,1)S(1)}, u32[]{:S(2)}, u32[]{:S(2)}) collective-permute-start(bf16[1872,128]{1,0:T(8,128)(2,1)} %get-tuple-element.61), channel_id=1, source_target_pairs={{0,6},{2,0},{4,2},{6,4},{1,7},{3,1},{5,3},{7,5},{8,14},{10,8},{12,... | collective-permute-start | bytes 1437704 | tf_op jit(solution)/shard_map/ppermute | solution.py:478
  89.6 3.4 %shard_map.156 = (bf16[144,2304]{1,0:T(8,128)(2,1)}, bf16[144,2304]{1,0:T(8,128)(2,1)}, bf16[2304,144]{1,0:T(8,128)(2,1)}, bf16[2304,144]{1,0:T(8,128)(2,1)}) custom-call(bf16[176,256]{1,0:T(8,128)(2,1)S(1)} %collective-permute-done.packed_ref), custom_call_target="tpu_custom_call" | custom-call | flops 679477248 | bytes 2654208 | tf_op jit(solution)/shard_map/pallas_call | solution.py:458
  93.0 6.2 %all-to-all-done.1 = bf16[96,24,128]{2,1,0:T(8,128)(2,1)S(1)} async-done(((bf16[96,24,128]{2,1,0:T(8,128)(2,1)}), bf16[96,24,128]{2,1,0:T(8,128)(2,1)S(1)}, u32[]{:S(2)}, u32[]{:S(2)}) %all-to-all-start.1) | async-done | bytes 589856 | tf_op jit(solution)/shard_map/all_to_all | solution.py:420
  99.3 0.0 copy-start.3
  99.3 4.5 %shard_map.157 = (bf16[144,256]{1,0:T(8,128)(2,1)S(1)}, bf16[2304,128]{1,0:T(8,128)(2,1)}) custom-call(bf16[2304,128]{1,0:T(8,128)(2,1)S(1)} %bitcast.36, bf16[144,256]{1,0:T(8,128)(2,1)S(1)} %collective-permute-done.1.target_ref, bf16[144,2304]{1,0:T(8,128)(2,1)} %get-tuple-element.51.refs_0_, bf16[144,2304]{1,0:T(8,128)(2,1)} %get-tuple-element.52.refs_1_, ...), custom_call_target="tpu_custom_call" | custom-call | flops 1019215872 | bytes 2654208 | tf_op jit(solution)/shard_map/pallas_call | solution.py:482
  103.7 11.0 %all-to-all-start.2 = ((bf16[96,24,128]{2,1,0:T(8,128)(2,1)}), bf16[96,24,128]{2,1,0:T(8,128)(2,1)}, u32[]{:S(2)}, u32[]{:S(2)}) async-start(bf16[96,24,128]{2,1,0:T(8,128)(2,1)} %bitcast.42), calls=%async_computation.2 | async-start | bytes 1179648 | tf_op jit(solution)/shard_map/all_to_all | solution.py:420
  114.8 0.0 collective-permute-done.3.part1
  114.8 0.0 collective-permute-done.4.part2
  114.8 0.0 collective-permute-done.5.part3
  114.8 0.0 copy-done.3
  114.8 1.9 %shard_map.160 = bf16[6336,128]{1,0:T(8,128)(2,1)} custom-call(s32[2]{0:T(128)S(1)} %pad_add_fusion.place_ref, bf16[2304,128]{1,0:T(8,128)(2,1)S(1)} %bitcast.31, bf16[1296,128]{1,0:T(8,128)(2,1)S(1)} %copy-done.3, bf16[1872,128]{1,0:T(8,128)(2,1)S(1)} %collective-permute-done.3.part1, bf16[1872,128]{1,0:T(8,128)(2,1)S(1)} %collective-permute-done.4.part2, ...), custom_call_target="tpu_custom_call" | custom-call | bytes 3244032 | tf_op jit(solution)/shard_map/pallas_call | solution.py:494
  116.7 0.0 copy-start.1
  116.7 0.8 copy-done.1
  117.5 0.0 copy-start
  117.5 4.6 %collective-permute-start.6 = (bf16[6336,128]{1,0:T(8,128)(2,1)}, bf16[6336,128]{1,0:T(8,128)(2,1)}, u32[]{:S(2)}, u32[]{:S(2)}) collective-permute-start(bf16[6336,128]{1,0:T(8,128)(2,1)} %shard_map.160), channel_id=1, source_target_pairs={{0,1},{1,0},{2,3},{3,2},{4,5},{5,4},{6,7},{7,6},{8,9},{9,8},{10,11... | collective-permute-start | bytes 4866056 | tf_op jit(solution)/shard_map/ppermute | solution.py:497
  122.1 1.8 %copy.18 = bf16[32,8,2,384]{3,1,2,0:T(8,128)(2,1)} copy(bf16[32,8,2,384]{3,2,1,0:T(2,128)(2,1)} %bitcast.44) | data formatting | bytes 786432
  123.9 1.8 %copy.19 = bf16[32,8,2,384]{3,1,2,0:T(8,128)(2,1)} copy(bf16[32,8,2,384]{3,2,1,0:T(2,128)(2,1)} %bitcast.45) | data formatting | bytes 786432
  125.7 0.0 copy-start.2
  125.7 1.8 %constant_dynamic-slice_fusion.refs_6_ = bf16[256,768]{1,0:T(8,128)(2,1)} fusion(bf16[2048,768]{1,0:T(8,128)(2,1)} %bitcast.38, s32[]{:T(128)S(6)} %select_n.4), kind=kLoop, calls=%fused_computation.2 | loop fusion | bytes 786436 | tf_op jit(solution)/shard_map/dynamic_slice | solution.py:509
  127.5 2.8 %collective-permute-start.2 = (bf16[144,256]{1,0:T(8,128)(2,1)S(1)}, bf16[144,256]{1,0:T(8,128)(2,1)S(1)}, u32[]{:S(2)}, u32[]{:S(2)}) collective-permute-start(bf16[144,256]{1,0:T(8,128)(2,1)S(1)} %get-tuple-element.56), channel_id=1, source_target_pairs={{0,0},{1,8},{2,16},{3,24},{4,32},{5,40},{6,48},{7,56},{8,1},{9,9},... | collective-permute-start | bytes 221192 | tf_op jit(solution)/shard_map/ppermute | solution.py:415
  130.3 0.0 copy-done
  130.3 0.7 dynamic-slice_bitcast_fusion.refs_1_
  131.0 4.0 %collective-permute-done.2.value_ref = bf16[144,256]{1,0:T(8,128)(2,1)S(1)} collective-permute-done((bf16[144,256]{1,0:T(8,128)(2,1)S(1)}, bf16[144,256]{1,0:T(8,128)(2,1)S(1)}, u32[]{:S(2)}, u32[]{:S(2)}) %collective-permute-start.2) | collective-permute-done | bytes 73760 | tf_op jit(solution)/shard_map/ppermute | solution.py:415
  135.1 0.6 shard_map.158
  135.7 0.0 collective-permute-done.6.far_ref
  135.7 0.0 copy-done.2
  135.7 4.0 %shard_map.161 = (bf16[256,1152]{1,0:T(8,128)(2,1)}, bf16[384,1152]{1,0:T(8,128)(2,1)}, bf16[1152,768]{1,0:T(8,128)(2,1)}) custom-call(s32[2]{0:T(128)S(1)} %pad_add_fusion.place_ref, bf16[2304,128]{1,0:T(8,128)(2,1)S(1)} %bitcast.32, bf16[1296,128]{1,0:T(8,128)(2,1)S(1)} %copy-done.3, bf16[1872,128]{1,0:T(8,128)(2,1)S(1)} %collective-permute-done.3.part1, ...), custom_call_target="tpu_custom_call" | custom-call | flops 339738624 | bytes 3538944 | tf_op jit(solution)/shard_map/pallas_call | solution.py:498
  139.7 0.0 all-to-all-done.2
  139.7 11.6 %all-to-all-start.3 = ((bf16[8,288,128]{2,1,0:T(8,128)(2,1)}), bf16[8,288,128]{2,1,0:T(8,128)(2,1)S(1)}, u32[]{:S(2)}, u32[]{:S(2)}) async-start(bf16[8,288,128]{2,1,0:T(8,128)(2,1)} %bitcast.14), calls=%async_computation.3 | async-start | bytes 1179648 | tf_op jit(solution)/shard_map/all_to_all | solution.py:520
  151.4 2.1 %shard_map.162 = bf16[144,384]{1,0:T(8,128)(2,1)S(1)} custom-call(bf16[2304,128]{1,0:T(8,128)(2,1)} %bitcast.8.rows_ref, bf16[384,2048]{1,0:T(8,128)(2,1)S(1)} %bitcast.34), custom_call_target="tpu_custom_call" | custom-call | flops 452984832 | bytes 1572864 | tf_op jit(solution)/shard_map/pallas_call | solution.py:523
  153.5 17.3 %all_gather.3.hidden_grad_ref = bf16[1152,384]{1,0:T(8,128)(2,1)S(1)} all-gather(bf16[144,384]{1,0:T(8,128)(2,1)S(1)} %shard_map.162), channel_id=1, replica_groups=mesh['z'=12,'y'=8,'x'=4,'core'=2] {'x','core'}, dimensions={0}, use_global_device_ids=true | all-gather | bytes 995328 | tf_op jit(solution)/shard_map/all_gather | solution.py:526
  170.8 0.0 all-to-all-done.3
  170.8 4.4 %shard_map.163 = (bf16[256,768]{1,0:T(8,128)(2,1)S(1)}, bf16[256,768]{1,0:T(8,128)(2,1)S(1)}, bf16[256,768]{1,0:T(8,128)(2,1)S(1)}, bf16[384,256]{1,0:T(8,128)(2...) custom-call(bf16[2304,128]{1,0:T(8,128)(2,1)S(1)} %bitcast.35, bf16[1152,384]{1,0:T(8,128)(2,1)S(1)} %all_gather.3.hidden_grad_ref, ...), custom_call_target="tpu_custom_call" | custom-call | flops 679477248 | bytes 1572864 | tf_op jit(solution)/shard_map/pallas_call | solution.py:529
  175.2 0.8 reshape.89
  176.1 0.8 reshape.90
  176.9 0.8 reshape.91
Async XLA Ops:
  0.6 36.9 %copy-start.5 = (bf16[144,256]{1,0:T(8,128)(2,1)S(1)}, bf16[144,256]{1,0:T(8,128)(2,1)}, u32[]{:S(2)}) copy-start(bf16[144,256]{1,0:T(8,128)(2,1)} %param.11) | copy-start | bytes 221188
  1.6 6.8 %collective-permute-start = (bf16[176,256]{1,0:T(8,128)(2,1)S(1)}, bf16[176,256]{1,0:T(8,128)(2,1)S(1)}, u32[]{:S(2)}, u32[]{:S(2)}) collective-permute-start(bf16[176,256]{1,0:T(8,128)(2,1)S(1)} %shard_map.153), channel_id=1, source_target_pairs={{0,0},{1,8},{2,16},{3,24},{4,32},{5,40},{6,48},{7,56},{8,1},{9,9},... | collective-permute-start | bytes 270344 | tf_op jit(solution)/shard_map/ppermute | solution.py:415
  10.3 50.4 %all-to-all-start = ((bf16[96,24,128]{2,1,0:T(8,128)(2,1)}), bf16[96,24,128]{2,1,0:T(8,128)(2,1)S(1)}, u32[]{:S(2)}, u32[]{:S(2)}) async-start(bf16[96,24,128]{2,1,0:T(8,128)(2,1)} %bitcast.2), calls=%async_computation | async-start | bytes 1179648 | tf_op jit(solution)/shard_map/all_to_all | solution.py:420
  37.5 10.2 %collective-permute-start.1 = (bf16[144,256]{1,0:T(8,128)(2,1)S(1)}, bf16[144,256]{1,0:T(8,128)(2,1)S(1)}, u32[]{:S(2)}, u32[]{:S(2)}) collective-permute-start(bf16[144,256]{1,0:T(8,128)(2,1)S(1)} %copy-done.5), channel_id=1, source_target_pairs={{0,0},{1,8},{2,16},{3,24},{4,32},{5,40},{6,48},{7,56},{8,1},{9,9},... | collective-permute-start | bytes 221192 | tf_op jit(solution)/shard_map/ppermute | solution.py:415
  65.4 10.7 %copy-start.4 = (f32[288,768]{1,0:T(8,128)S(1)}, f32[288,768]{1,0:T(8,128)}, u32[]{:S(2)}) copy-start(f32[288,768]{1,0:T(8,128)} %get-tuple-element.57.preacts_ref) | copy-start | bytes 2654212
  65.4 33.8 %all-to-all-start.1 = ((bf16[96,24,128]{2,1,0:T(8,128)(2,1)}), bf16[96,24,128]{2,1,0:T(8,128)(2,1)S(1)}, u32[]{:S(2)}, u32[]{:S(2)}) async-start(bf16[96,24,128]{2,1,0:T(8,128)(2,1)} %bitcast.43), calls=%async_computation.1 | async-start | bytes 1179648 | tf_op jit(solution)/shard_map/all_to_all | solution.py:420
  78.4 36.3 %collective-permute-start.3 = (bf16[1872,128]{1,0:T(8,128)(2,1)}, bf16[1872,128]{1,0:T(8,128)(2,1)S(1)}, u32[]{:S(2)}, u32[]{:S(2)}) collective-permute-start(bf16[1872,128]{1,0:T(8,128)(2,1)} %get-tuple-element.59), channel_id=1, source_target_pairs={{0,2},{2,4},{4,6},{6,0},{1,3},{3,5},{5,7},{7,1},{8,10},{10,12},{12... | collective-permute-start | bytes 1437704 | tf_op jit(solution)/shard_map/ppermute | solution.py:478
  83.4 31.4 %collective-permute-start.4 = (bf16[1872,128]{1,0:T(8,128)(2,1)}, bf16[1872,128]{1,0:T(8,128)(2,1)S(1)}, u32[]{:S(2)}, u32[]{:S(2)}) collective-permute-start(bf16[1872,128]{1,0:T(8,128)(2,1)} %get-tuple-element.60), channel_id=1, source_target_pairs={{0,4},{2,6},{4,0},{6,2},{1,5},{3,7},{5,1},{7,3},{8,12},{10,14},{12... | collective-permute-start | bytes 1437704 | tf_op jit(solution)/shard_map/ppermute | solution.py:478
  85.8 29.0 %collective-permute-start.5 = (bf16[1872,128]{1,0:T(8,128)(2,1)}, bf16[1872,128]{1,0:T(8,128)(2,1)S(1)}, u32[]{:S(2)}, u32[]{:S(2)}) collective-permute-start(bf16[1872,128]{1,0:T(8,128)(2,1)} %get-tuple-element.61), channel_id=1, source_target_pairs={{0,6},{2,0},{4,2},{6,4},{1,7},{3,1},{5,3},{7,5},{8,14},{10,8},{12,... | collective-permute-start | bytes 1437704 | tf_op jit(solution)/shard_map/ppermute | solution.py:478
  99.3 15.5 %copy-start.3 = (bf16[1296,128]{1,0:T(8,128)(2,1)S(1)}, bf16[1296,128]{1,0:T(8,128)(2,1)}, u32[]{:S(2)}) copy-start(bf16[1296,128]{1,0:T(8,128)(2,1)} %get-tuple-element.58.factors_ref.near_factors_ref) | copy-start | bytes 995332
  103.7 36.0 %all-to-all-start.2 = ((bf16[96,24,128]{2,1,0:T(8,128)(2,1)}), bf16[96,24,128]{2,1,0:T(8,128)(2,1)}, u32[]{:S(2)}, u32[]{:S(2)}) async-start(bf16[96,24,128]{2,1,0:T(8,128)(2,1)} %bitcast.42), calls=%async_computation.2 | async-start | bytes 1179648 | tf_op jit(solution)/shard_map/all_to_all | solution.py:420
  116.7 0.8 copy-start.1
  117.5 12.8 %copy-start = (bf16[1,384,2048]{2,1,0:T(8,128)(2,1)S(1)}, bf16[1,384,2048]{2,1,0:T(8,128)(2,1)}, u32[]{:S(2)}) copy-start(bf16[1,384,2048]{2,1,0:T(8,128)(2,1)} %param.17) | copy-start | bytes 4718596
  117.5 18.2 %collective-permute-start.6 = (bf16[6336,128]{1,0:T(8,128)(2,1)}, bf16[6336,128]{1,0:T(8,128)(2,1)}, u32[]{:S(2)}, u32[]{:S(2)}) collective-permute-start(bf16[6336,128]{1,0:T(8,128)(2,1)} %shard_map.160), channel_id=1, source_target_pairs={{0,1},{1,0},{2,3},{3,2},{4,5},{5,4},{6,7},{7,6},{8,9},{9,8},{10,11... | collective-permute-start | bytes 4866056 | tf_op jit(solution)/shard_map/ppermute | solution.py:497
  125.7 10.0 %copy-start.2 = (bf16[1872,128]{1,0:T(8,128)(2,1)S(1)}, bf16[1872,128]{1,0:T(8,128)(2,1)}, u32[]{:S(2)}) copy-start(bf16[1872,128]{1,0:T(8,128)(2,1)} %copy-done.1) | copy-start | bytes 1437700
  127.5 7.6 %collective-permute-start.2 = (bf16[144,256]{1,0:T(8,128)(2,1)S(1)}, bf16[144,256]{1,0:T(8,128)(2,1)S(1)}, u32[]{:S(2)}, u32[]{:S(2)}) collective-permute-start(bf16[144,256]{1,0:T(8,128)(2,1)S(1)} %get-tuple-element.56), channel_id=1, source_target_pairs={{0,0},{1,8},{2,16},{3,24},{4,32},{5,40},{6,48},{7,56},{8,1},{9,9},... | collective-permute-start | bytes 221192 | tf_op jit(solution)/shard_map/ppermute | solution.py:415
  139.7 31.0 %all-to-all-start.3 = ((bf16[8,288,128]{2,1,0:T(8,128)(2,1)}), bf16[8,288,128]{2,1,0:T(8,128)(2,1)S(1)}, u32[]{:S(2)}, u32[]{:S(2)}) async-start(bf16[8,288,128]{2,1,0:T(8,128)(2,1)} %bitcast.14), calls=%async_computation.3 | async-start | bytes 1179648 | tf_op jit(solution)/shard_map/all_to_all | solution.py:520

commit v5 on v4

--- a/solution.py
+++ b/solution.py
@@ -81,7 +81,9 @@
 
 def row_expert_map():
     shape = (NY, NZ, MSG, EXPERTS)
-    expert = iota(shape, 1) * NY + iota(shape, 0)
+    place = iota(shape, 0)
+    y = jnp.right_shift(place, 1) + (NY // 2) * jnp.bitwise_and(place, 1)
+    expert = iota(shape, 1) * NY + y
     return (expert == iota(shape, 3)).astype(F32).reshape(ROWS, EXPERTS).astype(BF16)
 
 
@@ -406,18 +408,19 @@
 
 
 def change_places(value):
+    of_y = [2 * (y % 4) + y // 4 for y in range(NY)]
     pairs = [
-        ((z * NY + y) * NE + e, (z * NY + e) * NE + y)
+        ((z * NY + y) * NE + e, (z * NY + of_y.index(e)) * NE + of_y[y])
         for z in range(NZ)
         for y in range(NY)
         for e in range(NE)
     ]
-    return lax.ppermute(value, ("z", "y", "x", "core"), pairs)
+    return lax.ppermute(value, ("z", "y_high", "y_low", "x", "core"), pairs)
 
 
 def over_experts(rows):
     messages = rows.reshape(EXPERTS, MSG, HALF)
-    moved = lax.all_to_all(messages, ("y", "z"), split_axis=0, concat_axis=0, tiled=True)
+    moved = lax.all_to_all(messages, ("y_low", "y_high", "z"), split_axis=0, concat_axis=0, tiled=True)
     return moved.reshape(ROWS, HALF)
 
 
@@ -437,7 +440,16 @@
     target_here = change_places(target)
     wide = [pltpu.VMEM((GROUP, WIDTH), BF16)]
     vmem, hbm = pl.BlockSpec(memory_space=pltpu.VMEM), pl.BlockSpec(memory_space=pltpu.HBM)
-    arrived, target_here = lax.optimization_barrier((arrived, target_here))
+    flat_in, flat_out = (SLICE, 2 * FF), (FF, SLICE)
+    states = [
+        lax.dynamic_slice_in_dim(w_gate_up, column * SLICE, SLICE, 0),
+        m_in.reshape(flat_in),
+        v_in.reshape(flat_in),
+        lax.dynamic_slice_in_dim(w_down, column * SLICE, SLICE, 1),
+        m_out.reshape(flat_out),
+        v_out.reshape(flat_out),
+    ]
+    arrived, target_here, *states = lax.optimization_barrier((arrived, target_here, *states))
     out_rows, preacts = call(
         forward_kernel,
         [in_hbm(ROWS, HALF), pltpu.HBM((GROUP, 2 * FF), F32)],
@@ -489,7 +501,7 @@
         [vmem] * 2 + [hbm] * 4,
     )(returned, target_here, *map(pin, weights))
     grads = over_experts(slot_grad)
-    mixed = call(copy_kernel, in_hbm(TOK, SLICE), 0, 4 * TOK * SLICE, 4)(change_places(mixed_here))
+    mixed = change_places(mixed_here)
     slot_grad, *parts = lax.optimization_barrier((slot_grad, *parts))
     far = call(
         far_kernel, shape_of(CHIPS * FAR, HALF), 0, 4 * CHIPS * FAR * HALF, 16, (), placed + [vmem] * 5
@@ -504,17 +516,10 @@
         [pltpu.VMEM((EXPERT_ROWS, SLICE), F32), pltpu.VMEM((EXPERT_ROWS, FF), F32)],
         placed + [vmem] * 6,
     )(place, arrived, factors, *parts, far)
-    flat_in, flat_out = (SLICE, 2 * FF), (FF, SLICE)
-    states = [
-        lax.dynamic_slice_in_dim(w_gate_up, column * SLICE, SLICE, 0),
-        m_in.reshape(flat_in),
-        v_in.reshape(flat_in),
-        lax.dynamic_slice_in_dim(w_down, column * SLICE, SLICE, 1),
-        m_out.reshape(flat_out),
-        v_out.reshape(flat_out),
-    ]
-    grads, mixed, rows_t, hidden_t, slopes, *states = lax.optimization_barrier(
-        (grads, mixed, rows_t, hidden_t, slopes, *states)
+    mixed, rows_t = lax.optimization_barrier((mixed, rows_t))
+    mixed = call(copy_kernel, in_hbm(TOK, SLICE), 0, 4 * TOK * SLICE, 4)(mixed)
+    grads, mixed, rows_t, hidden_t, slopes = lax.optimization_barrier(
+        (grads, mixed, rows_t, hidden_t, slopes)
     )
 
     own_grads = lax.all_to_all(
@@ -542,8 +547,10 @@
 
 
 def solution(mesh):
-    whole = Mesh(mesh.devices.reshape(NZ, NY, NE // 2, 2), ("z", "y", "x", "core"))
-    dp, expert = ("z", "y"), ("x", "core")
+    whole = Mesh(
+        mesh.devices.reshape(NZ, 2, NY // 2, NE // 2, 2), ("z", "y_high", "y_low", "x", "core")
+    )
+    dp, expert = ("z", "y_high", "y_low"), ("x", "core")
     return jax.shard_map(
         shards,
         mesh=whole,

time: 180 us -> 174 us (0.967); the launches traced: 178 us -> 174 us
  starting transfers between devices: 89.1 us -> 86.1 us
  Pallas kernels: 30.8 us -> 28.7 us
    ppermute x3, starting transfers between devices: 12.8 us -> 24.1 us  [change_places(): return lax.ppermute(value, ('z', 'y_high', 'y_low', 'x', 'core'), pairs)]
    all_to_all x3, starting transfers between devices: 48.9 us -> 39 us  [over_experts(): lax.all_to_all(messages, ('y_low', 'y_high', 'z'), split_axis=0, concat_a...]
    all_to_all x3, waiting for transfers between devices: 19.2 us -> 25 us  [over_experts(): lax.all_to_all(messages, ('y_low', 'y_high', 'z'), split_axis=0, concat_a...]
    ppermute x3, waiting for transfers between devices: 6.89 us -> 2.68 us  [change_places(): return lax.ppermute(value, ('z', 'y_high', 'y_low', 'x', 'core'), pairs)]
    all_to_all x1, starting transfers between devices: 11.6 us -> 8.52 us  [shards(): lax.all_to_all(grads.reshape(NE, GROUP, HALF), ('x', 'core'), split_axis=...]
    unnamed x15 -> x19, local copies, waits for them, and re-layouts: 8.59 us -> 6.93 us
  transfers between devices with their start and end apart: 11 -> 11, of which waited for: 5 -> 5; matrix products, arithmetic and copies ran while one was open for 6% -> 5% of each run, Pallas kernels for 11% -> 10%
where the time goes in v5:
time: 174 us
  starting transfers between devices  86.1 us (49%)
  Pallas kernels  28.7 us (16%)
  waiting for transfers between devices  27.7 us (16%)
  blocking collectives  17.3 us (10%)
  local copies, waits for them, and re-layouts  12.8 us (7%)
    all_to_all x3, starting transfers between devices, over_experts(): lax.all_to_all(messages, ('y_low', 'y_high', 'z'), split_axis=0, concat_a...  39 us
    all_to_all x3, waiting for transfers between devices, over_experts(): lax.all_to_all(messages, ('y_low', 'y_high', 'z'), split_axis=0, concat_a...  25 us
    ppermute x3, starting transfers between devices, change_places(): return lax.ppermute(value, ('z', 'y_high', 'y_low', 'x', 'core'), pairs)  24.1 us
    all_gather x1, blocking collectives, shards(): all_grads = lax.all_gather(hidden_grad, ('x', 'core'), axis=0, tiled=True)  17.3 us
    ppermute x3, starting transfers between devices, shards(): lax.ppermute(part, 'x', [(i, (i + shift) % CHIPS) for i in range(CHIPS)])  10.3 us
    all_to_all x1, starting transfers between devices, shards(): lax.all_to_all(grads.reshape(NE, GROUP, HALF), ('x', 'core'), split_axis=...  8.52 us
    unnamed x19, local copies, waits for them, and re-layouts  6.93 us
    pallas_call x1, Pallas kernels, shards(): call(forward_kernel, [in_hbm(ROWS, HALF), pltpu.HBM((GROUP, 2 * FF), F32)...  4.69 us
  transfers between devices with their start and end apart: 11, of which 5 were waited for; matrix products, arithmetic and copies ran while one was open for 5% of the time, Pallas kernels for 10%

profile of v5, /device:TPU:1, one launch (start us, length us, event | category | flops | bytes accessed | tf_op | source)
XLA Modules:
  0.0 173.6 jit_solution(9963376673669955302)
XLA Ops:
  0.6 0.0 copy-start.7
  0.6 0.0 copy-start.5
  0.7 1.0 shard_map.153
  1.6 0.0 copy-start.6
  1.6 9.0 %collective-permute-start = (bf16[176,256]{1,0:T(8,128)(2,1)S(1)}, bf16[176,256]{1,0:T(8,128)(2,1)S(1)}, u32[]{:S(2)}, u32[]{:S(2)}) collective-permute-start(bf16[176,256]{1,0:T(8,128)(2,1)S(1)} %shard_map.153), channel_id=1, source_target_pairs={{0,0},{1,32},{2,8},{3,40},{4,16},{5,48},{6,24},{7,56},{8,2},{9,34}... | collective-permute-start | bytes 270344 | tf_op jit(solution)/shard_map/ppermute | solution.py:418
  10.6 2.5 %collective-permute-done.packed_ref = bf16[176,256]{1,0:T(8,128)(2,1)S(1)} collective-permute-done((bf16[176,256]{1,0:T(8,128)(2,1)S(1)}, bf16[176,256]{1,0:T(8,128)(2,1)S(1)}, u32[]{:S(2)}, u32[]{:S(2)}) %collective-permute-start) | collective-permute-done | bytes 90144 | tf_op jit(solution)/shard_map/ppermute | solution.py:418
  13.1 1.9 %shard_map.154 = bf16[2304,128]{1,0:T(8,128)(2,1)} custom-call(bf16[176,256]{1,0:T(8,128)(2,1)S(1)} %collective-permute-done.packed_ref), custom_call_target="tpu_custom_call" | custom-call | flops 509607936 | bytes 589824 | tf_op jit(solution)/shard_map/pallas_call | solution.py:438
  15.0 20.5 %all-to-all-start = ((bf16[96,24,128]{2,1,0:T(8,128)(2,1)}), bf16[96,24,128]{2,1,0:T(8,128)(2,1)S(1)}, u32[]{:S(2)}, u32[]{:S(2)}) async-start(bf16[96,24,128]{2,1,0:T(8,128)(2,1)} %bitcast.2), calls=%async_computation | async-start | bytes 1179648 | tf_op jit(solution)/shard_map/all_to_all | solution.py:423
  35.5 0.0 copy-done.7
  35.5 8.4 %collective-permute-start.1 = (bf16[144,256]{1,0:T(8,128)(2,1)S(1)}, bf16[144,256]{1,0:T(8,128)(2,1)S(1)}, u32[]{:S(2)}, u32[]{:S(2)}) collective-permute-start(bf16[144,256]{1,0:T(8,128)(2,1)S(1)} %copy-done.7), channel_id=1, source_target_pairs={{0,0},{1,32},{2,8},{3,40},{4,16},{5,48},{6,24},{7,56},{8,2},{9,34}... | collective-permute-start | bytes 221192 | tf_op jit(solution)/shard_map/ppermute | solution.py:418
  44.0 0.0 copy-done.5
  44.0 0.8 copy.18
  44.8 0.0 copy-done.6
  44.8 0.8 copy.19
  45.6 4.2 %copy.17 = bf16[256,8,2,384]{3,1,2,0:T(8,128)(2,1)} copy(bf16[256,8,2,384]{3,2,1,0:T(2,128)(2,1)} %bitcast.39) | data formatting | bytes 6291456
  49.7 1.8 %constant_dynamic-slice_fusion.refs_6_ = bf16[256,768]{1,0:T(8,128)(2,1)} fusion(bf16[2048,768]{1,0:T(8,128)(2,1)} %bitcast.37, s32[]{:T(128)S(6)} %select_n.4), kind=kLoop, calls=%fused_computation.2 | loop fusion | bytes 786436 | tf_op jit(solution)/shard_map/dynamic_slice | solution.py:445
  51.5 1.6 dynamic-slice_bitcast_fusion.refs_1_
  53.1 0.0 collective-permute-done.1.target_ref
  53.1 7.8 %all-to-all-done = bf16[96,24,128]{2,1,0:T(8,128)(2,1)S(1)} async-done(((bf16[96,24,128]{2,1,0:T(8,128)(2,1)}), bf16[96,24,128]{2,1,0:T(8,128)(2,1)S(1)}, u32[]{:S(2)}, u32[]{:S(2)}) %all-to-all-start) | async-done | bytes 589856 | tf_op jit(solution)/shard_map/all_to_all | solution.py:423
  61.0 4.7 %shard_map.155 = (bf16[2304,128]{1,0:T(8,128)(2,1)}, f32[288,768]{1,0:T(8,128)}) custom-call(bf16[2304,128]{1,0:T(8,128)(2,1)S(1)} %bitcast.29, bf16[2048,768]{1,0:T(8,128)(2,1)} %bitcast.38, bf16[384,2048]{1,0:T(8,128)(2,1)} %bitcast.33), custom_call_target="tpu_custom_call" | custom-call | flops 1358954496 | bytes 4718592 | tf_op jit(solution)/shard_map/pallas_call | solution.py:453
  65.7 0.0 copy-start.4
  65.7 9.0 %all-to-all-start.1 = ((bf16[96,24,128]{2,1,0:T(8,128)(2,1)}), bf16[96,24,128]{2,1,0:T(8,128)(2,1)S(1)}, u32[]{:S(2)}, u32[]{:S(2)}) async-start(bf16[96,24,128]{2,1,0:T(8,128)(2,1)} %bitcast.43), calls=%async_computation.1 | async-start | bytes 1179648 | tf_op jit(solution)/shard_map/all_to_all | solution.py:423
  74.7 0.1 pad_add_fusion.place_ref
  74.8 0.0 copy-done.4
  74.8 2.3 %shard_map.158 = (bf16[1296,128]{1,0:T(8,128)(2,1)}, bf16[1872,128]{1,0:T(8,128)(2,1)}, bf16[1872,128]{1,0:T(8,128)(2,1)}, bf16[1872,128]{1,0:T(8,128)(2,1)}) custom-call(s32[2]{0:T(128)S(1)} %pad_add_fusion.place_ref, bf16[2304,128]{1,0:T(8,128)(2,1)S(1)} %bitcast.30, f32[288,768]{1,0:T(8,128)S(1)} %copy-done.4), custom_call_target="tpu_custom_call" | custom-call | bytes 958464 | tf_op jit(solution)/shard_map/pallas_call | solution.py:480
  77.1 3.9 %collective-permute-start.3 = (bf16[1872,128]{1,0:T(8,128)(2,1)}, bf16[1872,128]{1,0:T(8,128)(2,1)S(1)}, u32[]{:S(2)}, u32[]{:S(2)}) collective-permute-start(bf16[1872,128]{1,0:T(8,128)(2,1)} %get-tuple-element.61), channel_id=1, source_target_pairs={{0,2},{2,4},{4,6},{6,0},{1,3},{3,5},{5,7},{7,1},{8,10},{10,12},{12... | collective-permute-start | bytes 1437704 | tf_op jit(solution)/shard_map/ppermute | solution.py:490
  81.0 3.0 %collective-permute-start.4 = (bf16[1872,128]{1,0:T(8,128)(2,1)}, bf16[1872,128]{1,0:T(8,128)(2,1)S(1)}, u32[]{:S(2)}, u32[]{:S(2)}) collective-permute-start(bf16[1872,128]{1,0:T(8,128)(2,1)} %get-tuple-element.62), channel_id=1, source_target_pairs={{0,4},{2,6},{4,0},{6,2},{1,5},{3,7},{5,1},{7,3},{8,12},{10,14},{12... | collective-permute-start | bytes 1437704 | tf_op jit(solution)/shard_map/ppermute | solution.py:490
  84.0 3.4 %collective-permute-start.5 = (bf16[1872,128]{1,0:T(8,128)(2,1)}, bf16[1872,128]{1,0:T(8,128)(2,1)S(1)}, u32[]{:S(2)}, u32[]{:S(2)}) collective-permute-start(bf16[1872,128]{1,0:T(8,128)(2,1)} %get-tuple-element.63), channel_id=1, source_target_pairs={{0,6},{2,0},{4,2},{6,4},{1,7},{3,1},{5,3},{7,5},{8,14},{10,8},{12,... | collective-permute-start | bytes 1437704 | tf_op jit(solution)/shard_map/ppermute | solution.py:490
  87.5 3.4 %shard_map.156 = (bf16[144,2304]{1,0:T(8,128)(2,1)}, bf16[144,2304]{1,0:T(8,128)(2,1)}, bf16[2304,144]{1,0:T(8,128)(2,1)}, bf16[2304,144]{1,0:T(8,128)(2,1)}) custom-call(bf16[176,256]{1,0:T(8,128)(2,1)S(1)} %collective-permute-done.packed_ref), custom_call_target="tpu_custom_call" | custom-call | flops 679477248 | bytes 2654208 | tf_op jit(solution)/shard_map/pallas_call | solution.py:470
  90.9 9.2 %all-to-all-done.1 = bf16[96,24,128]{2,1,0:T(8,128)(2,1)S(1)} async-done(((bf16[96,24,128]{2,1,0:T(8,128)(2,1)}), bf16[96,24,128]{2,1,0:T(8,128)(2,1)S(1)}, u32[]{:S(2)}, u32[]{:S(2)}) %all-to-all-start.1) | async-done | bytes 589856 | tf_op jit(solution)/shard_map/all_to_all | solution.py:423
  100.0 0.0 copy-start.3
  100.0 4.5 %shard_map.157 = (bf16[144,256]{1,0:T(8,128)(2,1)S(1)}, bf16[2304,128]{1,0:T(8,128)(2,1)}) custom-call(bf16[2304,128]{1,0:T(8,128)(2,1)S(1)} %bitcast.36, bf16[144,256]{1,0:T(8,128)(2,1)S(1)} %collective-permute-done.1.target_ref, bf16[144,2304]{1,0:T(8,128)(2,1)} %get-tuple-element.53.refs_0_, bf16[144,2304]{1,0:T(8,128)(2,1)} %get-tuple-element.54.refs_1_, ...), custom_call_target="tpu_custom_call" | custom-call | flops 1019215872 | bytes 2654208 | tf_op jit(solution)/shard_map/pallas_call | solution.py:494
  104.5 9.5 %all-to-all-start.2 = ((bf16[96,24,128]{2,1,0:T(8,128)(2,1)}), bf16[96,24,128]{2,1,0:T(8,128)(2,1)}, u32[]{:S(2)}, u32[]{:S(2)}) async-start(bf16[96,24,128]{2,1,0:T(8,128)(2,1)} %bitcast.42), calls=%async_computation.2 | async-start | bytes 1179648 | tf_op jit(solution)/shard_map/all_to_all | solution.py:423
  114.0 0.0 collective-permute-done.3.part1
  114.0 0.0 collective-permute-done.4.part2
  114.0 0.0 collective-permute-done.5.part3
  114.0 0.0 copy-start.1
  114.0 0.0 copy-done.3
  114.0 0.6 shard_map.159
  114.7 0.1 copy-done.1
  114.8 4.1 %collective-permute-start.6 = (bf16[6336,128]{1,0:T(8,128)(2,1)S(1)}, bf16[6336,128]{1,0:T(8,128)(2,1)S(1)}, u32[]{:S(2)}, u32[]{:S(2)}) collective-permute-start(bf16[6336,128]{1,0:T(8,128)(2,1)S(1)} %shard_map.159), channel_id=1, source_target_pairs={{0,1},{1,0},{2,3},{3,2},{4,5},{5,4},{6,7},{7,6},{8,9},{9,8},{10,11... | collective-permute-start | bytes 4866056 | tf_op jit(solution)/shard_map/ppermute | solution.py:509
  118.9 6.7 %collective-permute-start.2 = (bf16[144,256]{1,0:T(8,128)(2,1)S(1)}, bf16[144,256]{1,0:T(8,128)(2,1)S(1)}, u32[]{:S(2)}, u32[]{:S(2)}) collective-permute-start(bf16[144,256]{1,0:T(8,128)(2,1)S(1)} %get-tuple-element.58), channel_id=1, source_target_pairs={{0,0},{1,32},{2,8},{3,40},{4,16},{5,48},{6,24},{7,56},{8,2},{9,34}... | collective-permute-start | bytes 221192 | tf_op jit(solution)/shard_map/ppermute | solution.py:418
  125.7 0.0 collective-permute-done.6.far_ref
  125.7 0.0 copy-start.2
  125.7 1.0 copy-done.2
  126.7 0.0 copy-start
  126.7 3.1 %shard_map.160 = (bf16[256,1152]{1,0:T(8,128)(2,1)}, bf16[384,1152]{1,0:T(8,128)(2,1)}, bf16[1152,768]{1,0:T(8,128)(2,1)}) custom-call(s32[2]{0:T(128)S(1)} %pad_add_fusion.place_ref, bf16[2304,128]{1,0:T(8,128)(2,1)S(1)} %bitcast.32, bf16[1296,128]{1,0:T(8,128)(2,1)S(1)} %copy-done.3, bf16[1872,128]{1,0:T(8,128)(2,1)S(1)} %collective-permute-done.3.part1, ...), custom_call_target="tpu_custom_call" | custom-call | flops 339738624 | bytes 3538944 | tf_op jit(solution)/shard_map/pallas_call | solution.py:510
  129.8 0.2 collective-permute-done.2.value_ref
  130.0 0.6 shard_map.161
  130.7 8.0 %all-to-all-done.2 = bf16[96,24,128]{2,1,0:T(8,128)(2,1)} async-done(((bf16[96,24,128]{2,1,0:T(8,128)(2,1)}), bf16[96,24,128]{2,1,0:T(8,128)(2,1)}, u32[]{:S(2)}, u32[]{:S(2)}) %all-to-all-start.2) | async-done | bytes 589856 | tf_op jit(solution)/shard_map/all_to_all | solution.py:423
  138.7 8.5 %all-to-all-start.3 = ((bf16[8,288,128]{2,1,0:T(8,128)(2,1)}), bf16[8,288,128]{2,1,0:T(8,128)(2,1)S(1)}, u32[]{:S(2)}, u32[]{:S(2)}) async-start(bf16[8,288,128]{2,1,0:T(8,128)(2,1)} %bitcast.14), calls=%async_computation.3 | async-start | bytes 1179648 | tf_op jit(solution)/shard_map/all_to_all | solution.py:525
  147.2 0.0 copy-done
  147.2 2.1 %shard_map.162 = bf16[144,384]{1,0:T(8,128)(2,1)S(1)} custom-call(bf16[2304,128]{1,0:T(8,128)(2,1)} %bitcast.11.rows_ref, bf16[384,2048]{1,0:T(8,128)(2,1)S(1)} %bitcast.34), custom_call_target="tpu_custom_call" | custom-call | flops 452984832 | bytes 1572864 | tf_op jit(solution)/shard_map/pallas_call | solution.py:528
  149.4 17.3 %all_gather.3.hidden_grad_ref = bf16[1152,384]{1,0:T(8,128)(2,1)S(1)} all-gather(bf16[144,384]{1,0:T(8,128)(2,1)S(1)} %shard_map.162), channel_id=1, replica_groups=mesh['z'=12,'y_high'=2,'y_low'=4,'x'=4,'core'=2] {'x','core'}, dimensions={0}, use_global_device_ids=true | all-gather | bytes 995328 | tf_op jit(solution)/shard_map/all_gather | solution.py:531
  166.6 0.0 all-to-all-done.3
  166.6 4.4 %shard_map.163 = (bf16[256,768]{1,0:T(8,128)(2,1)S(1)}, bf16[256,768]{1,0:T(8,128)(2,1)S(1)}, bf16[256,768]{1,0:T(8,128)(2,1)S(1)}, bf16[384,256]{1,0:T(8,128)(2...) custom-call(bf16[2304,128]{1,0:T(8,128)(2,1)S(1)} %bitcast.35, bf16[1152,384]{1,0:T(8,128)(2,1)S(1)} %all_gather.3.hidden_grad_ref, ...), custom_call_target="tpu_custom_call" | custom-call | flops 679477248 | bytes 1572864 | tf_op jit(solution)/shard_map/pallas_call | solution.py:534
  171.1 0.8 reshape.89
  171.9 0.8 reshape.90
  172.7 0.8 reshape.91
Async XLA Ops:
  0.6 34.9 %copy-start.7 = (bf16[144,256]{1,0:T(8,128)(2,1)S(1)}, bf16[144,256]{1,0:T(8,128)(2,1)}, u32[]{:S(2)}) copy-start(bf16[144,256]{1,0:T(8,128)(2,1)} %param.11) | copy-start | bytes 221188
  0.6 43.3 %copy-start.5 = (bf16[1,256,2,384]{3,2,1,0:T(2,128)(2,1)S(1)}, bf16[1,256,2,384]{3,2,1,0:T(2,128)(2,1)}, u32[]{:S(2)}) copy-start(bf16[1,256,2,384]{3,2,1,0:T(2,128)(2,1)} %param.15) | copy-start | bytes 1179652
  1.6 43.1 %copy-start.6 = (bf16[1,256,2,384]{3,2,1,0:T(2,128)(2,1)S(1)}, bf16[1,256,2,384]{3,2,1,0:T(2,128)(2,1)}, u32[]{:S(2)}) copy-start(bf16[1,256,2,384]{3,2,1,0:T(2,128)(2,1)} %param.16) | copy-start | bytes 1179652
  1.6 11.5 %collective-permute-start = (bf16[176,256]{1,0:T(8,128)(2,1)S(1)}, bf16[176,256]{1,0:T(8,128)(2,1)S(1)}, u32[]{:S(2)}, u32[]{:S(2)}) collective-permute-start(bf16[176,256]{1,0:T(8,128)(2,1)S(1)} %shard_map.153), channel_id=1, source_target_pairs={{0,0},{1,32},{2,8},{3,40},{4,16},{5,48},{6,24},{7,56},{8,2},{9,34}... | collective-permute-start | bytes 270344 | tf_op jit(solution)/shard_map/ppermute | solution.py:418
  15.0 46.0 %all-to-all-start = ((bf16[96,24,128]{2,1,0:T(8,128)(2,1)}), bf16[96,24,128]{2,1,0:T(8,128)(2,1)S(1)}, u32[]{:S(2)}, u32[]{:S(2)}) async-start(bf16[96,24,128]{2,1,0:T(8,128)(2,1)} %bitcast.2), calls=%async_computation | async-start | bytes 1179648 | tf_op jit(solution)/shard_map/all_to_all | solution.py:423
  35.5 17.6 %collective-permute-start.1 = (bf16[144,256]{1,0:T(8,128)(2,1)S(1)}, bf16[144,256]{1,0:T(8,128)(2,1)S(1)}, u32[]{:S(2)}, u32[]{:S(2)}) collective-permute-start(bf16[144,256]{1,0:T(8,128)(2,1)S(1)} %copy-done.7), channel_id=1, source_target_pairs={{0,0},{1,32},{2,8},{3,40},{4,16},{5,48},{6,24},{7,56},{8,2},{9,34}... | collective-permute-start | bytes 221192 | tf_op jit(solution)/shard_map/ppermute | solution.py:418
  65.7 9.1 %copy-start.4 = (f32[288,768]{1,0:T(8,128)S(1)}, f32[288,768]{1,0:T(8,128)}, u32[]{:S(2)}) copy-start(f32[288,768]{1,0:T(8,128)} %get-tuple-element.59.preacts_ref) | copy-start | bytes 2654212
  65.7 34.4 %all-to-all-start.1 = ((bf16[96,24,128]{2,1,0:T(8,128)(2,1)}), bf16[96,24,128]{2,1,0:T(8,128)(2,1)S(1)}, u32[]{:S(2)}, u32[]{:S(2)}) async-start(bf16[96,24,128]{2,1,0:T(8,128)(2,1)} %bitcast.43), calls=%async_computation.1 | async-start | bytes 1179648 | tf_op jit(solution)/shard_map/all_to_all | solution.py:423
  77.1 36.9 %collective-permute-start.3 = (bf16[1872,128]{1,0:T(8,128)(2,1)}, bf16[1872,128]{1,0:T(8,128)(2,1)S(1)}, u32[]{:S(2)}, u32[]{:S(2)}) collective-permute-start(bf16[1872,128]{1,0:T(8,128)(2,1)} %get-tuple-element.61), channel_id=1, source_target_pairs={{0,2},{2,4},{4,6},{6,0},{1,3},{3,5},{5,7},{7,1},{8,10},{10,12},{12... | collective-permute-start | bytes 1437704 | tf_op jit(solution)/shard_map/ppermute | solution.py:490
  81.0 33.0 %collective-permute-start.4 = (bf16[1872,128]{1,0:T(8,128)(2,1)}, bf16[1872,128]{1,0:T(8,128)(2,1)S(1)}, u32[]{:S(2)}, u32[]{:S(2)}) collective-permute-start(bf16[1872,128]{1,0:T(8,128)(2,1)} %get-tuple-element.62), channel_id=1, source_target_pairs={{0,4},{2,6},{4,0},{6,2},{1,5},{3,7},{5,1},{7,3},{8,12},{10,14},{12... | collective-permute-start | bytes 1437704 | tf_op jit(solution)/shard_map/ppermute | solution.py:490
  84.0 30.0 %collective-permute-start.5 = (bf16[1872,128]{1,0:T(8,128)(2,1)}, bf16[1872,128]{1,0:T(8,128)(2,1)S(1)}, u32[]{:S(2)}, u32[]{:S(2)}) collective-permute-start(bf16[1872,128]{1,0:T(8,128)(2,1)} %get-tuple-element.63), channel_id=1, source_target_pairs={{0,6},{2,0},{4,2},{6,4},{1,7},{3,1},{5,3},{7,5},{8,14},{10,8},{12,... | collective-permute-start | bytes 1437704 | tf_op jit(solution)/shard_map/ppermute | solution.py:490
  100.0 14.0 %copy-start.3 = (bf16[1296,128]{1,0:T(8,128)(2,1)S(1)}, bf16[1296,128]{1,0:T(8,128)(2,1)}, u32[]{:S(2)}) copy-start(bf16[1296,128]{1,0:T(8,128)(2,1)} %get-tuple-element.60.factors_ref.near_factors_ref) | copy-start | bytes 995332
  104.5 34.2 %all-to-all-start.2 = ((bf16[96,24,128]{2,1,0:T(8,128)(2,1)}), bf16[96,24,128]{2,1,0:T(8,128)(2,1)}, u32[]{:S(2)}, u32[]{:S(2)}) async-start(bf16[96,24,128]{2,1,0:T(8,128)(2,1)} %bitcast.42), calls=%async_computation.2 | async-start | bytes 1179648 | tf_op jit(solution)/shard_map/all_to_all | solution.py:423
  114.0 0.8 copy-start.1
  114.8 10.9 %collective-permute-start.6 = (bf16[6336,128]{1,0:T(8,128)(2,1)S(1)}, bf16[6336,128]{1,0:T(8,128)(2,1)S(1)}, u32[]{:S(2)}, u32[]{:S(2)}) collective-permute-start(bf16[6336,128]{1,0:T(8,128)(2,1)S(1)} %shard_map.159), channel_id=1, source_target_pairs={{0,1},{1,0},{2,3},{3,2},{4,5},{5,4},{6,7},{7,6},{8,9},{9,8},{10,11... | collective-permute-start | bytes 4866056 | tf_op jit(solution)/shard_map/ppermute | solution.py:509
  118.9 11.1 %collective-permute-start.2 = (bf16[144,256]{1,0:T(8,128)(2,1)S(1)}, bf16[144,256]{1,0:T(8,128)(2,1)S(1)}, u32[]{:S(2)}, u32[]{:S(2)}) collective-permute-start(bf16[144,256]{1,0:T(8,128)(2,1)S(1)} %get-tuple-element.58), channel_id=1, source_target_pairs={{0,0},{1,32},{2,8},{3,40},{4,16},{5,48},{6,24},{7,56},{8,2},{9,34}... | collective-permute-start | bytes 221192 | tf_op jit(solution)/shard_map/ppermute | solution.py:418
  125.7 1.0 copy-start.2
  126.7 20.5 %copy-start = (bf16[1,384,2048]{2,1,0:T(8,128)(2,1)S(1)}, bf16[1,384,2048]{2,1,0:T(8,128)(2,1)}, u32[]{:S(2)}) copy-start(bf16[1,384,2048]{2,1,0:T(8,128)(2,1)} %param.17) | copy-start | bytes 4718596
  138.7 27.9 %all-to-all-start.3 = ((bf16[8,288,128]{2,1,0:T(8,128)(2,1)}), bf16[8,288,128]{2,1,0:T(8,128)(2,1)S(1)}, u32[]{:S(2)}, u32[]{:S(2)}) async-start(bf16[8,288,128]{2,1,0:T(8,128)(2,1)} %bitcast.14), calls=%async_computation.3 | async-start | bytes 1179648 | tf_op jit(solution)/shard_map/all_to_all | solution.py:525

commit v6 on v5

--- a/solution.py
+++ b/solution.py
@@ -28,7 +28,7 @@
 FACTORS = 3 * LANES * CHUNK
 PART = 2 * GROUP + FACTORS
 FAR = GROUP + FACTORS
-LOADS = 4
+LOADS = 8
 
 beta_one = 0.9
 beta_two = 0.95
@@ -248,8 +248,12 @@
     grad_high, grad_low = split_pair(mixed.astype(F32) - target_ref[...].astype(F32))
     for copy in copies[2:]:
         copy.wait()
-    spread = dot(high_ref[...], grad_high) + dot(high_ref[...], grad_low) + dot(low_ref[...], grad_high)
-    send_ref[...] = pick_half(spread).astype(BF16)
+    for y in range(NY):
+        part = pl.ds(y * GROUP, GROUP)
+        high, low = high_ref[part, :], low_ref[part, :]
+        both = dot(high, jnp.concatenate([grad_high, grad_low], axis=1))
+        spread = both[:, :SLICE] + both[:, SLICE:] + dot(low, grad_high)
+        send_ref[part, :] = pick_half(spread).astype(BF16)
 
 
 def backward_kernel(rows_ref, w_out_ref, grad_ref, wide_ref):
@@ -312,7 +316,7 @@
     same = pl.multiple_of(core * GROUP, GROUP)
     for other in range(2):
         for shift, part_ref in enumerate((None, part1, part2, part3)):
-            source = 2 * lax.rem(x + (CHIPS - shift), CHIPS) + (1 - core if other else core)
+            source = lax.rem(x + (CHIPS - shift), CHIPS) + CHIPS * (1 - core if other else core)
             own = pl.ds(pl.multiple_of(source * CHUNK, CHUNK), CHUNK)
             if other:
                 rows_of, first_row, factors_of, offset = far_ref, shift * FAR, far_ref, shift * FAR + GROUP
@@ -336,12 +340,11 @@
     first_new = beta_one * moment_one.astype(F32) + (1.0 - beta_one) * gradient
     second_new = beta_two * moment_two.astype(F32) + (1.0 - beta_two) * gradient * gradient
     master = weight.astype(F32)
-    update = (
-        first_new / first_fix / (jnp.sqrt(second_new / second_fix) + adam_epsilon)
-        + decay_rate * master
-    )
+    scaled = second_new * (1.0 / second_fix)
+    root = scaled * lax.rsqrt(scaled) + adam_epsilon
+    step = first_new * (learn_rate / first_fix) * pl.reciprocal(root)
     return (
-        (master - learn_rate * update).astype(BF16),
+        (master * (1.0 - learn_rate * decay_rate) - step).astype(BF16),
         first_new.astype(BF16),
         second_new.astype(BF16),
     )
@@ -355,7 +358,8 @@
     masks = (compact_map(True), *half_masks())
     for source in range(NE):
         part = grads_ref[pl.ds(source * GROUP, GROUP), :]
-        own_ref[pl.ds(source * CHUNK, CHUNK), :] = narrow(part, *masks).astype(BF16)
+        place = source // 2 + CHIPS * (source % 2)
+        own_ref[pl.ds(place * CHUNK, CHUNK), :] = narrow(part, *masks).astype(BF16)
     for copy in copies[:4]:
         copy.wait()
     grad_down = dot(hidden_t_ref[...], own_ref[...])
@@ -528,7 +532,7 @@
     hidden_grad = call(
         backward_kernel, shape_of(CHUNK, FF), 2 * GROUP * WIDTH * FF, 2 * WIDTH * FF, 24, wide
     )(grads, w_down)
-    all_grads = lax.all_gather(hidden_grad, ("x", "core"), axis=0, tiled=True)
+    all_grads = lax.all_gather(hidden_grad, ("core", "x"), axis=0, tiled=True)
 
     operands = [hidden_t, *states[3:], slopes, rows_t, *states[:3]]
     updated = call(

time: 174 us -> 184 us (1.057)
  blocking collectives: 17.3 us -> 27.4 us
    all_gather x1, blocking collectives: 17.3 us -> 27.4 us  [shards(): all_grads = lax.all_gather(hidden_grad, ('core', 'x'), axis=0, tiled=True)]
  transfers between devices with their start and end apart: 11 -> 11, of which waited for: 5 -> 5; matrix products, arithmetic and copies ran while one was open for 5% -> 5% of each run, Pallas kernels for 10% -> 9%
where the time goes in v6:
time: 184 us; the launch traced here: 183 us
  starting transfers between devices  85.9 us (47%)
  Pallas kernels  28.5 us (15%)
  waiting for transfers between devices  27.7 us (15%)
  blocking collectives  27.4 us (15%)
  local copies, waits for them, and re-layouts  12.8 us (7%)
    all_to_all x3, starting transfers between devices, over_experts(): lax.all_to_all(messages, ('y_low', 'y_high', 'z'), split_axis=0, concat_a...  38.8 us
    all_gather x1, blocking collectives, shards(): all_grads = lax.all_gather(hidden_grad, ('core', 'x'), axis=0, tiled=True)  27.4 us
    all_to_all x3, waiting for transfers between devices, over_experts(): lax.all_to_all(messages, ('y_low', 'y_high', 'z'), split_axis=0, concat_a...  25 us
    ppermute x3, starting transfers between devices, change_places(): return lax.ppermute(value, ('z', 'y_high', 'y_low', 'x', 'core'), pairs)  24.1 us
    ppermute x3, starting transfers between devices, shards(): lax.ppermute(part, 'x', [(i, (i + shift) % CHIPS) for i in range(CHIPS)])  10.3 us
    all_to_all x1, starting transfers between devices, shards(): lax.all_to_all(grads.reshape(NE, GROUP, HALF), ('x', 'core'), split_axis=...  8.55 us
    unnamed x19, local copies, waits for them, and re-layouts  6.93 us
    pallas_call x1, Pallas kernels, shards(): call(forward_kernel, [in_hbm(ROWS, HALF), pltpu.HBM((GROUP, 2 * FF), F32)...  4.67 us
  transfers between devices with their start and end apart: 11, of which 5 were waited for; matrix products, arithmetic and copies ran while one was open for 5% of the time, Pallas kernels for 9%

profile of v6, /device:TPU:1, one launch (start us, length us, event | category | flops | bytes accessed | tf_op | source)
XLA Modules:
  0.0 183.4 jit_solution(18281620650603176821)
XLA Ops:
  0.6 0.0 copy-start.7
  0.6 0.0 copy-start.5
  0.7 1.0 shard_map.153
  1.6 0.0 copy-start.6
  1.6 9.0 %collective-permute-start = (bf16[176,256]{1,0:T(8,128)(2,1)S(1)}, bf16[176,256]{1,0:T(8,128)(2,1)S(1)}, u32[]{:S(2)}, u32[]{:S(2)}) collective-permute-start(bf16[176,256]{1,0:T(8,128)(2,1)S(1)} %shard_map.153), channel_id=1, source_target_pairs={{0,0},{1,32},{2,8},{3,40},{4,16},{5,48},{6,24},{7,56},{8,2},{9,34}... | collective-permute-start | bytes 270344 | tf_op jit(solution)/shard_map/ppermute | solution.py:422
  10.6 2.5 %collective-permute-done.packed_ref = bf16[176,256]{1,0:T(8,128)(2,1)S(1)} collective-permute-done((bf16[176,256]{1,0:T(8,128)(2,1)S(1)}, bf16[176,256]{1,0:T(8,128)(2,1)S(1)}, u32[]{:S(2)}, u32[]{:S(2)}) %collective-permute-start) | collective-permute-done | bytes 90144 | tf_op jit(solution)/shard_map/ppermute | solution.py:422
  13.1 1.9 %shard_map.154 = bf16[2304,128]{1,0:T(8,128)(2,1)} custom-call(bf16[176,256]{1,0:T(8,128)(2,1)S(1)} %collective-permute-done.packed_ref), custom_call_target="tpu_custom_call" | custom-call | flops 509607936 | bytes 589824 | tf_op jit(solution)/shard_map/pallas_call | solution.py:442
  15.0 20.5 %all-to-all-start = ((bf16[96,24,128]{2,1,0:T(8,128)(2,1)}), bf16[96,24,128]{2,1,0:T(8,128)(2,1)S(1)}, u32[]{:S(2)}, u32[]{:S(2)}) async-start(bf16[96,24,128]{2,1,0:T(8,128)(2,1)} %bitcast.2), calls=%async_computation | async-start | bytes 1179648 | tf_op jit(solution)/shard_map/all_to_all | solution.py:427
  35.5 0.0 copy-done.7
  35.5 8.4 %collective-permute-start.1 = (bf16[144,256]{1,0:T(8,128)(2,1)S(1)}, bf16[144,256]{1,0:T(8,128)(2,1)S(1)}, u32[]{:S(2)}, u32[]{:S(2)}) collective-permute-start(bf16[144,256]{1,0:T(8,128)(2,1)S(1)} %copy-done.7), channel_id=1, source_target_pairs={{0,0},{1,32},{2,8},{3,40},{4,16},{5,48},{6,24},{7,56},{8,2},{9,34}... | collective-permute-start | bytes 221192 | tf_op jit(solution)/shard_map/ppermute | solution.py:422
  44.0 0.0 copy-done.5
  44.0 0.8 copy.18
  44.8 0.0 copy-done.6
  44.8 0.8 copy.19
  45.6 4.2 %copy.17 = bf16[256,8,2,384]{3,1,2,0:T(8,128)(2,1)} copy(bf16[256,8,2,384]{3,2,1,0:T(2,128)(2,1)} %bitcast.39) | data formatting | bytes 6291456
  49.7 1.8 constant_dynamic-slice_fusion.refs_6_
  51.5 1.6 dynamic-slice_bitcast_fusion.refs_1_
  53.1 0.0 collective-permute-done.1.target_ref
  53.1 7.8 %all-to-all-done = bf16[96,24,128]{2,1,0:T(8,128)(2,1)S(1)} async-done(((bf16[96,24,128]{2,1,0:T(8,128)(2,1)}), bf16[96,24,128]{2,1,0:T(8,128)(2,1)S(1)}, u32[]{:S(2)}, u32[]{:S(2)}) %all-to-all-start) | async-done | bytes 589856 | tf_op jit(solution)/shard_map/all_to_all | solution.py:427
  61.0 4.7 %shard_map.155 = (bf16[2304,128]{1,0:T(8,128)(2,1)}, f32[288,768]{1,0:T(8,128)}) custom-call(bf16[2304,128]{1,0:T(8,128)(2,1)S(1)} %bitcast.29, bf16[2048,768]{1,0:T(8,128)(2,1)} %bitcast.38, bf16[384,2048]{1,0:T(8,128)(2,1)} %bitcast.33), custom_call_target="tpu_custom_call" | custom-call | flops 1358954496 | bytes 4718592 | tf_op jit(solution)/shard_map/pallas_call | solution.py:457
  65.7 0.0 copy-start.4
  65.7 9.0 %all-to-all-start.1 = ((bf16[96,24,128]{2,1,0:T(8,128)(2,1)}), bf16[96,24,128]{2,1,0:T(8,128)(2,1)S(1)}, u32[]{:S(2)}, u32[]{:S(2)}) async-start(bf16[96,24,128]{2,1,0:T(8,128)(2,1)} %bitcast.43), calls=%async_computation.1 | async-start | bytes 1179648 | tf_op jit(solution)/shard_map/all_to_all | solution.py:427
  74.7 0.1 pad_add_fusion.place_ref
  74.8 0.0 copy-done.4
  74.8 2.3 %shard_map.158 = (bf16[1296,128]{1,0:T(8,128)(2,1)}, bf16[1872,128]{1,0:T(8,128)(2,1)}, bf16[1872,128]{1,0:T(8,128)(2,1)}, bf16[1872,128]{1,0:T(8,128)(2,1)}) custom-call(s32[2]{0:T(128)S(1)} %pad_add_fusion.place_ref, bf16[2304,128]{1,0:T(8,128)(2,1)S(1)} %bitcast.30, f32[288,768]{1,0:T(8,128)S(1)} %copy-done.4), custom_call_target="tpu_custom_call" | custom-call | bytes 958464 | tf_op jit(solution)/shard_map/pallas_call | solution.py:484
  77.1 3.9 %collective-permute-start.3 = (bf16[1872,128]{1,0:T(8,128)(2,1)}, bf16[1872,128]{1,0:T(8,128)(2,1)S(1)}, u32[]{:S(2)}, u32[]{:S(2)}) collective-permute-start(bf16[1872,128]{1,0:T(8,128)(2,1)} %get-tuple-element.61), channel_id=1, source_target_pairs={{0,2},{2,4},{4,6},{6,0},{1,3},{3,5},{5,7},{7,1},{8,10},{10,12},{12... | collective-permute-start | bytes 1437704 | tf_op jit(solution)/shard_map/ppermute | solution.py:494
  81.0 3.0 %collective-permute-start.4 = (bf16[1872,128]{1,0:T(8,128)(2,1)}, bf16[1872,128]{1,0:T(8,128)(2,1)S(1)}, u32[]{:S(2)}, u32[]{:S(2)}) collective-permute-start(bf16[1872,128]{1,0:T(8,128)(2,1)} %get-tuple-element.62), channel_id=1, source_target_pairs={{0,4},{2,6},{4,0},{6,2},{1,5},{3,7},{5,1},{7,3},{8,12},{10,14},{12... | collective-permute-start | bytes 1437704 | tf_op jit(solution)/shard_map/ppermute | solution.py:494
  84.0 3.4 %collective-permute-start.5 = (bf16[1872,128]{1,0:T(8,128)(2,1)}, bf16[1872,128]{1,0:T(8,128)(2,1)S(1)}, u32[]{:S(2)}, u32[]{:S(2)}) collective-permute-start(bf16[1872,128]{1,0:T(8,128)(2,1)} %get-tuple-element.63), channel_id=1, source_target_pairs={{0,6},{2,0},{4,2},{6,4},{1,7},{3,1},{5,3},{7,5},{8,14},{10,8},{12,... | collective-permute-start | bytes 1437704 | tf_op jit(solution)/shard_map/ppermute | solution.py:494
  87.5 3.4 %shard_map.156 = (bf16[144,2304]{1,0:T(8,128)(2,1)}, bf16[144,2304]{1,0:T(8,128)(2,1)}, bf16[2304,144]{1,0:T(8,128)(2,1)}, bf16[2304,144]{1,0:T(8,128)(2,1)}) custom-call(bf16[176,256]{1,0:T(8,128)(2,1)S(1)} %collective-permute-done.packed_ref), custom_call_target="tpu_custom_call" | custom-call | flops 679477248 | bytes 2654208 | tf_op jit(solution)/shard_map/pallas_call | solution.py:474
  90.9 9.2 %all-to-all-done.1 = bf16[96,24,128]{2,1,0:T(8,128)(2,1)S(1)} async-done(((bf16[96,24,128]{2,1,0:T(8,128)(2,1)}), bf16[96,24,128]{2,1,0:T(8,128)(2,1)S(1)}, u32[]{:S(2)}, u32[]{:S(2)}) %all-to-all-start.1) | async-done | bytes 589856 | tf_op jit(solution)/shard_map/all_to_all | solution.py:427
  100.0 0.0 copy-start.3
  100.0 4.5 %shard_map.157 = (bf16[144,256]{1,0:T(8,128)(2,1)S(1)}, bf16[2304,128]{1,0:T(8,128)(2,1)}) custom-call(bf16[2304,128]{1,0:T(8,128)(2,1)S(1)} %bitcast.36, bf16[144,256]{1,0:T(8,128)(2,1)S(1)} %collective-permute-done.1.target_ref, bf16[144,2304]{1,0:T(8,128)(2,1)} %get-tuple-element.53.refs_0_, bf16[144,2304]{1,0:T(8,128)(2,1)} %get-tuple-element.54.refs_1_, ...), custom_call_target="tpu_custom_call" | custom-call | flops 1019215872 | bytes 2654208 | tf_op jit(solution)/shard_map/pallas_call | solution.py:498
  104.5 9.3 %all-to-all-start.2 = ((bf16[96,24,128]{2,1,0:T(8,128)(2,1)}), bf16[96,24,128]{2,1,0:T(8,128)(2,1)}, u32[]{:S(2)}, u32[]{:S(2)}) async-start(bf16[96,24,128]{2,1,0:T(8,128)(2,1)} %bitcast.42), calls=%async_computation.2 | async-start | bytes 1179648 | tf_op jit(solution)/shard_map/all_to_all | solution.py:427
  113.8 0.0 collective-permute-done.3.part1
  113.8 0.0 collective-permute-done.4.part2
  113.8 0.0 collective-permute-done.5.part3
  113.8 0.0 copy-start.1
  113.8 0.0 copy-done.3
  113.8 0.6 shard_map.159
  114.5 0.1 copy-done.1
  114.6 4.1 %collective-permute-start.6 = (bf16[6336,128]{1,0:T(8,128)(2,1)S(1)}, bf16[6336,128]{1,0:T(8,128)(2,1)S(1)}, u32[]{:S(2)}, u32[]{:S(2)}) collective-permute-start(bf16[6336,128]{1,0:T(8,128)(2,1)S(1)} %shard_map.159), channel_id=1, source_target_pairs={{0,1},{1,0},{2,3},{3,2},{4,5},{5,4},{6,7},{7,6},{8,9},{9,8},{10,11... | collective-permute-start | bytes 4866056 | tf_op jit(solution)/shard_map/ppermute | solution.py:513
  118.7 6.7 %collective-permute-start.2 = (bf16[144,256]{1,0:T(8,128)(2,1)S(1)}, bf16[144,256]{1,0:T(8,128)(2,1)S(1)}, u32[]{:S(2)}, u32[]{:S(2)}) collective-permute-start(bf16[144,256]{1,0:T(8,128)(2,1)S(1)} %get-tuple-element.58), channel_id=1, source_target_pairs={{0,0},{1,32},{2,8},{3,40},{4,16},{5,48},{6,24},{7,56},{8,2},{9,34}... | collective-permute-start | bytes 221192 | tf_op jit(solution)/shard_map/ppermute | solution.py:422
  125.5 0.0 collective-permute-done.6.far_ref
  125.5 0.0 copy-start.2
  125.5 1.0 copy-done.2
  126.5 0.0 copy-start
  126.5 3.2 %shard_map.160 = (bf16[256,1152]{1,0:T(8,128)(2,1)}, bf16[384,1152]{1,0:T(8,128)(2,1)}, bf16[1152,768]{1,0:T(8,128)(2,1)}) custom-call(s32[2]{0:T(128)S(1)} %pad_add_fusion.place_ref, bf16[2304,128]{1,0:T(8,128)(2,1)S(1)} %bitcast.32, bf16[1296,128]{1,0:T(8,128)(2,1)S(1)} %copy-done.3, bf16[1872,128]{1,0:T(8,128)(2,1)S(1)} %collective-permute-done.3.part1, ...), custom_call_target="tpu_custom_call" | custom-call | flops 339738624 | bytes 3538944 | tf_op jit(solution)/shard_map/pallas_call | solution.py:514
  129.7 0.1 collective-permute-done.2.value_ref
  129.8 0.6 shard_map.161
  130.5 8.0 %all-to-all-done.2 = bf16[96,24,128]{2,1,0:T(8,128)(2,1)} async-done(((bf16[96,24,128]{2,1,0:T(8,128)(2,1)}), bf16[96,24,128]{2,1,0:T(8,128)(2,1)}, u32[]{:S(2)}, u32[]{:S(2)}) %all-to-all-start.2) | async-done | bytes 589856 | tf_op jit(solution)/shard_map/all_to_all | solution.py:427
  138.5 8.6 %all-to-all-start.3 = ((bf16[8,288,128]{2,1,0:T(8,128)(2,1)}), bf16[8,288,128]{2,1,0:T(8,128)(2,1)S(1)}, u32[]{:S(2)}, u32[]{:S(2)}) async-start(bf16[8,288,128]{2,1,0:T(8,128)(2,1)} %bitcast.14), calls=%async_computation.3 | async-start | bytes 1179648 | tf_op jit(solution)/shard_map/all_to_all | solution.py:529
  147.0 0.0 copy-done
  147.0 2.1 %shard_map.162 = bf16[144,384]{1,0:T(8,128)(2,1)S(1)} custom-call(bf16[2304,128]{1,0:T(8,128)(2,1)} %bitcast.11.rows_ref, bf16[384,2048]{1,0:T(8,128)(2,1)S(1)} %bitcast.34), custom_call_target="tpu_custom_call" | custom-call | flops 452984832 | bytes 1572864 | tf_op jit(solution)/shard_map/pallas_call | solution.py:532
  149.2 27.4 %all_gather.3.hidden_grad_ref = bf16[1152,384]{1,0:T(8,128)(2,1)S(1)} all-gather(bf16[144,384]{1,0:T(8,128)(2,1)S(1)} %shard_map.162), channel_id=1, replica_groups=mesh['z'=12,'y_high'=2,'y_low'=4,'x'=4,'core'=2] {'core','x'}, dimensions={0}, use_global_device_ids=true | all-gather | bytes 995328 | tf_op jit(solution)/shard_map/all_gather | solution.py:535
  176.6 0.0 all-to-all-done.3
  176.6 4.2 %shard_map.163 = (bf16[256,768]{1,0:T(8,128)(2,1)S(1)}, bf16[256,768]{1,0:T(8,128)(2,1)S(1)}, bf16[256,768]{1,0:T(8,128)(2,1)S(1)}, bf16[384,256]{1,0:T(8,128)(2...) custom-call(bf16[2304,128]{1,0:T(8,128)(2,1)S(1)} %bitcast.35, bf16[1152,384]{1,0:T(8,128)(2,1)S(1)} %all_gather.3.hidden_grad_ref, ...), custom_call_target="tpu_custom_call" | custom-call | flops 679477248 | bytes 1572864 | tf_op jit(solution)/shard_map/pallas_call | solution.py:538
  180.9 0.8 reshape.89
  181.7 0.8 reshape.90
  182.5 0.8 reshape.91
Async XLA Ops:
  0.6 34.9 %copy-start.7 = (bf16[144,256]{1,0:T(8,128)(2,1)S(1)}, bf16[144,256]{1,0:T(8,128)(2,1)}, u32[]{:S(2)}) copy-start(bf16[144,256]{1,0:T(8,128)(2,1)} %param.11) | copy-start | bytes 221188
  0.6 43.3 %copy-start.5 = (bf16[1,256,2,384]{3,2,1,0:T(2,128)(2,1)S(1)}, bf16[1,256,2,384]{3,2,1,0:T(2,128)(2,1)}, u32[]{:S(2)}) copy-start(bf16[1,256,2,384]{3,2,1,0:T(2,128)(2,1)} %param.15) | copy-start | bytes 1179652
  1.6 43.1 %copy-start.6 = (bf16[1,256,2,384]{3,2,1,0:T(2,128)(2,1)S(1)}, bf16[1,256,2,384]{3,2,1,0:T(2,128)(2,1)}, u32[]{:S(2)}) copy-start(bf16[1,256,2,384]{3,2,1,0:T(2,128)(2,1)} %param.16) | copy-start | bytes 1179652
  1.6 11.5 %collective-permute-start = (bf16[176,256]{1,0:T(8,128)(2,1)S(1)}, bf16[176,256]{1,0:T(8,128)(2,1)S(1)}, u32[]{:S(2)}, u32[]{:S(2)}) collective-permute-start(bf16[176,256]{1,0:T(8,128)(2,1)S(1)} %shard_map.153), channel_id=1, source_target_pairs={{0,0},{1,32},{2,8},{3,40},{4,16},{5,48},{6,24},{7,56},{8,2},{9,34}... | collective-permute-start | bytes 270344 | tf_op jit(solution)/shard_map/ppermute | solution.py:422
  15.0 46.0 %all-to-all-start = ((bf16[96,24,128]{2,1,0:T(8,128)(2,1)}), bf16[96,24,128]{2,1,0:T(8,128)(2,1)S(1)}, u32[]{:S(2)}, u32[]{:S(2)}) async-start(bf16[96,24,128]{2,1,0:T(8,128)(2,1)} %bitcast.2), calls=%async_computation | async-start | bytes 1179648 | tf_op jit(solution)/shard_map/all_to_all | solution.py:427
  35.5 17.6 %collective-permute-start.1 = (bf16[144,256]{1,0:T(8,128)(2,1)S(1)}, bf16[144,256]{1,0:T(8,128)(2,1)S(1)}, u32[]{:S(2)}, u32[]{:S(2)}) collective-permute-start(bf16[144,256]{1,0:T(8,128)(2,1)S(1)} %copy-done.7), channel_id=1, source_target_pairs={{0,0},{1,32},{2,8},{3,40},{4,16},{5,48},{6,24},{7,56},{8,2},{9,34}... | collective-permute-start | bytes 221192 | tf_op jit(solution)/shard_map/ppermute | solution.py:422
  65.7 9.1 %copy-start.4 = (f32[288,768]{1,0:T(8,128)S(1)}, f32[288,768]{1,0:T(8,128)}, u32[]{:S(2)}) copy-start(f32[288,768]{1,0:T(8,128)} %get-tuple-element.59.preacts_ref) | copy-start | bytes 2654212
  65.7 34.4 %all-to-all-start.1 = ((bf16[96,24,128]{2,1,0:T(8,128)(2,1)}), bf16[96,24,128]{2,1,0:T(8,128)(2,1)S(1)}, u32[]{:S(2)}, u32[]{:S(2)}) async-start(bf16[96,24,128]{2,1,0:T(8,128)(2,1)} %bitcast.43), calls=%async_computation.1 | async-start | bytes 1179648 | tf_op jit(solution)/shard_map/all_to_all | solution.py:427
  77.1 36.7 %collective-permute-start.3 = (bf16[1872,128]{1,0:T(8,128)(2,1)}, bf16[1872,128]{1,0:T(8,128)(2,1)S(1)}, u32[]{:S(2)}, u32[]{:S(2)}) collective-permute-start(bf16[1872,128]{1,0:T(8,128)(2,1)} %get-tuple-element.61), channel_id=1, source_target_pairs={{0,2},{2,4},{4,6},{6,0},{1,3},{3,5},{5,7},{7,1},{8,10},{10,12},{12... | collective-permute-start | bytes 1437704 | tf_op jit(solution)/shard_map/ppermute | solution.py:494
  81.0 32.8 %collective-permute-start.4 = (bf16[1872,128]{1,0:T(8,128)(2,1)}, bf16[1872,128]{1,0:T(8,128)(2,1)S(1)}, u32[]{:S(2)}, u32[]{:S(2)}) collective-permute-start(bf16[1872,128]{1,0:T(8,128)(2,1)} %get-tuple-element.62), channel_id=1, source_target_pairs={{0,4},{2,6},{4,0},{6,2},{1,5},{3,7},{5,1},{7,3},{8,12},{10,14},{12... | collective-permute-start | bytes 1437704 | tf_op jit(solution)/shard_map/ppermute | solution.py:494
  84.0 29.8 %collective-permute-start.5 = (bf16[1872,128]{1,0:T(8,128)(2,1)}, bf16[1872,128]{1,0:T(8,128)(2,1)S(1)}, u32[]{:S(2)}, u32[]{:S(2)}) collective-permute-start(bf16[1872,128]{1,0:T(8,128)(2,1)} %get-tuple-element.63), channel_id=1, source_target_pairs={{0,6},{2,0},{4,2},{6,4},{1,7},{3,1},{5,3},{7,5},{8,14},{10,8},{12,... | collective-permute-start | bytes 1437704 | tf_op jit(solution)/shard_map/ppermute | solution.py:494
  100.0 13.8 %copy-start.3 = (bf16[1296,128]{1,0:T(8,128)(2,1)S(1)}, bf16[1296,128]{1,0:T(8,128)(2,1)}, u32[]{:S(2)}) copy-start(bf16[1296,128]{1,0:T(8,128)(2,1)} %get-tuple-element.60.factors_ref.near_factors_ref) | copy-start | bytes 995332
  104.5 34.0 %all-to-all-start.2 = ((bf16[96,24,128]{2,1,0:T(8,128)(2,1)}), bf16[96,24,128]{2,1,0:T(8,128)(2,1)}, u32[]{:S(2)}, u32[]{:S(2)}) async-start(bf16[96,24,128]{2,1,0:T(8,128)(2,1)} %bitcast.42), calls=%async_computation.2 | async-start | bytes 1179648 | tf_op jit(solution)/shard_map/all_to_all | solution.py:427
  113.8 0.8 copy-start.1
  114.6 10.9 %collective-permute-start.6 = (bf16[6336,128]{1,0:T(8,128)(2,1)S(1)}, bf16[6336,128]{1,0:T(8,128)(2,1)S(1)}, u32[]{:S(2)}, u32[]{:S(2)}) collective-permute-start(bf16[6336,128]{1,0:T(8,128)(2,1)S(1)} %shard_map.159), channel_id=1, source_target_pairs={{0,1},{1,0},{2,3},{3,2},{4,5},{5,4},{6,7},{7,6},{8,9},{9,8},{10,11... | collective-permute-start | bytes 4866056 | tf_op jit(solution)/shard_map/ppermute | solution.py:513
  118.7 11.1 %collective-permute-start.2 = (bf16[144,256]{1,0:T(8,128)(2,1)S(1)}, bf16[144,256]{1,0:T(8,128)(2,1)S(1)}, u32[]{:S(2)}, u32[]{:S(2)}) collective-permute-start(bf16[144,256]{1,0:T(8,128)(2,1)S(1)} %get-tuple-element.58), channel_id=1, source_target_pairs={{0,0},{1,32},{2,8},{3,40},{4,16},{5,48},{6,24},{7,56},{8,2},{9,34}... | collective-permute-start | bytes 221192 | tf_op jit(solution)/shard_map/ppermute | solution.py:422
  125.5 1.0 copy-start.2
  126.5 20.5 %copy-start = (bf16[1,384,2048]{2,1,0:T(8,128)(2,1)S(1)}, bf16[1,384,2048]{2,1,0:T(8,128)(2,1)}, u32[]{:S(2)}) copy-start(bf16[1,384,2048]{2,1,0:T(8,128)(2,1)} %param.17) | copy-start | bytes 4718596
  138.5 38.1 %all-to-all-start.3 = ((bf16[8,288,128]{2,1,0:T(8,128)(2,1)}), bf16[8,288,128]{2,1,0:T(8,128)(2,1)S(1)}, u32[]{:S(2)}, u32[]{:S(2)}) async-start(bf16[8,288,128]{2,1,0:T(8,128)(2,1)} %bitcast.14), calls=%async_computation.3 | async-start | bytes 1179648 | tf_op jit(solution)/shard_map/all_to_all | solution.py:529

commit v7 on v6

--- a/solution.py
+++ b/solution.py
@@ -316,7 +316,7 @@
     same = pl.multiple_of(core * GROUP, GROUP)
     for other in range(2):
         for shift, part_ref in enumerate((None, part1, part2, part3)):
-            source = lax.rem(x + (CHIPS - shift), CHIPS) + CHIPS * (1 - core if other else core)
+            source = 2 * lax.rem(x + (CHIPS - shift), CHIPS) + (1 - core if other else core)
             own = pl.ds(pl.multiple_of(source * CHUNK, CHUNK), CHUNK)
             if other:
                 rows_of, first_row, factors_of, offset = far_ref, shift * FAR, far_ref, shift * FAR + GROUP
@@ -358,8 +358,7 @@
     masks = (compact_map(True), *half_masks())
     for source in range(NE):
         part = grads_ref[pl.ds(source * GROUP, GROUP), :]
-        place = source // 2 + CHIPS * (source % 2)
-        own_ref[pl.ds(place * CHUNK, CHUNK), :] = narrow(part, *masks).astype(BF16)
+        own_ref[pl.ds(source * CHUNK, CHUNK), :] = narrow(part, *masks).astype(BF16)
     for copy in copies[:4]:
         copy.wait()
     grad_down = dot(hidden_t_ref[...], own_ref[...])
@@ -532,7 +531,7 @@
     hidden_grad = call(
         backward_kernel, shape_of(CHUNK, FF), 2 * GROUP * WIDTH * FF, 2 * WIDTH * FF, 24, wide
     )(grads, w_down)
-    all_grads = lax.all_gather(hidden_grad, ("core", "x"), axis=0, tiled=True)
+    all_grads = lax.all_gather(hidden_grad, ("x", "core"), axis=0, tiled=True)
 
     operands = [hidden_t, *states[3:], slopes, rows_t, *states[:3]]
     updated = call(

time: 184 us -> 174 us (0.946)
  blocking collectives: 27.4 us -> 17.3 us
    all_gather x1, blocking collectives: 27.4 us -> 17.3 us  [shards(): all_grads = lax.all_gather(hidden_grad, ('x', 'core'), axis=0, tiled=True)]
  transfers between devices with their start and end apart: 11 -> 11, of which waited for: 5 -> 5; matrix products, arithmetic and copies ran while one was open for 5% -> 5% of each run, Pallas kernels for 9% -> 10%
where the time goes in v7:
time: 174 us; the launch traced here: 173 us
  starting transfers between devices  85.9 us (49%)
  Pallas kernels  28.5 us (16%)
  waiting for transfers between devices  27.7 us (16%)
  blocking collectives  17.3 us (10%)
  local copies, waits for them, and re-layouts  12.8 us (7%)
    all_to_all x3, starting transfers between devices, over_experts(): lax.all_to_all(messages, ('y_low', 'y_high', 'z'), split_axis=0, concat_a...  38.8 us
    all_to_all x3, waiting for transfers between devices, over_experts(): lax.all_to_all(messages, ('y_low', 'y_high', 'z'), split_axis=0, concat_a...  25 us
    ppermute x3, starting transfers between devices, change_places(): return lax.ppermute(value, ('z', 'y_high', 'y_low', 'x', 'core'), pairs)  24.1 us
    all_gather x1, blocking collectives, shards(): all_grads = lax.all_gather(hidden_grad, ('x', 'core'), axis=0, tiled=True)  17.3 us
    ppermute x3, starting transfers between devices, shards(): lax.ppermute(part, 'x', [(i, (i + shift) % CHIPS) for i in range(CHIPS)])  10.3 us
    all_to_all x1, starting transfers between devices, shards(): lax.all_to_all(grads.reshape(NE, GROUP, HALF), ('x', 'core'), split_axis=...  8.55 us
    unnamed x19, local copies, waits for them, and re-layouts  6.93 us
    pallas_call x1, Pallas kernels, shards(): call(forward_kernel, [in_hbm(ROWS, HALF), pltpu.HBM((GROUP, 2 * FF), F32)...  4.67 us
  transfers between devices with their start and end apart: 11, of which 5 were waited for; matrix products, arithmetic and copies ran while one was open for 5% of the time, Pallas kernels for 10%

profile of v7, /device:TPU:1, one launch (start us, length us, event | category | flops | bytes accessed | tf_op | source)
XLA Modules:
  0.0 173.2 jit_solution(5290981600809469372)
XLA Ops:
  0.6 0.0 copy-start.7
  0.6 0.0 copy-start.5
  0.7 1.0 shard_map.153
  1.6 0.0 copy-start.6
  1.6 9.0 %collective-permute-start = (bf16[176,256]{1,0:T(8,128)(2,1)S(1)}, bf16[176,256]{1,0:T(8,128)(2,1)S(1)}, u32[]{:S(2)}, u32[]{:S(2)}) collective-permute-start(bf16[176,256]{1,0:T(8,128)(2,1)S(1)} %shard_map.153), channel_id=1, source_target_pairs={{0,0},{1,32},{2,8},{3,40},{4,16},{5,48},{6,24},{7,56},{8,2},{9,34}... | collective-permute-start | bytes 270344 | tf_op jit(solution)/shard_map/ppermute | solution.py:421
  10.6 2.5 %collective-permute-done.packed_ref = bf16[176,256]{1,0:T(8,128)(2,1)S(1)} collective-permute-done((bf16[176,256]{1,0:T(8,128)(2,1)S(1)}, bf16[176,256]{1,0:T(8,128)(2,1)S(1)}, u32[]{:S(2)}, u32[]{:S(2)}) %collective-permute-start) | collective-permute-done | bytes 90144 | tf_op jit(solution)/shard_map/ppermute | solution.py:421
  13.1 1.9 %shard_map.154 = bf16[2304,128]{1,0:T(8,128)(2,1)} custom-call(bf16[176,256]{1,0:T(8,128)(2,1)S(1)} %collective-permute-done.packed_ref), custom_call_target="tpu_custom_call" | custom-call | flops 509607936 | bytes 589824 | tf_op jit(solution)/shard_map/pallas_call | solution.py:441
  15.0 20.5 %all-to-all-start = ((bf16[96,24,128]{2,1,0:T(8,128)(2,1)}), bf16[96,24,128]{2,1,0:T(8,128)(2,1)S(1)}, u32[]{:S(2)}, u32[]{:S(2)}) async-start(bf16[96,24,128]{2,1,0:T(8,128)(2,1)} %bitcast.2), calls=%async_computation | async-start | bytes 1179648 | tf_op jit(solution)/shard_map/all_to_all | solution.py:426
  35.5 0.0 copy-done.7
  35.5 8.4 %collective-permute-start.1 = (bf16[144,256]{1,0:T(8,128)(2,1)S(1)}, bf16[144,256]{1,0:T(8,128)(2,1)S(1)}, u32[]{:S(2)}, u32[]{:S(2)}) collective-permute-start(bf16[144,256]{1,0:T(8,128)(2,1)S(1)} %copy-done.7), channel_id=1, source_target_pairs={{0,0},{1,32},{2,8},{3,40},{4,16},{5,48},{6,24},{7,56},{8,2},{9,34}... | collective-permute-start | bytes 221192 | tf_op jit(solution)/shard_map/ppermute | solution.py:421
  44.0 0.0 copy-done.5
  44.0 0.8 copy.18
  44.8 0.0 copy-done.6
  44.8 0.8 copy.19
  45.6 4.2 %copy.17 = bf16[256,8,2,384]{3,1,2,0:T(8,128)(2,1)} copy(bf16[256,8,2,384]{3,2,1,0:T(2,128)(2,1)} %bitcast.39) | data formatting | bytes 6291456
  49.7 1.8 %constant_dynamic-slice_fusion.refs_6_ = bf16[256,768]{1,0:T(8,128)(2,1)} fusion(bf16[2048,768]{1,0:T(8,128)(2,1)} %bitcast.37, s32[]{:T(128)S(6)} %select_n.4), kind=kLoop, calls=%fused_computation.2 | loop fusion | bytes 786436 | tf_op jit(solution)/shard_map/dynamic_slice | solution.py:448
  51.5 1.6 dynamic-slice_bitcast_fusion.refs_1_
  53.1 0.0 collective-permute-done.1.target_ref
  53.1 7.8 %all-to-all-done = bf16[96,24,128]{2,1,0:T(8,128)(2,1)S(1)} async-done(((bf16[96,24,128]{2,1,0:T(8,128)(2,1)}), bf16[96,24,128]{2,1,0:T(8,128)(2,1)S(1)}, u32[]{:S(2)}, u32[]{:S(2)}) %all-to-all-start) | async-done | bytes 589856 | tf_op jit(solution)/shard_map/all_to_all | solution.py:426
  61.0 4.7 %shard_map.155 = (bf16[2304,128]{1,0:T(8,128)(2,1)}, f32[288,768]{1,0:T(8,128)}) custom-call(bf16[2304,128]{1,0:T(8,128)(2,1)S(1)} %bitcast.29, bf16[2048,768]{1,0:T(8,128)(2,1)} %bitcast.38, bf16[384,2048]{1,0:T(8,128)(2,1)} %bitcast.33), custom_call_target="tpu_custom_call" | custom-call | flops 1358954496 | bytes 4718592 | tf_op jit(solution)/shard_map/pallas_call | solution.py:456
  65.7 0.0 copy-start.4
  65.7 9.0 %all-to-all-start.1 = ((bf16[96,24,128]{2,1,0:T(8,128)(2,1)}), bf16[96,24,128]{2,1,0:T(8,128)(2,1)S(1)}, u32[]{:S(2)}, u32[]{:S(2)}) async-start(bf16[96,24,128]{2,1,0:T(8,128)(2,1)} %bitcast.43), calls=%async_computation.1 | async-start | bytes 1179648 | tf_op jit(solution)/shard_map/all_to_all | solution.py:426
  74.7 0.1 pad_add_fusion.place_ref
  74.8 0.0 copy-done.4
  74.8 2.3 %shard_map.158 = (bf16[1296,128]{1,0:T(8,128)(2,1)}, bf16[1872,128]{1,0:T(8,128)(2,1)}, bf16[1872,128]{1,0:T(8,128)(2,1)}, bf16[1872,128]{1,0:T(8,128)(2,1)}) custom-call(s32[2]{0:T(128)S(1)} %pad_add_fusion.place_ref, bf16[2304,128]{1,0:T(8,128)(2,1)S(1)} %bitcast.30, f32[288,768]{1,0:T(8,128)S(1)} %copy-done.4), custom_call_target="tpu_custom_call" | custom-call | bytes 958464 | tf_op jit(solution)/shard_map/pallas_call | solution.py:483
  77.1 3.9 %collective-permute-start.3 = (bf16[1872,128]{1,0:T(8,128)(2,1)}, bf16[1872,128]{1,0:T(8,128)(2,1)S(1)}, u32[]{:S(2)}, u32[]{:S(2)}) collective-permute-start(bf16[1872,128]{1,0:T(8,128)(2,1)} %get-tuple-element.61), channel_id=1, source_target_pairs={{0,2},{2,4},{4,6},{6,0},{1,3},{3,5},{5,7},{7,1},{8,10},{10,12},{12... | collective-permute-start | bytes 1437704 | tf_op jit(solution)/shard_map/ppermute | solution.py:493
  81.0 3.0 %collective-permute-start.4 = (bf16[1872,128]{1,0:T(8,128)(2,1)}, bf16[1872,128]{1,0:T(8,128)(2,1)S(1)}, u32[]{:S(2)}, u32[]{:S(2)}) collective-permute-start(bf16[1872,128]{1,0:T(8,128)(2,1)} %get-tuple-element.62), channel_id=1, source_target_pairs={{0,4},{2,6},{4,0},{6,2},{1,5},{3,7},{5,1},{7,3},{8,12},{10,14},{12... | collective-permute-start | bytes 1437704 | tf_op jit(solution)/shard_map/ppermute | solution.py:493
  84.0 3.4 %collective-permute-start.5 = (bf16[1872,128]{1,0:T(8,128)(2,1)}, bf16[1872,128]{1,0:T(8,128)(2,1)S(1)}, u32[]{:S(2)}, u32[]{:S(2)}) collective-permute-start(bf16[1872,128]{1,0:T(8,128)(2,1)} %get-tuple-element.63), channel_id=1, source_target_pairs={{0,6},{2,0},{4,2},{6,4},{1,7},{3,1},{5,3},{7,5},{8,14},{10,8},{12,... | collective-permute-start | bytes 1437704 | tf_op jit(solution)/shard_map/ppermute | solution.py:493
  87.5 3.4 %shard_map.156 = (bf16[144,2304]{1,0:T(8,128)(2,1)}, bf16[144,2304]{1,0:T(8,128)(2,1)}, bf16[2304,144]{1,0:T(8,128)(2,1)}, bf16[2304,144]{1,0:T(8,128)(2,1)}) custom-call(bf16[176,256]{1,0:T(8,128)(2,1)S(1)} %collective-permute-done.packed_ref), custom_call_target="tpu_custom_call" | custom-call | flops 679477248 | bytes 2654208 | tf_op jit(solution)/shard_map/pallas_call | solution.py:473
  90.9 9.2 %all-to-all-done.1 = bf16[96,24,128]{2,1,0:T(8,128)(2,1)S(1)} async-done(((bf16[96,24,128]{2,1,0:T(8,128)(2,1)}), bf16[96,24,128]{2,1,0:T(8,128)(2,1)S(1)}, u32[]{:S(2)}, u32[]{:S(2)}) %all-to-all-start.1) | async-done | bytes 589856 | tf_op jit(solution)/shard_map/all_to_all | solution.py:426
  100.0 0.0 copy-start.3
  100.0 4.5 %shard_map.157 = (bf16[144,256]{1,0:T(8,128)(2,1)S(1)}, bf16[2304,128]{1,0:T(8,128)(2,1)}) custom-call(bf16[2304,128]{1,0:T(8,128)(2,1)S(1)} %bitcast.36, bf16[144,256]{1,0:T(8,128)(2,1)S(1)} %collective-permute-done.1.target_ref, bf16[144,2304]{1,0:T(8,128)(2,1)} %get-tuple-element.53.refs_0_, bf16[144,2304]{1,0:T(8,128)(2,1)} %get-tuple-element.54.refs_1_, ...), custom_call_target="tpu_custom_call" | custom-call | flops 1019215872 | bytes 2654208 | tf_op jit(solution)/shard_map/pallas_call | solution.py:497
  104.5 9.3 %all-to-all-start.2 = ((bf16[96,24,128]{2,1,0:T(8,128)(2,1)}), bf16[96,24,128]{2,1,0:T(8,128)(2,1)}, u32[]{:S(2)}, u32[]{:S(2)}) async-start(bf16[96,24,128]{2,1,0:T(8,128)(2,1)} %bitcast.42), calls=%async_computation.2 | async-start | bytes 1179648 | tf_op jit(solution)/shard_map/all_to_all | solution.py:426
  113.8 0.0 collective-permute-done.3.part1
  113.8 0.0 collective-permute-done.4.part2
  113.8 0.0 collective-permute-done.5.part3
  113.8 0.0 copy-start.1
  113.8 0.0 copy-done.3
  113.8 0.6 shard_map.159
  114.5 0.1 copy-done.1
  114.6 4.1 %collective-permute-start.6 = (bf16[6336,128]{1,0:T(8,128)(2,1)S(1)}, bf16[6336,128]{1,0:T(8,128)(2,1)S(1)}, u32[]{:S(2)}, u32[]{:S(2)}) collective-permute-start(bf16[6336,128]{1,0:T(8,128)(2,1)S(1)} %shard_map.159), channel_id=1, source_target_pairs={{0,1},{1,0},{2,3},{3,2},{4,5},{5,4},{6,7},{7,6},{8,9},{9,8},{10,11... | collective-permute-start | bytes 4866056 | tf_op jit(solution)/shard_map/ppermute | solution.py:512
  118.7 6.7 %collective-permute-start.2 = (bf16[144,256]{1,0:T(8,128)(2,1)S(1)}, bf16[144,256]{1,0:T(8,128)(2,1)S(1)}, u32[]{:S(2)}, u32[]{:S(2)}) collective-permute-start(bf16[144,256]{1,0:T(8,128)(2,1)S(1)} %get-tuple-element.58), channel_id=1, source_target_pairs={{0,0},{1,32},{2,8},{3,40},{4,16},{5,48},{6,24},{7,56},{8,2},{9,34}... | collective-permute-start | bytes 221192 | tf_op jit(solution)/shard_map/ppermute | solution.py:421
  125.5 0.0 collective-permute-done.6.far_ref
  125.5 0.0 copy-start.2
  125.5 1.0 copy-done.2
  126.5 0.0 copy-start
  126.5 3.1 %shard_map.160 = (bf16[256,1152]{1,0:T(8,128)(2,1)}, bf16[384,1152]{1,0:T(8,128)(2,1)}, bf16[1152,768]{1,0:T(8,128)(2,1)}) custom-call(s32[2]{0:T(128)S(1)} %pad_add_fusion.place_ref, bf16[2304,128]{1,0:T(8,128)(2,1)S(1)} %bitcast.32, bf16[1296,128]{1,0:T(8,128)(2,1)S(1)} %copy-done.3, bf16[1872,128]{1,0:T(8,128)(2,1)S(1)} %collective-permute-done.3.part1, ...), custom_call_target="tpu_custom_call" | custom-call | flops 339738624 | bytes 3538944 | tf_op jit(solution)/shard_map/pallas_call | solution.py:513
  129.6 0.2 collective-permute-done.2.value_ref
  129.8 0.6 shard_map.161
  130.5 8.0 %all-to-all-done.2 = bf16[96,24,128]{2,1,0:T(8,128)(2,1)} async-done(((bf16[96,24,128]{2,1,0:T(8,128)(2,1)}), bf16[96,24,128]{2,1,0:T(8,128)(2,1)}, u32[]{:S(2)}, u32[]{:S(2)}) %all-to-all-start.2) | async-done | bytes 589856 | tf_op jit(solution)/shard_map/all_to_all | solution.py:426
  138.5 8.6 %all-to-all-start.3 = ((bf16[8,288,128]{2,1,0:T(8,128)(2,1)}), bf16[8,288,128]{2,1,0:T(8,128)(2,1)S(1)}, u32[]{:S(2)}, u32[]{:S(2)}) async-start(bf16[8,288,128]{2,1,0:T(8,128)(2,1)} %bitcast.14), calls=%async_computation.3 | async-start | bytes 1179648 | tf_op jit(solution)/shard_map/all_to_all | solution.py:528
  147.0 0.0 copy-done
  147.0 2.1 %shard_map.162 = bf16[144,384]{1,0:T(8,128)(2,1)S(1)} custom-call(bf16[2304,128]{1,0:T(8,128)(2,1)} %bitcast.11.rows_ref, bf16[384,2048]{1,0:T(8,128)(2,1)S(1)} %bitcast.34), custom_call_target="tpu_custom_call" | custom-call | flops 452984832 | bytes 1572864 | tf_op jit(solution)/shard_map/pallas_call | solution.py:531
  149.2 17.3 %all_gather.3.hidden_grad_ref = bf16[1152,384]{1,0:T(8,128)(2,1)S(1)} all-gather(bf16[144,384]{1,0:T(8,128)(2,1)S(1)} %shard_map.162), channel_id=1, replica_groups=mesh['z'=12,'y_high'=2,'y_low'=4,'x'=4,'core'=2] {'x','core'}, dimensions={0}, use_global_device_ids=true | all-gather | bytes 995328 | tf_op jit(solution)/shard_map/all_gather | solution.py:534
  166.5 0.0 all-to-all-done.3
  166.5 4.2 %shard_map.163 = (bf16[256,768]{1,0:T(8,128)(2,1)S(1)}, bf16[256,768]{1,0:T(8,128)(2,1)S(1)}, bf16[256,768]{1,0:T(8,128)(2,1)S(1)}, bf16[384,256]{1,0:T(8,128)(2...) custom-call(bf16[2304,128]{1,0:T(8,128)(2,1)S(1)} %bitcast.35, bf16[1152,384]{1,0:T(8,128)(2,1)S(1)} %all_gather.3.hidden_grad_ref, ...), custom_call_target="tpu_custom_call" | custom-call | flops 679477248 | bytes 1572864 | tf_op jit(solution)/shard_map/pallas_call | solution.py:537
  170.7 0.8 reshape.89
  171.5 0.8 reshape.90
  172.4 0.8 reshape.91
Async XLA Ops:
  0.6 34.9 %copy-start.7 = (bf16[144,256]{1,0:T(8,128)(2,1)S(1)}, bf16[144,256]{1,0:T(8,128)(2,1)}, u32[]{:S(2)}) copy-start(bf16[144,256]{1,0:T(8,128)(2,1)} %param.11) | copy-start | bytes 221188
  0.6 43.3 %copy-start.5 = (bf16[1,256,2,384]{3,2,1,0:T(2,128)(2,1)S(1)}, bf16[1,256,2,384]{3,2,1,0:T(2,128)(2,1)}, u32[]{:S(2)}) copy-start(bf16[1,256,2,384]{3,2,1,0:T(2,128)(2,1)} %param.15) | copy-start | bytes 1179652
  1.6 43.1 %copy-start.6 = (bf16[1,256,2,384]{3,2,1,0:T(2,128)(2,1)S(1)}, bf16[1,256,2,384]{3,2,1,0:T(2,128)(2,1)}, u32[]{:S(2)}) copy-start(bf16[1,256,2,384]{3,2,1,0:T(2,128)(2,1)} %param.16) | copy-start | bytes 1179652
  1.6 11.5 %collective-permute-start = (bf16[176,256]{1,0:T(8,128)(2,1)S(1)}, bf16[176,256]{1,0:T(8,128)(2,1)S(1)}, u32[]{:S(2)}, u32[]{:S(2)}) collective-permute-start(bf16[176,256]{1,0:T(8,128)(2,1)S(1)} %shard_map.153), channel_id=1, source_target_pairs={{0,0},{1,32},{2,8},{3,40},{4,16},{5,48},{6,24},{7,56},{8,2},{9,34}... | collective-permute-start | bytes 270344 | tf_op jit(solution)/shard_map/ppermute | solution.py:421
  15.0 46.0 %all-to-all-start = ((bf16[96,24,128]{2,1,0:T(8,128)(2,1)}), bf16[96,24,128]{2,1,0:T(8,128)(2,1)S(1)}, u32[]{:S(2)}, u32[]{:S(2)}) async-start(bf16[96,24,128]{2,1,0:T(8,128)(2,1)} %bitcast.2), calls=%async_computation | async-start | bytes 1179648 | tf_op jit(solution)/shard_map/all_to_all | solution.py:426
  35.5 17.6 %collective-permute-start.1 = (bf16[144,256]{1,0:T(8,128)(2,1)S(1)}, bf16[144,256]{1,0:T(8,128)(2,1)S(1)}, u32[]{:S(2)}, u32[]{:S(2)}) collective-permute-start(bf16[144,256]{1,0:T(8,128)(2,1)S(1)} %copy-done.7), channel_id=1, source_target_pairs={{0,0},{1,32},{2,8},{3,40},{4,16},{5,48},{6,24},{7,56},{8,2},{9,34}... | collective-permute-start | bytes 221192 | tf_op jit(solution)/shard_map/ppermute | solution.py:421
  65.7 9.1 %copy-start.4 = (f32[288,768]{1,0:T(8,128)S(1)}, f32[288,768]{1,0:T(8,128)}, u32[]{:S(2)}) copy-start(f32[288,768]{1,0:T(8,128)} %get-tuple-element.59.preacts_ref) | copy-start | bytes 2654212
  65.7 34.4 %all-to-all-start.1 = ((bf16[96,24,128]{2,1,0:T(8,128)(2,1)}), bf16[96,24,128]{2,1,0:T(8,128)(2,1)S(1)}, u32[]{:S(2)}, u32[]{:S(2)}) async-start(bf16[96,24,128]{2,1,0:T(8,128)(2,1)} %bitcast.43), calls=%async_computation.1 | async-start | bytes 1179648 | tf_op jit(solution)/shard_map/all_to_all | solution.py:426
  77.1 36.7 %collective-permute-start.3 = (bf16[1872,128]{1,0:T(8,128)(2,1)}, bf16[1872,128]{1,0:T(8,128)(2,1)S(1)}, u32[]{:S(2)}, u32[]{:S(2)}) collective-permute-start(bf16[1872,128]{1,0:T(8,128)(2,1)} %get-tuple-element.61), channel_id=1, source_target_pairs={{0,2},{2,4},{4,6},{6,0},{1,3},{3,5},{5,7},{7,1},{8,10},{10,12},{12... | collective-permute-start | bytes 1437704 | tf_op jit(solution)/shard_map/ppermute | solution.py:493
  81.0 32.8 %collective-permute-start.4 = (bf16[1872,128]{1,0:T(8,128)(2,1)}, bf16[1872,128]{1,0:T(8,128)(2,1)S(1)}, u32[]{:S(2)}, u32[]{:S(2)}) collective-permute-start(bf16[1872,128]{1,0:T(8,128)(2,1)} %get-tuple-element.62), channel_id=1, source_target_pairs={{0,4},{2,6},{4,0},{6,2},{1,5},{3,7},{5,1},{7,3},{8,12},{10,14},{12... | collective-permute-start | bytes 1437704 | tf_op jit(solution)/shard_map/ppermute | solution.py:493
  84.0 29.8 %collective-permute-start.5 = (bf16[1872,128]{1,0:T(8,128)(2,1)}, bf16[1872,128]{1,0:T(8,128)(2,1)S(1)}, u32[]{:S(2)}, u32[]{:S(2)}) collective-permute-start(bf16[1872,128]{1,0:T(8,128)(2,1)} %get-tuple-element.63), channel_id=1, source_target_pairs={{0,6},{2,0},{4,2},{6,4},{1,7},{3,1},{5,3},{7,5},{8,14},{10,8},{12,... | collective-permute-start | bytes 1437704 | tf_op jit(solution)/shard_map/ppermute | solution.py:493
  100.0 13.8 %copy-start.3 = (bf16[1296,128]{1,0:T(8,128)(2,1)S(1)}, bf16[1296,128]{1,0:T(8,128)(2,1)}, u32[]{:S(2)}) copy-start(bf16[1296,128]{1,0:T(8,128)(2,1)} %get-tuple-element.60.factors_ref.near_factors_ref) | copy-start | bytes 995332
  104.5 34.0 %all-to-all-start.2 = ((bf16[96,24,128]{2,1,0:T(8,128)(2,1)}), bf16[96,24,128]{2,1,0:T(8,128)(2,1)}, u32[]{:S(2)}, u32[]{:S(2)}) async-start(bf16[96,24,128]{2,1,0:T(8,128)(2,1)} %bitcast.42), calls=%async_computation.2 | async-start | bytes 1179648 | tf_op jit(solution)/shard_map/all_to_all | solution.py:426
  113.8 0.8 copy-start.1
  114.6 10.9 %collective-permute-start.6 = (bf16[6336,128]{1,0:T(8,128)(2,1)S(1)}, bf16[6336,128]{1,0:T(8,128)(2,1)S(1)}, u32[]{:S(2)}, u32[]{:S(2)}) collective-permute-start(bf16[6336,128]{1,0:T(8,128)(2,1)S(1)} %shard_map.159), channel_id=1, source_target_pairs={{0,1},{1,0},{2,3},{3,2},{4,5},{5,4},{6,7},{7,6},{8,9},{9,8},{10,11... | collective-permute-start | bytes 4866056 | tf_op jit(solution)/shard_map/ppermute | solution.py:512
  118.7 11.1 %collective-permute-start.2 = (bf16[144,256]{1,0:T(8,128)(2,1)S(1)}, bf16[144,256]{1,0:T(8,128)(2,1)S(1)}, u32[]{:S(2)}, u32[]{:S(2)}) collective-permute-start(bf16[144,256]{1,0:T(8,128)(2,1)S(1)} %get-tuple-element.58), channel_id=1, source_target_pairs={{0,0},{1,32},{2,8},{3,40},{4,16},{5,48},{6,24},{7,56},{8,2},{9,34}... | collective-permute-start | bytes 221192 | tf_op jit(solution)/shard_map/ppermute | solution.py:421
  125.5 1.0 copy-start.2
  126.5 20.5 %copy-start = (bf16[1,384,2048]{2,1,0:T(8,128)(2,1)S(1)}, bf16[1,384,2048]{2,1,0:T(8,128)(2,1)}, u32[]{:S(2)}) copy-start(bf16[1,384,2048]{2,1,0:T(8,128)(2,1)} %param.17) | copy-start | bytes 4718596
  138.5 28.0 %all-to-all-start.3 = ((bf16[8,288,128]{2,1,0:T(8,128)(2,1)}), bf16[8,288,128]{2,1,0:T(8,128)(2,1)S(1)}, u32[]{:S(2)}, u32[]{:S(2)}) async-start(bf16[8,288,128]{2,1,0:T(8,128)(2,1)} %bitcast.14), calls=%async_computation.3 | async-start | bytes 1179648 | tf_op jit(solution)/shard_map/all_to_all | solution.py:528
